TPU v7x, 32 devices: a whole 2x2x4 slice. The times are simulated.
32 devices in a mesh: dp: 8 (over z, y), blk: 4 (over x, core).
Axes of the slice: x: 2, y: 2, z: 4, core: 2. Of those that a mesh axis runs over, the one named last changes fastest.
Arguments:
- tokens: bfloat16 [26624, 1024], P(('dp', 'blk')), may hold values from -6 to 6
- cotangent: bfloat16 [26624, 1024], P(('dp', 'blk')), may hold values from -6 to 6
- lengths: int32 [8, 3], P('dp'), may hold values from 1 to 2368, as said below
- qkv_weight: bfloat16 [1024, 3072], replicated, may hold values from -0.1875 to 0.1875
- out_weight: bfloat16 [1024, 1024], replicated, may hold values from -0.1875 to 0.1875
- up_weight: bfloat16 [1024, 4096], replicated, may hold values from -0.1875 to 0.1875
- down_weight: bfloat16 [4096, 1024], replicated, may hold values from -0.09375 to 0.09375
- norm_gain: float32 [4, 1024], replicated, may hold values from 0.5 to 1.5
- norm_bias: float32 [4, 1024], replicated, may hold values from -1.5 to 1.5
- proj_bias: float32 [4, 1024], replicated, may hold values from -1.5 to 1.5
- ffn_bias: float32 [4096], replicated, may hold values from -1.5 to 1.5
Outputs:
- mixed: bfloat16 [26624, 1024], P(('dp', 'blk'))
- token_grad: bfloat16 [26624, 1024], P(('dp', 'blk'))
- qkv_grad: float32 [1024, 3072], P('dp', 'blk')
- out_grad: float32 [1024, 1024], P('dp', 'blk')
- up_grad: float32 [1024, 4096], P('dp', 'blk')
- down_grad: float32 [4096, 1024], P('dp', 'blk')
- gain_grad: float32 [4, 1024], P(None, 'dp')
- norm_bias_grad: float32 [4, 1024], P(None, 'dp')
- proj_bias_grad: float32 [4, 1024], P(None, 'dp')
- ffn_bias_grad: float32 [4096], P('dp')
Inputs may be any that keep to these rules, and one draw needn't show every extreme that they name: In each row the three lengths sum to 3328; the middle one is exactly 2368 and its sequence holds a position of the group's first 832 rows and one of its last 832 rows.
All inputs are finite; a program needn't handle non-finite values.
Results may differ from a plain program's by a relative error of at most 0.015.
Values may be sent and summed in bfloat16 or wider, within the bound.
A program may use at most 384 MiB of HBM per device.

v0:
```python
import math

import jax
import jax.numpy as jnp
from jax import lax
from jax.sharding import PartitionSpec as P

HEADS = 16


relax_factor = 32.0
epsilon = 1e-05


def layer_norm(values, gain, shift):
    centre = values - jnp.mean(values, -1, keepdims=True)
    spread = jnp.mean(centre * centre, -1, keepdims=True)
    return centre * lax.rsqrt(spread + epsilon) * gain + shift


def gelu_tanh(values):
    return jax.nn.gelu(values, approximate=True)


def segment_of(positions, ends):
    return (positions >= ends[0]).astype(jnp.int32) + (positions >= ends[1]).astype(jnp.int32)


def outer_sum(left, right):
    return lax.dot_general(
        left, right, (((0,), (0,)), ((), ())), preferred_element_type=jnp.float32
    )


def times_transposed(left, right):
    return lax.dot_general(
        left, right, (((1,), (1,)), ((), ())), preferred_element_type=jnp.float32
    )


def column_sums(values):
    return jnp.sum(values.astype(jnp.float32), 0)


def local(
    tokens,
    cotangent,
    lengths,
    qkv_weight,
    out_weight,
    up_weight,
    down_weight,
    norm_gain,
    norm_bias,
    proj_bias,
    ffn_bias,
):
    rows, width = tokens.shape
    head_size = width // HEADS
    blocks = lax.axis_size("blk")
    anchor = lax.axis_index("blk") * rows
    ends = jnp.cumsum(lengths[0])
    query_pos = anchor + jnp.arange(rows, dtype=jnp.int32)
    scale = 1.0 / (relax_factor * math.sqrt(head_size))
    inputs = tokens.astype(jnp.float32)
    normed_in, pull_first = jax.vjp(layer_norm, inputs, norm_gain[0], norm_bias[0])
    first_normed = normed_in.astype(jnp.bfloat16)
    projected = jnp.dot(first_normed, qkv_weight, preferred_element_type=jnp.float32)
    query_rows = (projected[:, :width] + proj_bias[0]).astype(jnp.bfloat16)
    key_rows = projected[:, width : 2 * width].astype(jnp.bfloat16)
    value_rows = (projected[:, 2 * width :] + proj_bias[1]).astype(jnp.bfloat16)
    query_heads = query_rows.reshape(rows, HEADS, head_size)

    def allowed_between(q_positions, k_positions):
        same = segment_of(q_positions, ends)[:, None] == segment_of(k_positions, ends)[None, :]
        return same & (k_positions[None, :] <= q_positions[:, None])

    def allowed_for(start, count):
        return allowed_between(query_pos, start + jnp.arange(count, dtype=jnp.int32))

    def scores_for(key_piece, allowed):
        raw = (
            jnp.einsum(
                "qhd,khd->hqk",
                query_heads,
                key_piece.reshape(-1, HEADS, head_size),
                preferred_element_type=jnp.float32,
            )
            * scale
        )
        return jnp.where(allowed[None], raw, -1e30)

    start_state = (
        jnp.full((HEADS, rows), -1e30, jnp.float32),
        jnp.zeros((HEADS, rows), jnp.float32),
        jnp.zeros((rows, width), jnp.float32),
    )
    key_piece = lax.all_gather(key_rows, "blk", axis=0, tiled=True)
    value_piece = lax.all_gather(value_rows, "blk", axis=0, tiled=True)
    count = key_piece.shape[0]
    fold_allowed = allowed_for(jnp.int32(0), count)

    def update(state):
        top, total, summed = state
        scores = scores_for(key_piece, fold_allowed)
        new_top = jnp.maximum(top, jnp.max(scores, axis=-1))
        weights_raw = jnp.where(
            fold_allowed[None], jnp.exp(relax_factor * (scores - new_top[:, :, None])), 0.0
        )
        fade = jnp.exp(relax_factor * (top - new_top))
        part = jnp.einsum(
            "hqk,khd->qhd",
            weights_raw.astype(jnp.bfloat16),
            value_piece.reshape(count, HEADS, head_size),
            preferred_element_type=jnp.float32,
        )
        summed_new = summed.reshape(rows, HEADS, head_size) * fade.T[:, :, None] + part
        return (new_top, total * fade + jnp.sum(weights_raw, -1), summed_new.reshape(rows, width))

    state = lax.cond(jnp.any(fold_allowed), update, lambda state: state, start_state)
    top, total, summed = state
    log_total = relax_factor * top + jnp.log(total)
    attended = (
        (summed.reshape(rows, HEADS, head_size) / total.T[:, :, None])
        .reshape(rows, width)
        .astype(jnp.bfloat16)
    )
    attn_branch = jnp.dot(attended, out_weight, preferred_element_type=jnp.float32) + proj_bias[2]
    attn_normed, pull_attn = jax.vjp(layer_norm, attn_branch, norm_gain[1], norm_bias[1])
    middle = inputs + attn_normed
    second_full, pull_second = jax.vjp(layer_norm, middle, norm_gain[2], norm_bias[2])
    second_normed = second_full.astype(jnp.bfloat16)
    pre_gelu = jnp.dot(second_normed, up_weight, preferred_element_type=jnp.float32) + ffn_bias
    activated_full, pull_gelu = jax.vjp(gelu_tanh, pre_gelu)
    activated = activated_full.astype(jnp.bfloat16)
    ffn_branch = jnp.dot(activated, down_weight, preferred_element_type=jnp.float32) + proj_bias[3]
    ffn_normed, pull_ffn = jax.vjp(layer_norm, ffn_branch, norm_gain[3], norm_bias[3])
    mixed = (middle + ffn_normed).astype(jnp.bfloat16)
    incoming = cotangent.astype(jnp.float32)
    grad_ffn, gain_three, shift_three = pull_ffn(incoming)
    grad_ffn_low = grad_ffn.astype(jnp.bfloat16)
    down_term = outer_sum(activated, grad_ffn_low)
    bias_three = column_sums(grad_ffn_low)
    (grad_pre,) = pull_gelu(times_transposed(grad_ffn_low, down_weight))
    grad_pre_low = grad_pre.astype(jnp.bfloat16)
    up_term = outer_sum(second_normed, grad_pre_low)
    hidden_bias = column_sums(grad_pre_low)
    grad_from_ffn, gain_two, shift_two = pull_second(times_transposed(grad_pre_low, up_weight))
    grad_middle = incoming + grad_from_ffn
    grad_attn, gain_one, shift_one = pull_attn(grad_middle)
    grad_attn_low = grad_attn.astype(jnp.bfloat16)
    out_term = outer_sum(attended, grad_attn_low)
    bias_two = column_sums(grad_attn_low)
    grad_attended = times_transposed(grad_attn_low, out_weight).astype(jnp.bfloat16)
    grad_heads = grad_attended.reshape(rows, HEADS, head_size)
    attended_heads = attended.reshape(rows, HEADS, head_size)
    delta = jnp.sum(grad_heads.astype(jnp.float32) * attended_heads.astype(jnp.float32), -1).T
    key_all, value_all = (
        lax.all_gather(key_rows, "blk", axis=0, tiled=True),
        lax.all_gather(value_rows, "blk", axis=0, tiled=True),
    )

    def pair_terms(q_heads, g_heads, delta_rows, log_rows, key_piece, value_piece, allowed):
        count = key_piece.shape[0]
        key_heads = key_piece.reshape(count, HEADS, head_size)
        value_heads = value_piece.reshape(count, HEADS, head_size)
        raw = (
            jnp.einsum("qhd,khd->hqk", q_heads, key_heads, preferred_element_type=jnp.float32)
            * scale
        )
        scores = jnp.where(allowed[None], raw, -1e30)
        probs = jnp.where(allowed[None], jnp.exp(relax_factor * scores - log_rows[:, :, None]), 0.0)
        grad_probs = jnp.einsum(
            "qhd,khd->hqk", g_heads, value_heads, preferred_element_type=jnp.float32
        )
        grad_scores = (relax_factor * probs * (grad_probs - delta_rows[:, :, None])).astype(
            jnp.bfloat16
        )
        results = []
        results.append(
            jnp.einsum("hqk,khd->qhd", grad_scores, key_heads, preferred_element_type=jnp.float32)
        )
        part_key = (
            jnp.einsum("hqk,qhd->khd", grad_scores, q_heads, preferred_element_type=jnp.float32)
            * scale
        )
        part_value = jnp.einsum(
            "hqk,qhd->khd", probs.astype(jnp.bfloat16), g_heads, preferred_element_type=jnp.float32
        )
        results.append(
            jnp.concatenate([part_key.reshape(count, width), part_value.reshape(count, width)], 1)
        )
        return tuple(results)

    query_grad = jnp.zeros((rows, HEADS, head_size), jnp.float32)

    def block_grads(operand):
        key_piece, value_piece, allowed = operand
        return pair_terms(
            query_heads, grad_heads, delta, log_total, key_piece, value_piece, allowed
        )

    def block_empty(operand):
        return (
            jnp.zeros((rows, HEADS, head_size), jnp.float32),
            jnp.zeros((rows, 2 * width), jnp.float32),
        )

    terms = []
    for block in range(blocks):
        allowed = allowed_for(block * rows, rows)
        operand = (
            key_all[block * rows : (block + 1) * rows],
            value_all[block * rows : (block + 1) * rows],
            allowed,
        )
        part_query, term = lax.cond(jnp.any(allowed), block_grads, block_empty, operand)
        query_grad = query_grad + part_query
        terms.append(term)
    pair_grads = lax.psum_scatter(
        jnp.concatenate(terms, 0).astype(jnp.bfloat16), "blk", scatter_dimension=0, tiled=True
    ).astype(jnp.float32)
    query_low = (query_grad.reshape(rows, width) * scale).astype(jnp.bfloat16)
    key_low = pair_grads[:, :width].astype(jnp.bfloat16)
    value_low = pair_grads[:, width:].astype(jnp.bfloat16)
    grad_projected = jnp.concatenate([query_low, key_low, value_low], 1)
    qkv_term = outer_sum(first_normed, grad_projected)
    bias_query = column_sums(query_low)
    bias_value = column_sums(value_low)
    grad_from_attn, gain_zero, shift_zero = pull_first(times_transposed(grad_projected, qkv_weight))
    token_grad = (grad_middle + grad_from_attn).astype(jnp.bfloat16)
    gain_term = jnp.stack([gain_zero, gain_one, gain_two, gain_three])
    shift_term = jnp.stack([shift_zero, shift_one, shift_two, shift_three])
    proj_term = jnp.stack([bias_query, bias_value, bias_two, bias_three])
    summed_all = (
        lax.psum_scatter(qkv_term, "dp", scatter_dimension=0, tiled=True),
        lax.psum_scatter(out_term, "dp", scatter_dimension=0, tiled=True),
        lax.psum_scatter(up_term, "dp", scatter_dimension=0, tiled=True),
        lax.psum_scatter(down_term, "dp", scatter_dimension=0, tiled=True),
        lax.psum_scatter(gain_term, "dp", scatter_dimension=1, tiled=True),
        lax.psum_scatter(shift_term, "dp", scatter_dimension=1, tiled=True),
        lax.psum_scatter(proj_term, "dp", scatter_dimension=1, tiled=True),
        lax.psum_scatter(hidden_bias, "dp", scatter_dimension=0, tiled=True),
    )
    qkv_grad, out_grad, up_grad, down_grad = (
        lax.psum_scatter(
            summed_all[0].astype(jnp.bfloat16), "blk", scatter_dimension=1, tiled=True
        ).astype(jnp.float32),
        lax.psum_scatter(
            summed_all[1].astype(jnp.bfloat16), "blk", scatter_dimension=1, tiled=True
        ).astype(jnp.float32),
        lax.psum_scatter(
            summed_all[2].astype(jnp.bfloat16), "blk", scatter_dimension=1, tiled=True
        ).astype(jnp.float32),
        lax.psum_scatter(
            summed_all[3].astype(jnp.bfloat16), "blk", scatter_dimension=1, tiled=True
        ).astype(jnp.float32),
    )
    gain_grad, norm_bias_grad, proj_bias_grad, ffn_bias_grad = lax.psum(
        (summed_all[4], summed_all[5], summed_all[6], summed_all[7]), "blk"
    )
    return (
        mixed,
        token_grad,
        qkv_grad,
        out_grad,
        up_grad,
        down_grad,
        gain_grad,
        norm_bias_grad,
        proj_bias_grad,
        ffn_bias_grad,
    )


def solution(mesh):
    return jax.shard_map(
        local,
        mesh=mesh,
        in_specs=(
            P(("dp", "blk"), None),
            P(("dp", "blk"), None),
            P("dp", None),
            P(),
            P(),
            P(),
            P(),
            P(),
            P(),
            P(),
            P(),
        ),
        out_specs=(
            P(("dp", "blk"), None),
            P(("dp", "blk"), None),
            P("dp", "blk"),
            P("dp", "blk"),
            P("dp", "blk"),
            P("dp", "blk"),
            P(None, "dp"),
            P(None, "dp"),
            P(None, "dp"),
            P("dp"),
        ),
        check_vma=False,
    )
```

profile of v0, /device:TPU:0, one launch (start us, length us, event | category | flops | bytes accessed | tf_op | source)
XLA Modules:
  0.0 2305.9 jit_solution(1425025035322373367)
XLA Ops:
  53.6 24.4 %all-gather.5.cloned.1.call-done = bf16[3328,1024]{1,0:T(8,128)(2,1)} async-done(((bf16[832,1024]{1,0:T(8,128)(2,1)}), bf16[3328,1024]{1,0:T(8,128)(2,1)}) %all-gather.5.cloned.1.call-update) | async-done | bytes 6815760 | tf_op jit(solution)/shard_map/all_gather | solution.py:99
  78.1 51.5 %all-gather.3.cloned.1.call-done = bf16[3328,1024]{1,0:T(8,128)(2,1)} async-done(((bf16[832,1024]{1,0:T(8,128)(2,1)}), bf16[3328,1024]{1,0:T(8,128)(2,1)}) %all-gather.3.cloned.1.call-update) | async-done | bytes 6815760 | tf_op jit(solution)/shard_map/all_gather | solution.py:98
  129.6 246.3 %conditional.5 = (f32[16,832]{1,0:T(8,128)}, f32[16,832]{1,0:T(8,128)}, f32[832,1024]{0,1:T(8,128)}, f32[16,832]{1,0:T(8,128)}) conditional(s32[]{:T(128)} %convert_element_type.242, () %tuple.50, (pred[832,3328]{1,0:T(8,128)(4,1)}, bf16[3328,1024]{1,0:T(8,128)(2,1)}, bf16[832,16,64]{0,2,1:T(8,128)(2,1)}, bf16[3328,1024]{1,0:T(8,128)(2,1)}) %tuple.174), branch_computations={%region_4.5_spmd, %region_5.8_spmd} | conditional | flops 12006864896 | bytes 586579968 | solution.py:120
  139.6 68.3 %fusion = (f32[16,832]{1,0:T(8,128)S(1)}, f32[16,832,3328]{2,1,0:T(8,128)}) fusion(pred[832,3328]{1,0:T(8,128)(4,1)} %get-tuple-element.73, bf16[832,16,64]{0,2,1:T(8,128)(2,1)} %get-tuple-element.74, bf16[3328,16,64]{0,2,1:T(8,128)(2,1)} %bitcast.172), kind=kOutput, calls=%fused_computation.2 | convolution fusion | flops 5803592704 | bytes 188551168 | tf_op jit(solution)/shard_map/cond/branch_1_fun/qhd,khd->hqk/dot_general | solution.py:83
  208.6 81.0 %fusion.2 = f32[16,832]{1,0:T(8,128)S(1)} fusion(f32[16,832,3328]{2,1,0:T(8,128)} %get-tuple-element.284, f32[16,832]{1,0:T(8,128)} %get-tuple-element.332, pred[832,3328]{1,0:T(8,128)(4,1)} %get-tuple-element.73), kind=kLoop, calls=%fused_computation.4 | loop fusion | flops 265800704 | bytes 180084736 | tf_op jit(solution)/shard_map/cond/branch_1_fun/reduce_sum | solution.py:118
  300.8 74.6 %bitcast_add_fusion = f32[832,16,64]{0,2,1:T(8,128)} fusion(bf16[3328,16,64]{0,2,1:T(8,128)(2,1)} %bitcast.173, f32[16,832,3328]{2,1,0:T(8,128)} %get-tuple-element.284, f32[16,832]{1,0:T(8,128)} %get-tuple-element.332, pred[832,3328]{1,0:T(8,128)(4,1)} %get-tuple-element.73, f32[832,16]{0,1:T(8,128)S(1)} %get-tuple-element.258), kind=kOutput, calls=%fused_computation.7 | convolution fusion | flops 5937364992 | bytes 190308352 | tf_op jit(solution)/shard_map/cond/branch_1_fun/hqk,khd->qhd/dot_general | solution.py:111
  383.9 19.9 multiply_convert_fusion.4
  422.5 22.4 convert_reduce_fusion
  517.6 124.3 %conditional.6 = (f32[832,16,64]{0,2,1:T(8,128)}, bf16[832,2048]{0,1:T(8,128)(2,1)}) conditional(s32[]{:T(128)} %convert_element_type.255, () %tuple.52, (pred[832,832]{1,0:T(8,128)(4,1)S(1)}, bf16[3328,1024]{1,0:T(8,128)(2,1)}, bf16[832,16,64]{0,2,1:T(8,128)(2,1)S(1)}, f32[16,832]{1,0:T(8,128)S(1)}, bf16[3328,1024]{1,0:T(8,128)(2,1)}, ...), branch_computations={%region_22.23_spmd, %region_23.24_spmd} | conditional | flops 7263027200 | bytes 274174016 | solution.py:217
  530.5 19.5 fusion.105
  562.8 31.3 %multiply_convert_fusion = bf16[16,832,832]{2,1,0:T(8,128)(2,1)} fusion(f32[16,832,832]{2,1,0:T(8,128)} %fusion.105, f32[16,832]{1,0:T(8,128)S(1)} %get-tuple-element.83, f32[16,832]{1,0:T(8,128)S(1)} %get-tuple-element.80, pred[832,832]{1,0:T(8,128)(4,1)S(1)} %get-tuple-element.77, bf16[832,16,64]{0,2,1:T(8,128)(2,1)} %get-tuple-element.81, ...), kind=kOutput, calls=%fused_computation.16 | convolution fusion | flops 1517355008 | bytes 70660096 | tf_op jit(solution)/shard_map/cond/branch_1_fun/qhd,khd->hqk/dot_general | solution.py:173
  606.4 20.3 fusion.15
  641.9 22.9 concatenate.20
  730.5 396.6 %reduce-scatter.37.cloned.1.call-done = bf16[832,2048]{1,0:T(8,128)(2,1)} async-done(((bf16[3328,2048]{1,0:T(8,128)(2,1)}), bf16[832,2048]{1,0:T(8,128)(2,1)}) %reduce-scatter.37.cloned.1.call-update) | async-done | bytes 3407888
  1146.2 72.3 %reduce-scatter.25.cloned.1.call-done = f32[128,1024]{1,0:T(8,128)} async-done(((f32[1024,1024]{1,0:T(8,128)}), f32[128,1024]{1,0:T(8,128)}) %reduce-scatter.25.cloned.1.call-update) | async-done | bytes 524304 | tf_op jit(solution)/shard_map/reduce_scatter | solution.py:237
  1240.3 264.1 %reduce-scatter.29.cloned.1.call-done = f32[128,4096]{1,0:T(8,128)} async-done(((f32[1024,4096]{1,0:T(8,128)}), f32[128,4096]{1,0:T(8,128)}) %reduce-scatter.29.cloned.1.call-update) | async-done | bytes 2097168 | tf_op jit(solution)/shard_map/reduce_scatter | solution.py:238
  1507.1 282.5 %reduce-scatter.33.cloned.1.call-done = f32[512,1024]{1,0:T(8,128)} async-done(((f32[4096,1024]{1,0:T(8,128)}), f32[512,1024]{1,0:T(8,128)}) %reduce-scatter.33.cloned.1.call-update) | async-done | bytes 2097168 | tf_op jit(solution)/shard_map/reduce_scatter | solution.py:239
  1792.4 207.7 %reduce-scatter.21.cloned.1.call-done = f32[128,3072]{1,0:T(8,128)} async-done(((f32[1024,3072]{1,0:T(8,128)}), f32[128,3072]{1,0:T(8,128)}) %reduce-scatter.21.cloned.1.call-update) | async-done | bytes 1572880 | tf_op jit(solution)/shard_map/reduce_scatter | solution.py:236
  2003.8 35.2 %all-reduce = f32[4096]{0:T(1024)S(1)} all-reduce(f32[4096]{0:T(1024)S(1)} %copy-done.52), channel_id=14, replica_groups=mesh['dp'=8,'blk'=4] {'dp'}, use_global_device_ids=true, to_apply=%region_63.64.clone | all-reduce | flops 4096 | bytes 32768
  2045.8 42.0 %reduce-scatter.43.cloned.1.call-done = f32[128,4]{1,0:T(8,128)} async-done(((f32[1024,4]{1,0:T(8,128)}), f32[128,4]{1,0:T(8,128)}) %reduce-scatter.43.cloned.1.call-update) | async-done | bytes 2064
  2088.7 64.2 %reduce-scatter.41.cloned.1.call-done = f32[128,4]{1,0:T(8,128)} async-done(((f32[1024,4]{1,0:T(8,128)}), f32[128,4]{1,0:T(8,128)}) %reduce-scatter.41.cloned.1.call-update) | async-done | bytes 2064
  2153.8 64.0 %reduce-scatter.39.cloned.1.call-done = f32[128,4]{1,0:T(8,128)} async-done(((f32[1024,4]{1,0:T(8,128)}), f32[128,4]{1,0:T(8,128)}) %reduce-scatter.39.cloned.1.call-update) | async-done | bytes 2064
  2246.0 25.7 %reduce-scatter.35.cloned.1.call-done = bf16[512,256]{1,0:T(8,128)(2,1)} async-done(((bf16[512,1024]{1,0:T(8,128)(2,1)}), bf16[512,256]{1,0:T(8,128)(2,1)}) %reduce-scatter.35.cloned.1.call-update) | async-done | bytes 262160 | tf_op jit(solution)/shard_map/reduce_scatter | solution.py:255
  2273.4 24.1 %reduce-scatter.23.cloned.1.call-done = bf16[128,768]{1,0:T(8,128)(2,1)} async-done(((bf16[128,3072]{1,0:T(8,128)(2,1)}), bf16[128,768]{1,0:T(8,128)(2,1)}) %reduce-scatter.23.cloned.1.call-update) | async-done | bytes 196624 | tf_op jit(solution)/shard_map/reduce_scatter | solution.py:246
  (259 shorter events, 384.5 us)
Async XLA Ops:
  7.2 371.1 %copy-start = (bf16[1024,1024]{1,0:T(8,128)(2,1)S(1)}, bf16[1024,1024]{1,0:T(8,128)(2,1)}, u32[]{:S(2)}) copy-start(bf16[1024,1024]{1,0:T(8,128)(2,1)} %param.25) | copy-start | bytes 6291460
  7.2 70.8 %all-gather.5.cloned.1.call-start = ((), (), s32[]{:S(2)}) async-start(), calls=%async_computation.13 | async-start | bytes 8519680 | tf_op jit(solution)/shard_map/all_gather | solution.py:99
  25.9 103.7 %all-gather.3.cloned.1.call-start = ((), (), s32[]{:S(2)}) async-start(), calls=%async_computation.12 | async-start | bytes 8519680 | tf_op jit(solution)/shard_map/all_gather | solution.py:98
  29.3 1097.8 %reduce-scatter.37.cloned.1.call-start = ((), (), s32[]{:S(2)}) async-start(), calls=%async_computation.22 | async-start | bytes 17039360
  383.1 75.3 %copy-start.3 = (f32[832,1024]{1,0:T(8,128)}, f32[832,1024]{1,0:T(8,128)S(1)}, u32[]{:S(2)}) copy-start(f32[832,1024]{1,0:T(8,128)S(1)} %get-tuple-element.282) | copy-start | bytes 10223620
  683.3 535.2 %reduce-scatter.25.cloned.1.call-start = ((), (), s32[]{:S(2)}) async-start(), calls=%async_computation.16 | async-start | bytes 4718592 | tf_op jit(solution)/shard_map/reduce_scatter | solution.py:237
  690.5 813.8 %reduce-scatter.29.cloned.1.call-start = ((), (), s32[]{:S(2)}) async-start(), calls=%async_computation.18 | async-start | bytes 18874368 | tf_op jit(solution)/shard_map/reduce_scatter | solution.py:238
  707.1 1082.5 %reduce-scatter.33.cloned.1.call-start = ((), (), s32[]{:S(2)}) async-start(), calls=%async_computation.20 | async-start | bytes 18874368 | tf_op jit(solution)/shard_map/reduce_scatter | solution.py:239
  722.8 1277.3 %reduce-scatter.21.cloned.1.call-start = ((), (), s32[]{:S(2)}) async-start(), calls=%async_computation.14 | async-start | bytes 14155776 | tf_op jit(solution)/shard_map/reduce_scatter | solution.py:236
  730.5 402.6 %copy-start.6 = (bf16[832,1024]{1,0:T(8,128)(2,1)S(1)}, bf16[832,1024]{1,0:T(8,128)(2,1)}, u32[]{:S(2)}) copy-start(bf16[832,1024]{1,0:T(8,128)(2,1)} %param.21) | copy-start | bytes 5111812
  730.5 402.6 %copy-start.28 = (f32[832]{0:T(1024)S(1)}, f32[832]{0:T(1024)}, u32[]{:S(2)}) copy-start(f32[832]{0:T(1024)} %copy-done.27) | copy-start | bytes 9988
  730.5 402.6 %copy-start.31 = (f32[832]{0:T(1024)S(1)}, f32[832]{0:T(1024)}, u32[]{:S(2)}) copy-start(f32[832]{0:T(1024)} %copy-done.30) | copy-start | bytes 9988
  730.5 402.6 %copy-start.35 = (f32[1,1024]{1,0:T(1,128)S(1)}, f32[1,1024]{1,0:T(1,128)}, u32[]{:S(2)}) copy-start(f32[1,1024]{1,0:T(1,128)} %copy-done.34) | copy-start | bytes 12292
  730.5 402.6 %copy-start.56 = (f32[1,1024]{1,0:T(1,128)S(1)}, f32[1,1024]{1,0:T(1,128)}, u32[]{:S(2)}) copy-start(f32[1,1024]{1,0:T(1,128)} %copy-done.55) | copy-start | bytes 12292
  1146.1 893.0 %reduce-scatter.27.cloned.1.call-start = ((), (), s32[]{:S(2)}) async-start(), calls=%async_computation.17 | async-start | bytes 327680 | tf_op jit(solution)/shard_map/reduce_scatter | solution.py:249
  1220.4 867.4 %reduce-scatter.43.cloned.1.call-start = ((), (), s32[]{:S(2)}) async-start(), calls=%async_computation.25 | async-start | bytes 589824
  1234.3 918.6 %reduce-scatter.41.cloned.1.call-start = ((), (), s32[]{:S(2)}) async-start(), calls=%async_computation.24 | async-start | bytes 589824
  1235.4 982.3 %reduce-scatter.39.cloned.1.call-start = ((), (), s32[]{:S(2)}) async-start(), calls=%async_computation.23 | async-start | bytes 589824
  1240.2 1004.0 %reduce-scatter.31.cloned.1.call-start = ((), (), s32[]{:S(2)}) async-start(), calls=%async_computation.19 | async-start | bytes 1310720 | tf_op jit(solution)/shard_map/reduce_scatter | solution.py:252
  1507.1 495.5 %copy-start.63 = (u32[32]{0:T(128)S(1)}, u32[32]{0:T(128)}, u32[]{:S(2)}) copy-start(u32[32]{0:T(128)} %constant.133) | copy-start | bytes 388
  1507.1 496.8 %copy-start.52 = (f32[4096]{0:T(1024)S(1)}, f32[4096]{0:T(1024)}, u32[]{:S(2)}) copy-start(f32[4096]{0:T(1024)} %get-tuple-element.260) | copy-start | bytes 49156
  1507.1 764.6 %reduce-scatter.35.cloned.1.call-start = ((), (), s32[]{:S(2)}) async-start(), calls=%async_computation.21 | async-start | bytes 1310720 | tf_op jit(solution)/shard_map/reduce_scatter | solution.py:255
  1792.4 505.1 %reduce-scatter.23.cloned.1.call-start = ((), (), s32[]{:S(2)}) async-start(), calls=%async_computation.15 | async-start | bytes 983040 | tf_op jit(solution)/shard_map/reduce_scatter | solution.py:246
  2040.6 258.6 %copy-start.1 = (bf16[1024,1024]{1,0:T(8,128)(2,1)S(1)}, bf16[1024,1024]{1,0:T(8,128)(2,1)}, u32[]{:S(2)}) copy-start(bf16[1024,1024]{1,0:T(8,128)(2,1)} %param.25) | copy-start | bytes 6291460
  (51 other events, 462.5 us)
Sparse Core Ops, SparseCore 0:
  26.0 52.0 all-gather.4
  80.2 49.3 all-gather.2
  683.4 443.6 reduce-scatter.36
  1130.6 87.9 reduce-scatter.24
  1222.6 281.6 reduce-scatter.28
  1508.0 281.5 reduce-scatter.32
  1793.6 206.4 reduce-scatter.20
  2003.3 19.1 reduce-scatter.26
  2025.9 61.8 reduce-scatter.42
  2091.9 60.9 reduce-scatter.40
  2156.8 60.8 reduce-scatter.38
  2220.3 23.8 reduce-scatter.30
  2246.7 24.8 reduce-scatter.34
  2274.2 23.2 reduce-scatter.22
where the time goes:
time: 2320 us; the launch traced here: 2310 us
  waiting for transfers between devices  1540 us (66%)
  matrix products  380 us (16%)
  other arithmetic  163 us (7%)
  local copies, waits for them, and re-layouts  135 us (6%)
  blocking collectives  41.5 us (2%)
  loops' own time  28.8 us (1%)
    unnamed x18, waiting for transfers between devices  567 us
    reduce_scatter x1, waiting for transfers between devices, local(): lax.psum_scatter(down_term, 'dp', scatter_dimension=0, tiled=True)  282 us
    reduce_scatter x1, waiting for transfers between devices, local(): lax.psum_scatter(up_term, 'dp', scatter_dimension=0, tiled=True)  264 us
    reduce_scatter x1, waiting for transfers between devices, local(): lax.psum_scatter(qkv_term, 'dp', scatter_dimension=0, tiled=True)  208 us
    reduce_sum x1, other arithmetic, update(): jnp.sum(weights_raw, -1)  81 us
    dot_general x1, matrix products, update(): jnp.einsum('hqk,khd->qhd', weights_raw.astype(jnp.bfloat16), value_piece....  74.6 us
    reduce_scatter x1, waiting for transfers between devices, local(): lax.psum_scatter(out_term, 'dp', scatter_dimension=0, tiled=True)  72.3 us
    dot_general x1, matrix products, scores_for(): jnp.einsum('qhd,khd->hqk', query_heads, key_piece.reshape(-1, HEADS, head...  68.3 us
  transfers between devices with their start and end apart: 14, of which 13 were waited for; matrix products, arithmetic and copies ran while one was open for 6% of the time, Pallas kernels for 0%

commit v1 on v0

v1 whole, which is shorter than its diff:
```python
import functools

import jax
import jax.numpy as jnp
from jax import lax
from jax.experimental import pallas as pl
from jax.experimental.pallas import tpu as pltpu
from jax.sharding import PartitionSpec as P

HEADS = 16
HD = 64
NT = (((1,), (1,)), ((), ()))
NEG = -1e30

def _bounds(len_ref, qb, tile):
    l0 = len_ref[0, 0]
    e1 = l0 + len_ref[0, 1]
    def start_of(r):
        return jnp.where(r >= e1, e1, jnp.where(r >= l0, l0, 0))
    first = qb * tile
    s_first, s_last = start_of(first), start_of(first + tile - 1)
    kmin = s_first // tile
    kmid = jnp.maximum(kmin, jnp.minimum(qb, (s_last + tile - 1) // tile))
    rows = first + lax.broadcasted_iota(jnp.int32, (1, tile), 1)
    return kmin, kmid, rows, start_of(rows)

def _fill_masked(dst, value, heads):
    lane = lax.broadcasted_iota(jnp.int32, value.shape, 1) // HD
    for h in range(heads):
        dst[pl.ds(h * value.shape[0], value.shape[0]), :] = jnp.where(lane == h, value, jnp.zeros_like(value))

def fwd_kernel(len_ref, q_ref, k_ref, vt_ref, o_ref, lse_ref, qm, acc, ps, *, tile, heads):
    qb = pl.program_id(0)
    kmin, kmid, rows, starts = _bounds(len_ref, qb, tile)
    _fill_masked(qm, q_ref[...] * jnp.bfloat16(0.125), heads)
    acc[...] = jnp.zeros_like(acc)
    def step(kb, carry, masked):
        at = pl.multiple_of(kb * tile, tile)
        kblk = k_ref[pl.ds(at, tile), :]
        if masked:
            kpos = at + lax.broadcasted_iota(jnp.int32, (tile, tile), 0)
            mask = (kpos >= starts) & (kpos <= rows)
        scores = [lax.dot_general(kblk, qm[pl.ds(h * tile, tile), :], NT, preferred_element_type=jnp.float32) for h in range(heads)]
        out, alphas = [], []
        for h in range(heads):
            m, l = carry[h]
            s = scores[h]
            if masked:
                s = jnp.where(mask, s, NEG)
            mn = jnp.maximum(m, jnp.max(s, 0, keepdims=True))
            p = jnp.exp(s - mn)
            if masked:
                p = jnp.where(mask, p, 0.0)
            alpha = jnp.exp(m - mn)
            l = l * alpha + jnp.sum(p, 0, keepdims=True)
            ps[:, pl.ds(h * tile, tile)] = p.astype(jnp.bfloat16)
            out.append((mn, l))
            alphas.append(alpha)
        for h in range(heads):
            part = jnp.dot(vt_ref[pl.ds(h * HD, HD), pl.ds(at, tile)], ps[:, pl.ds(h * tile, tile)], preferred_element_type=jnp.float32)
            acc[pl.ds(h * HD, HD), :] = acc[pl.ds(h * HD, HD), :] * alphas[h] + part
        return tuple(out)
    carry = tuple((jnp.full((1, tile), NEG, jnp.float32), jnp.zeros((1, tile), jnp.float32)) for _ in range(heads))
    carry = lax.fori_loop(kmin, kmid, functools.partial(step, masked=True), carry)
    carry = lax.fori_loop(kmid, qb, functools.partial(step, masked=False), carry)
    carry = step(qb, carry, True)
    for h in range(heads):
        m, l = carry[h]
        lse_ref[pl.ds(h, 1), :] = m + jnp.log(l)
        acc[pl.ds(h * HD, HD), :] = acc[pl.ds(h * HD, HD), :] / l
    o_ref[...] = acc[...].T.astype(jnp.bfloat16)

def attn_fwd(lengths, q, k, vt, tile=256):
    n, c = q.shape
    heads = c // HD
    return pl.pallas_call(
        functools.partial(fwd_kernel, tile=tile, heads=heads),
        grid_spec=pltpu.PrefetchScalarGridSpec(
            num_scalar_prefetch=1, grid=(n // tile,),
            in_specs=[pl.BlockSpec((tile, c), lambda i, L: (i, 0)), pl.BlockSpec((n, c), lambda i, L: (0, 0)), pl.BlockSpec((c, n), lambda i, L: (0, 0))],
            out_specs=[pl.BlockSpec((tile, c), lambda i, L: (i, 0)), pl.BlockSpec((heads, tile), lambda i, L: (0, i))],
            scratch_shapes=[pltpu.VMEM((heads * tile, c), jnp.bfloat16), pltpu.VMEM((c, tile), jnp.float32), pltpu.VMEM((tile, heads * tile), jnp.bfloat16)]),
        out_shape=[jax.ShapeDtypeStruct((n, c), jnp.bfloat16), jax.ShapeDtypeStruct((heads, n), jnp.float32)],
        compiler_params=pltpu.CompilerParams(vmem_limit_bytes=40 * 2**20),
        name="attn_fwd",
    )(lengths, q, k, vt)

def bwd_kernel(len_ref, q_ref, do_ref, o_ref, lse_ref, k_ref, v_ref, kt_ref, d_ref, qm, dom, ps, ds, dqt, dk, dv, *, tile, heads):
    qb = pl.program_id(0)
    c = heads * HD
    kmin, kmid, rows, starts = _bounds(len_ref, qb, tile)
    @pl.when(qb == 0)
    def _():
        dk[...] = jnp.zeros_like(dk)
        dv[...] = jnp.zeros_like(dv)
    _fill_masked(qm, q_ref[...] * jnp.bfloat16(0.125), heads)
    _fill_masked(dom, do_ref[...], heads)
    prod = (do_ref[...].astype(jnp.float32) * o_ref[...].astype(jnp.float32)).T
    delta = [jnp.sum(prod[h * HD:(h + 1) * HD], 0, keepdims=True) for h in range(heads)]
    dqt[...] = jnp.zeros_like(dqt)
    def step(kb, carry, masked):
        at = pl.multiple_of(kb * tile, tile)
        kblk = k_ref[pl.ds(at, tile), :]
        vblk = v_ref[pl.ds(at, tile), :]
        if masked:
            kpos = at + lax.broadcasted_iota(jnp.int32, (tile, tile), 0)
            mask = (kpos >= starts) & (kpos <= rows)
        for h in range(heads):
            mine = pl.ds(h * tile, tile)
            s = lax.dot_general(kblk, qm[mine, :], NT, preferred_element_type=jnp.float32)
            p = jnp.exp(s - lse_ref[pl.ds(h, 1), :])
            if masked:
                p = jnp.where(mask, p, 0.0)
            dp = lax.dot_general(vblk, dom[mine, :], NT, preferred_element_type=jnp.float32)
            g = (p * (dp - delta[h])).astype(jnp.bfloat16)
            ps[:, mine] = p.astype(jnp.bfloat16)
            ds[:, mine] = g
        dv[pl.ds(at, tile), :] += jnp.dot(ps[...], dom[...], preferred_element_type=jnp.float32)
        dk[pl.ds(at, tile), :] += jnp.dot(ds[...], qm[...], preferred_element_type=jnp.float32)
        for h in range(heads):
            lanes = pl.ds(h * HD, HD)
            dqt[lanes, :] += jnp.dot(kt_ref[lanes, pl.ds(at, tile)], ds[:, pl.ds(h * tile, tile)], preferred_element_type=jnp.float32)
        return carry
    lax.fori_loop(kmin, kmid, functools.partial(step, masked=True), 0)
    lax.fori_loop(kmid, qb, functools.partial(step, masked=False), 0)
    step(qb, 0, True)
    d_ref[pl.ds(pl.multiple_of(qb * tile, tile), tile), pl.ds(0, c)] = (dqt[...] * 0.125).T.astype(jnp.bfloat16)
    @pl.when(qb == pl.num_programs(0) - 1)
    def _():
        d_ref[:, pl.ds(c, c)] = dk[...].astype(jnp.bfloat16)
        d_ref[:, pl.ds(2 * c, c)] = dv[...].astype(jnp.bfloat16)

def attn_bwd(lengths, q, do, o, lse, k, v, kt, tile=256):
    n, c = q.shape
    heads = c // HD
    row = pl.BlockSpec((tile, c), lambda i, L: (i, 0))
    whole = pl.BlockSpec((n, c), lambda i, L: (0, 0))
    return pl.pallas_call(
        functools.partial(bwd_kernel, tile=tile, heads=heads),
        grid_spec=pltpu.PrefetchScalarGridSpec(
            num_scalar_prefetch=1, grid=(n // tile,),
            in_specs=[row, row, row, pl.BlockSpec((heads, tile), lambda i, L: (0, i)), whole, whole, pl.BlockSpec((c, n), lambda i, L: (0, 0))],
            out_specs=pl.BlockSpec((n, 3 * c), lambda i, L: (0, 0)),
            scratch_shapes=[pltpu.VMEM((heads * tile, c), jnp.bfloat16), pltpu.VMEM((heads * tile, c), jnp.bfloat16),
                            pltpu.VMEM((tile, heads * tile), jnp.bfloat16), pltpu.VMEM((tile, heads * tile), jnp.bfloat16),
                            pltpu.VMEM((c, tile), jnp.float32), pltpu.VMEM((n, c), jnp.float32), pltpu.VMEM((n, c), jnp.float32)]),
        out_shape=jax.ShapeDtypeStruct((n, 3 * c), jnp.bfloat16),
        compiler_params=pltpu.CompilerParams(vmem_limit_bytes=56 * 2**20),
        name="attn_bwd",
    )(lengths, q, do, o, lse, k, v, kt)

epsilon = 1e-05


def layer_norm(values, gain, shift):
    centre = values - jnp.mean(values, -1, keepdims=True)
    spread = jnp.mean(centre * centre, -1, keepdims=True)
    return centre * lax.rsqrt(spread + epsilon) * gain + shift


def gelu_tanh(values):
    return jax.nn.gelu(values, approximate=True)


def outer_sum(left, right):
    return lax.dot_general(left, right, (((0,), (0,)), ((), ())), preferred_element_type=jnp.float32)


def times_transposed(left, right):
    return lax.dot_general(left, right, NT, preferred_element_type=jnp.float32)


def column_sums(values):
    return jnp.sum(values.astype(jnp.float32), 0)


def exchange(values, axis, bit):
    return lax.ppermute(values, axis, [(i, i ^ bit) for i in range(lax.axis_size(axis))])


def columns_for(values, order, blocks):
    width = values.shape[1] // blocks
    return jnp.concatenate([lax.dynamic_slice_in_dim(values, b * width, width, 1) for b in order], 1)


def reduced_outer(left, right, me, blocks):
    low = lambda t: t.astype(jnp.bfloat16)
    away = low(outer_sum(left, columns_for(right, (me ^ 3, me ^ 1), blocks)))
    stay = outer_sum(left, columns_for(right, (me ^ 2, me), blocks))
    half = low(stay + exchange(away, "blk", 1).astype(jnp.float32))
    width = half.shape[1] // 2
    quarter = half[:, width:] + exchange(half[:, :width], "blk", 2)
    return lax.psum_scatter(quarter, "dp", scatter_dimension=0, tiled=True).astype(jnp.float32)


def local(tokens, cotangent, lengths, qkv_weight, out_weight, up_weight, down_weight, norm_gain, norm_bias, proj_bias, ffn_bias):
    rows, width = tokens.shape
    blocks = lax.axis_size("blk")
    me = lax.axis_index("blk")
    own = width // blocks
    inputs = tokens.astype(jnp.float32)
    normed_in, pull_first = jax.vjp(layer_norm, inputs, norm_gain[0], norm_bias[0])
    first_normed = normed_in.astype(jnp.bfloat16)
    first_all = lax.all_gather(first_normed, "blk", axis=0, tiled=True)

    def own_columns(values, third):
        return lax.dynamic_slice_in_dim(values, third * width + me * own, own, values.ndim - 1)

    own_weight = jnp.concatenate([own_columns(qkv_weight, third) for third in range(3)], 1)
    query_bias = lax.dynamic_slice_in_dim(proj_bias[0], me * own, own)
    value_bias = lax.dynamic_slice_in_dim(proj_bias[1], me * own, own)
    projected = jnp.dot(first_all, own_weight, preferred_element_type=jnp.float32)
    queries = (projected[:, :own] + query_bias).astype(jnp.bfloat16)
    keys = projected[:, own : 2 * own].astype(jnp.bfloat16)
    values = (projected[:, 2 * own :] + value_bias).astype(jnp.bfloat16)
    attended_own, log_total = attn_fwd(lengths, queries, keys, values.T)
    attended = lax.all_to_all(attended_own, "blk", split_axis=0, concat_axis=1, tiled=True)
    attn_branch = jnp.dot(attended, out_weight, preferred_element_type=jnp.float32) + proj_bias[2]
    attn_normed, pull_attn = jax.vjp(layer_norm, attn_branch, norm_gain[1], norm_bias[1])
    middle = inputs + attn_normed
    second_full, pull_second = jax.vjp(layer_norm, middle, norm_gain[2], norm_bias[2])
    second_normed = second_full.astype(jnp.bfloat16)
    pre_gelu = jnp.dot(second_normed, up_weight, preferred_element_type=jnp.float32) + ffn_bias
    activated_full, pull_gelu = jax.vjp(gelu_tanh, pre_gelu)
    activated = activated_full.astype(jnp.bfloat16)
    ffn_branch = jnp.dot(activated, down_weight, preferred_element_type=jnp.float32) + proj_bias[3]
    ffn_normed, pull_ffn = jax.vjp(layer_norm, ffn_branch, norm_gain[3], norm_bias[3])
    mixed = (middle + ffn_normed).astype(jnp.bfloat16)
    incoming = cotangent.astype(jnp.float32)
    grad_ffn, gain_three, shift_three = pull_ffn(incoming)
    grad_ffn_low = grad_ffn.astype(jnp.bfloat16)
    down_grad = reduced_outer(activated, grad_ffn_low, me, blocks)
    bias_three = column_sums(grad_ffn_low)
    (grad_pre,) = pull_gelu(times_transposed(grad_ffn_low, down_weight))
    grad_pre_low = grad_pre.astype(jnp.bfloat16)
    up_grad = reduced_outer(second_normed, grad_pre_low, me, blocks)
    hidden_bias = column_sums(grad_pre_low)
    grad_from_ffn, gain_two, shift_two = pull_second(times_transposed(grad_pre_low, up_weight))
    grad_middle = incoming + grad_from_ffn
    grad_attn, gain_one, shift_one = pull_attn(grad_middle)
    grad_attn_low = grad_attn.astype(jnp.bfloat16)
    out_grad = reduced_outer(attended, grad_attn_low, me, blocks)
    bias_two = column_sums(grad_attn_low)
    grad_attended = times_transposed(grad_attn_low, out_weight).astype(jnp.bfloat16)
    grad_own = lax.all_to_all(grad_attended, "blk", split_axis=1, concat_axis=0, tiled=True)
    grad_projected = attn_bwd(lengths, queries, grad_own, attended_own, log_total, keys, values, keys.T)

    qkv_term = lax.psum_scatter(outer_sum(first_all, grad_projected).astype(jnp.bfloat16), "dp", scatter_dimension=0, tiled=True)
    qkv_blocks = lax.all_gather(qkv_term, "blk", axis=0)
    qkv_rows = qkv_blocks.reshape(blocks, -1, 3, own).transpose(1, 2, 0, 3).reshape(-1, 3 * width)
    qkv_grad = lax.dynamic_slice_in_dim(qkv_rows, me * 3 * own, 3 * own, 1).astype(jnp.float32)
    bias_query = lax.dynamic_update_slice_in_dim(jnp.zeros((width,), jnp.float32), column_sums(grad_projected[:, :own]), me * own, 0)
    bias_value = lax.dynamic_update_slice_in_dim(jnp.zeros((width,), jnp.float32), column_sums(grad_projected[:, 2 * own :]), me * own, 0)
    partial = times_transposed(grad_projected, own_weight)
    by_block = partial.astype(jnp.bfloat16).reshape(2, 2, rows, width)
    core, chip = me % 2, me // 2
    away = lax.dynamic_index_in_dim(by_block, 1 - core, 1, False)
    stay = lax.dynamic_index_in_dim(by_block, core, 1, False)
    half = stay + exchange(away, "blk", 1)
    grad_from_attn = lax.dynamic_index_in_dim(half, chip, 0, False).astype(jnp.float32) + exchange(
        lax.dynamic_index_in_dim(half, 1 - chip, 0, False), "blk", 2
    ).astype(jnp.float32)
    grad_first, gain_zero, shift_zero = pull_first(grad_from_attn)
    token_grad = (grad_middle + grad_first).astype(jnp.bfloat16)
    small = jnp.stack(
        [gain_zero, gain_one, gain_two, gain_three, shift_zero, shift_one, shift_two, shift_three, bias_query, bias_value, bias_two, bias_three]
    )
    parts = lax.axis_size("dp")
    packed = jnp.concatenate(
        [small.reshape(12, parts, -1).transpose(1, 0, 2).reshape(parts, -1), hidden_bias.reshape(parts, -1)], 1
    )
    packed = lax.psum(lax.psum_scatter(packed, "dp", scatter_dimension=0, tiled=True), "blk")[0]
    small = packed[: 12 * width // parts].reshape(12, -1)
    return (
        mixed,
        token_grad,
        qkv_grad,
        out_grad,
        up_grad,
        down_grad,
        small[:4],
        small[4:8],
        small[8:],
        packed[12 * width // parts :],
    )


def solution(mesh):
    return jax.shard_map(
        local,
        mesh=mesh,
        in_specs=(P(("dp", "blk"), None), P(("dp", "blk"), None), P("dp", None)) + (P(),) * 8,
        out_specs=(P(("dp", "blk"), None), P(("dp", "blk"), None))
        + (P("dp", "blk"),) * 4
        + (P(None, "dp"),) * 3
        + (P("dp"),),
        check_vma=False,
    )
```

time: 2320 us -> 761 us (0.33)
  waiting for transfers between devices: 1540 us -> 339 us
  matrix products: 380 us -> 126 us
  Pallas kernels: 0 us -> 111 us
  other arithmetic: 163 us -> 55.2 us
  local copies, waits for them, and re-layouts: 135 us -> 56.5 us
  loops' own time: 28.8 us -> 0 us
    reduce_scatter x8 -> x4, waiting for transfers between devices: 896 us -> 132 us  [the longest x3 132 us: reduced_outer(): lax.psum_scatter(quarter, 'dp', scatter_dimension=0, tiled=True)]
    unnamed x18 -> x7, waiting for transfers between devices: 567 us -> 30.2 us
    dot_general x12 -> x5, matrix products: 299 us -> 53 us  [the longest x4 44.9 us: times_transposed(): return lax.dot_general(left, right, NT, preferred_element_type=jnp.float32)]
    pallas_call x0 -> x2, Pallas kernels: none -> 111 us  [the longest x1 62 us: attn_bwd(): pl.pallas_call(functools.partial(bwd_kernel, tile=tile, heads=heads), gri...]
    ppermute x0 -> x8, waiting for transfers between devices: none -> 106 us  [exchange(): lax.ppermute(values, axis, [(i, i ^ bit) for i in range(lax.axis_size(axi...]
    reduce_sum x2 -> x0, other arithmetic: 83.7 us -> none  [the longest x1 81 us: update(): jnp.sum(weights_raw, -1)]
    another operation x11 -> x3, local copies, waits for them, and re-layouts: 52.3 us -> 0.01 us  [local(): jnp.stack([gain_zero, gain_one, gain_two, gain_three, shift_zero, shift_o...]
    unnamed x1 -> x0, blocking collectives: 35.2 us -> none
  transfers between devices with their start and end apart: 14 -> 15, of which waited for: 13 -> 9; matrix products, arithmetic and copies ran while one was open for 6% -> 12% of each run, Pallas kernels for 0% -> 0%
where the time goes in v1:
time: 761 us; the launch traced here: 749 us
  waiting for transfers between devices  339 us (45%)
  matrix products  126 us (17%)
  Pallas kernels  111 us (15%)
  local copies, waits for them, and re-layouts  56.5 us (7%)
  other arithmetic  55.2 us (7%)
  blocking collectives  38 us (5%)
  between operations  15.2 us (2%)
  starting transfers between devices  8.41 us (1%)
    reduce_scatter x3, waiting for transfers between devices, reduced_outer(): lax.psum_scatter(quarter, 'dp', scatter_dimension=0, tiled=True)  132 us
    ppermute x8, waiting for transfers between devices, exchange(): lax.ppermute(values, axis, [(i, i ^ bit) for i in range(lax.axis_size(axi...  106 us
    pallas_call x1, Pallas kernels, attn_bwd(): pl.pallas_call(functools.partial(bwd_kernel, tile=tile, heads=heads), gri...  62 us
    all_gather x1, waiting for transfers between devices, local(): first_all = lax.all_gather(first_normed, 'blk', axis=0, tiled=True)  49.7 us
    pallas_call x1, Pallas kernels, attn_fwd(): pl.pallas_call(functools.partial(fwd_kernel, tile=tile, heads=heads), gri...  48.7 us
    dot_general x4, matrix products, times_transposed(): return lax.dot_general(left, right, NT, preferred_element_type=jnp.float32)  44.9 us
    dot_general x7, matrix products, outer_sum(): lax.dot_general(left, right, (((0,), (0,)), ((), ())), preferred_element_...  41.5 us
    unnamed x7, waiting for transfers between devices  30.2 us
  transfers between devices with their start and end apart: 15, of which 9 were waited for; matrix products, arithmetic and copies ran while one was open for 12% of the time, Pallas kernels for 0%

profile of v1, /device:TPU:0, one launch (start us, length us, event | category | flops | bytes accessed | tf_op | source)
XLA Modules:
  0.0 749.3 jit_solution(4080905884318136006)
XLA Ops:
  18.0 49.7 %all-gather.3.cloned.1.call-done = bf16[3328,1024]{1,0:T(8,128)(2,1)} async-done(((bf16[832,1024]{1,0:T(8,128)(2,1)}), bf16[3328,1024]{1,0:T(8,128)(2,1)}) %all-gather.3.cloned.1.call-update) | async-done | bytes 6815760 | tf_op jit(solution)/shard_map/all_gather | solution.py:204
  67.7 8.1 %fusion.52 = f32[3328,768]{1,0:T(8,128)S(1)} fusion(bf16[3328,1024]{1,0:T(8,128)(2,1)} %all-gather.3.cloned.1.call-done, bf16[1024,256]{1,0:T(8,128)(2,1)} %get-tuple-element.70, bf16[1024,256]{1,0:T(8,128)(2,1)} %get-tuple-element.71, bf16[1024,256]{1,0:T(8,128)(2,1)S(1)} %get-tuple-element.69), kind=kOutput, calls=%fused_computation.100 | convolution fusion | flops 5239209984 | bytes 18612224 | tf_op jit(solution)/shard_map/dot_general | solution.py:212
  102.0 48.7 %attn_fwd.1 = (bf16[3328,256]{1,0:T(8,128)(2,1)S(1)}, f32[4,3328]{1,0:T(4,128)S(1)}) custom-call(s32[1,3]{1,0:T(1,128)S(1)} %copy-done.6, bf16[3328,256]{1,0:T(8,128)(2,1)S(1)} %copy-done.2, bf16[3328,256]{1,0:T(8,128)(2,1)S(1)} %copy-done.1, bf16[256,3328]{1,0:T(8,128)(2,1)S(1)} %copy-done.3), custom_call_target="tpu_custom_call" | custom-call | tf_op jit(solution)/shard_map/attn_fwd/pallas_call | solution.py:76
  150.7 24.1 %all_to_all.38 = bf16[4,832,256]{2,1,0:T(8,128)(2,1)S(1)} all-to-all(bf16[4,832,256]{2,1,0:T(8,128)(2,1)S(1)} %bitcast.104), channel_id=1, replica_groups=mesh['dp'=8,'blk'=4] {'blk'}, dimensions={0} | all-to-all | bytes 3407872 | tf_op jit(solution)/shard_map/all_to_all | solution.py:217
  181.1 19.0 %multiply_convert_fusion = (bf16[832,4096]{1,0:T(8,128)(2,1)}, f32[832,4096]{1,0:T(8,128)}) fusion(f32[4096]{0:T(1024)S(1)} %copy-done.39, bf16[832,1024]{1,0:T(8,128)(2,1)S(1)} %add_convert_fusion.6, bf16[1024,4096]{1,0:T(8,128)(2,1)} %param.16), kind=kOutput, calls=%fused_computation.10 | convolution fusion | flops 7013400576 | bytes 30556160 | tf_op jit(solution)/shard_map/dot_general | solution.py:223
  200.1 10.3 %add_reduce_fusion = (f32[832]{0:T(1024)S(1)}, f32[832,1024]{1,0:T(8,128)S(1)}) fusion(f32[1024]{0:T(1024)S(1)} %bitcast.129, bf16[832,4096]{1,0:T(8,128)(2,1)} %get-tuple-element.99, bf16[4096,1024]{1,0:T(8,128)(2,1)S(1)} %bitcast.154), kind=kOutput, calls=%fused_computation.73 | convolution fusion | flops 6981024768 | bytes 18619648 | tf_op jit(solution)/shard_map/dot_general | solution.py:226
  217.7 21.7 %convert_reduce_fusion = (f32[4096]{0:T(1024)S(1)}, bf16[832,4096]{1,0:T(8,128)(2,1)}) fusion(f32[832,4096]{1,0:T(8,128)} %get-tuple-element.100, f32[4096]{0:T(1024)S(1)} %copy-done.39, bf16[832,1024]{1,0:T(8,128)(2,1)} %get-tuple-element.49, bf16[4096,1024]{1,0:T(8,128)(2,1)} %param.17), kind=kOutput, calls=%fused_computation.9 | convolution fusion | flops 7057698816 | bytes 30572544 | tf_op jit(solution)/shard_map/dot_general | solution.py:170
  239.5 13.0 %multiply_reduce_fusion = (f32[1024]{0:T(1024)S(1)}, f32[832]{0:T(1024)S(1)}, f32[1024]{0:T(1024)S(1)}, f32[832,1024]{1,0:T(8,128)S(1)}) fusion(f32[832,1024]{1,0:T(8,128)S(1)} %get-tuple-element.62, f32[832]{0:T(1024)S(1)} %fusion.55, f32[832]{0:T(1024)S(1)} %broadcast_multiply_fusion.1, f32[1024]{0:T(1024)S(1)} %bitcast.135, ...), kind=kOutput, calls=%fused_computation.59 | convolution fusion | flops 6986134528 | bytes 22042368 | tf_op jit(solution)/shard_map/dot_general | solution.py:170
  265.9 21.5 %all-to-all-done.1 = bf16[832,4,256]{2,0,1:T(8,128)(2,1)} async-done(((bf16[832,4,256]{2,0,1:T(8,128)(2,1)}), bf16[832,4,256]{2,0,1:T(8,128)(2,1)}, u32[]{:S(2)}, u32[]{:S(2)}) %all-to-all-start.1) | async-done | bytes 1703968 | tf_op jit(solution)/shard_map/all_to_all | solution.py:245
  287.3 62.0 %attn_bwd.1 = bf16[3328,768]{1,0:T(8,128)(2,1)} custom-call(s32[1,3]{1,0:T(1,128)} %len_ref.3, bf16[3328,256]{1,0:T(8,128)(2,1)} %get-tuple-element.64.q_ref, bf16[3328,256]{1,0:T(8,128)(2,1)} %bitcast.16.do_ref, bf16[3328,256]{1,0:T(8,128)(2,1)} %copy-done.4, f32[4,3328]{1,0:T(4,128)} %copy-done.5, bf16[3328,256]{1,0:T(8,128)(2,1)} %copy.50.k_ref, ...), custom_call_target="tpu_custom_call" | custom-call | tf_op jit(solution)/shard_map/attn_bwd/pallas_call | solution.py:138
  349.4 8.2 %convolution_convert_fusion = bf16[3328,1024]{1,0:T(8,128)(2,1)S(1)} fusion(bf16[3328,768]{1,0:T(8,128)(2,1)} %attn_bwd.1, bf16[1024,256]{1,0:T(8,128)(2,1)S(1)} %copy-done.26, bf16[1024,256]{1,0:T(8,128)(2,1)S(1)} %copy-done.27, bf16[1024,256]{1,0:T(8,128)(2,1)S(1)} %get-tuple-element.69), kind=kOutput, calls=%fused_computation.13 | convolution fusion | flops 5242617856 | bytes 13500416 | tf_op jit(solution)/shard_map/dot_general | solution.py:170
  371.3 6.4 convolution_convert_fusion.2
  381.4 6.4 convolution_convert_fusion.1
  387.9 7.7 %collective-permute-done.3 = bf16[1024,256]{1,0:T(8,128)(2,1)} collective-permute-done((bf16[1024,256]{1,0:T(8,128)(2,1)}, bf16[1024,256]{1,0:T(8,128)(2,1)}, u32[]{:S(2)}, u32[]{:S(2)}) %collective-permute-start.3) | collective-permute-done | bytes 524320 | tf_op jit(solution)/shard_map/ppermute | solution.py:178
  404.3 10.2 %convolution_convert_fusion.4 = bf16[1024,768]{1,0:T(8,128)(2,1)} fusion(bf16[3328,1024]{1,0:T(8,128)(2,1)} %all-gather.3.cloned.1.call-done, bf16[3328,768]{1,0:T(8,128)(2,1)} %attn_bwd.1), kind=kOutput, calls=%fused_computation.83 | convolution fusion | flops 5235277824 | bytes 13500416 | tf_op jit(solution)/shard_map/dot_general | solution.py:166
  417.6 7.1 add_convert_fusion.1
  428.1 16.3 %collective-permute-done.1 = bf16[832,1024]{1,0:T(8,128)(2,1)} collective-permute-done((bf16[832,1024]{1,0:T(8,128)(2,1)}, bf16[832,1024]{1,0:T(8,128)(2,1)}, u32[]{:S(2)}, u32[]{:S(2)}) %collective-permute-start.1) | collective-permute-done | bytes 1703968 | tf_op jit(solution)/shard_map/ppermute | solution.py:178
  451.3 36.6 %collective-permute-done.5 = bf16[1024,1024]{1,0:T(8,128)(2,1)} collective-permute-done((bf16[1024,1024]{1,0:T(8,128)(2,1)}, bf16[1024,1024]{1,0:T(8,128)(2,1)}, u32[]{:S(2)}, u32[]{:S(2)}) %collective-permute-start.5) | collective-permute-done | bytes 2097184 | tf_op jit(solution)/shard_map/ppermute | solution.py:178
  492.0 8.8 %add_convert_fusion = bf16[4096,512]{1,0:T(8,128)(2,1)S(1)} fusion(bf16[4096,512]{1,0:T(8,128)(2,1)} %collective-permute-done.6, bf16[832,4096]{1,0:T(8,128)(2,1)} %get-tuple-element.99, bf16[832,256]{1,0:T(8,128)(2,1)S(1)} %copy-done.29, bf16[832,256]{1,0:T(8,128)(2,1)S(1)} %copy-done.28), kind=kOutput, calls=%fused_computation.11 | convolution fusion | flops 3497656320 | bytes 16056320 | tf_op jit(solution)/shard_map/dot_general | solution.py:166
  501.4 45.8 %collective-permute-done.7 = bf16[4096,256]{1,0:T(8,128)(2,1)S(1)} collective-permute-done((bf16[4096,256]{1,0:T(8,128)(2,1)S(1)}, bf16[4096,256]{1,0:T(8,128)(2,1)S(1)}, u32[]{:S(2)}, u32[]{:S(2)}) %collective-permute-start.7) | collective-permute-done | bytes 2097184 | tf_op jit(solution)/shard_map/ppermute | solution.py:178
  551.0 8.1 %all-gather = bf16[512,768]{1,0:T(8,128)(2,1)} all-gather(bf16[128,768]{1,0:T(8,128)(2,1)} %reduce-scatter.5.cloned.1.call-done), channel_id=2, replica_groups=mesh['dp'=8,'blk'=4] {'blk'}, dimensions={0}, use_global_device_ids=true | all-gather | bytes 983040 | tf_op jit(solution)/shard_map/all_gather | solution.py:249
  569.0 30.1 %all-reduce.3.cloned.1.call-done = f32[8,2048]{1,0:T(8,128)} async-done(((f32[8,2048]{1,0:T(8,128)}), f32[8,2048]{1,0:T(8,128)}) %all-reduce.3.cloned.1.call-update) | async-done | bytes 65552
  607.0 63.4 %reduce-scatter.9.cloned.1.call-done = bf16[128,1024]{1,0:T(8,128)(2,1)} async-done(((bf16[1024,1024]{1,0:T(8,128)(2,1)}), bf16[128,1024]{1,0:T(8,128)(2,1)}) %reduce-scatter.9.cloned.1.call-update) | async-done | bytes 262160 | tf_op jit(solution)/shard_map/reduce_scatter | solution.py:193
  672.1 68.3 %reduce-scatter.11.cloned.1.call-done = bf16[512,256]{1,0:T(8,128)(2,1)} async-done(((bf16[4096,256]{1,0:T(8,128)(2,1)}), bf16[512,256]{1,0:T(8,128)(2,1)}) %reduce-scatter.11.cloned.1.call-update) | async-done | bytes 262160 | tf_op jit(solution)/shard_map/reduce_scatter | solution.py:193
  (212 shorter events, 132.5 us)
Async XLA Ops:
  7.2 168.0 %copy-start = (bf16[1024,1024]{1,0:T(8,128)(2,1)S(1)}, bf16[1024,1024]{1,0:T(8,128)(2,1)}, u32[]{:S(2)}) copy-start(bf16[1024,1024]{1,0:T(8,128)(2,1)} %param.15) | copy-start | bytes 6291460
  7.2 60.5 %all-gather.3.cloned.1.call-start = ((), (), s32[]{:S(2)}) async-start(), calls=%async_computation.6 | async-start | bytes 8519680 | tf_op jit(solution)/shard_map/all_gather | solution.py:204
  150.7 24.4 %copy-start.4 = (bf16[3328,256]{1,0:T(8,128)(2,1)}, bf16[3328,256]{1,0:T(8,128)(2,1)S(1)}, u32[]{:S(2)}) copy-start(bf16[3328,256]{1,0:T(8,128)(2,1)S(1)} %get-tuple-element.12.o_ref) | copy-start | bytes 5111812
  150.7 24.4 %copy-start.5 = (f32[4,3328]{1,0:T(4,128)}, f32[4,3328]{1,0:T(4,128)S(1)}, u32[]{:S(2)}) copy-start(f32[4,3328]{1,0:T(4,128)S(1)} %get-tuple-element.13.lse_ref) | copy-start | bytes 159748
  261.4 25.9 %all-to-all-start.1 = ((bf16[832,4,256]{2,0,1:T(8,128)(2,1)}), bf16[832,4,256]{2,0,1:T(8,128)(2,1)}, u32[]{:S(2)}, u32[]{:S(2)}) async-start(bf16[832,4,256]{2,0,1:T(8,128)(2,1)} %bitcast.109), calls=%async_computation.1 | async-start | bytes 3407872 | tf_op jit(solution)/shard_map/all_to_all | solution.py:245
  265.8 283.7 %reduce-scatter.7.cloned.1.call-start = ((), (), s32[]{:S(2)}) async-start(), calls=%async_computation.8 | async-start | bytes 589824 | tf_op jit(solution)/shard_map/reduce_scatter | solution.py:193
  287.3 62.0 %copy-start.26 = (bf16[1024,256]{1,0:T(8,128)(2,1)S(1)}, bf16[1024,256]{1,0:T(8,128)(2,1)}, u32[]{:S(2)}) copy-start(bf16[1024,256]{1,0:T(8,128)(2,1)} %get-tuple-element.70) | copy-start | bytes 1572868
  287.3 62.0 %copy-start.27 = (bf16[1024,256]{1,0:T(8,128)(2,1)S(1)}, bf16[1024,256]{1,0:T(8,128)(2,1)}, u32[]{:S(2)}) copy-start(bf16[1024,256]{1,0:T(8,128)(2,1)} %get-tuple-element.71) | copy-start | bytes 1572868
  361.5 36.1 %collective-permute-start = (bf16[2,832,1024]{2,1,0:T(8,128)(2,1)}, bf16[2,832,1024]{2,1,0:T(8,128)(2,1)}, u32[]{:S(2)}, u32[]{:S(2)}) collective-permute-start(bf16[2,832,1024]{2,1,0:T(8,128)(2,1)} %dynamic-slice_bitcast_fusion), channel_id=1, source_target_pairs={{0,1},{1,0},{2,3},{3,2},{4,5},{5,4},{6,7},{7,6},{8,9},{9,8},{10,11... | collective-permute-start | bytes 10223624 | tf_op jit(solution)/shard_map/ppermute | solution.py:178
  364.8 14.1 %collective-permute-start.2 = (bf16[1024,512]{1,0:T(8,128)(2,1)S(1)}, bf16[1024,512]{1,0:T(8,128)(2,1)S(1)}, u32[]{:S(2)}, u32[]{:S(2)}) collective-permute-start(bf16[1024,512]{1,0:T(8,128)(2,1)S(1)} %convolution_convert_fusion.5), channel_id=1, source_target_pairs={{0,1},{1,0},{2,3},{3,2},{4,5},{5,4},{6,7},{7,6},{8,9},{9,8},{10,11... | collective-permute-start | bytes 3145736 | tf_op jit(solution)/shard_map/ppermute | solution.py:178
  377.7 39.6 %collective-permute-start.4 = (bf16[1024,2048]{1,0:T(8,128)(2,1)}, bf16[1024,2048]{1,0:T(8,128)(2,1)}, u32[]{:S(2)}, u32[]{:S(2)}) collective-permute-start(bf16[1024,2048]{1,0:T(8,128)(2,1)} %convolution_convert_fusion.2), channel_id=1, source_target_pairs={{0,1},{1,0},{2,3},{3,2},{4,5},{5,4},{6,7},{7,6},{8,9},{9,8},{10,11... | collective-permute-start | bytes 12582920 | tf_op jit(solution)/shard_map/ppermute | solution.py:178
  381.0 14.5 %collective-permute-start.3 = (bf16[1024,256]{1,0:T(8,128)(2,1)}, bf16[1024,256]{1,0:T(8,128)(2,1)}, u32[]{:S(2)}, u32[]{:S(2)}) collective-permute-start(bf16[1024,256]{1,0:T(8,128)(2,1)} %slice.134), channel_id=1, source_target_pairs={{0,2},{1,3},{2,0},{3,1},{4,6},{5,7},{6,4},{7,5},{8,10},{9,11},{10,... | collective-permute-start | bytes 1572872 | tf_op jit(solution)/shard_map/ppermute | solution.py:178
  387.8 104.2 %collective-permute-start.6 = (bf16[4096,512]{1,0:T(8,128)(2,1)}, bf16[4096,512]{1,0:T(8,128)(2,1)}, u32[]{:S(2)}, u32[]{:S(2)}) collective-permute-start(bf16[4096,512]{1,0:T(8,128)(2,1)} %convolution_convert_fusion.1), channel_id=1, source_target_pairs={{0,1},{1,0},{2,3},{3,2},{4,5},{5,4},{6,7},{7,6},{8,9},{9,8},{10,11... | collective-permute-start | bytes 12582920 | tf_op jit(solution)/shard_map/ppermute | solution.py:178
  397.5 153.5 %reduce-scatter.5.cloned.1.call-start = ((), (), s32[]{:S(2)}) async-start(), calls=%async_computation.7 | async-start | bytes 1769472 | tf_op jit(solution)/shard_map/reduce_scatter | solution.py:248
  403.9 40.4 %collective-permute-start.1 = (bf16[832,1024]{1,0:T(8,128)(2,1)}, bf16[832,1024]{1,0:T(8,128)(2,1)}, u32[]{:S(2)}, u32[]{:S(2)}) collective-permute-start(bf16[832,1024]{1,0:T(8,128)(2,1)} %dynamic-slice_bitcast_fusion.1), channel_id=1, source_target_pairs={{0,2},{1,3},{2,0},{3,1},{4,6},{5,7},{6,4},{7,5},{8,10},{9,11},{10,... | collective-permute-start | bytes 5111816 | tf_op jit(solution)/shard_map/ppermute | solution.py:178
  414.5 184.6 %all-reduce.3.cloned.1.call-start = ((), (), s32[]{:S(2)}) async-start(), calls=%async_computation.11 | async-start | bytes 131072
  417.6 26.7 %copy-start.11 = (bf16[2,832,1024]{2,1,0:T(8,128)(2,1)S(1)}, bf16[2,832,1024]{2,1,0:T(8,128)(2,1)}, u32[]{:S(2)}) copy-start(bf16[2,832,1024]{2,1,0:T(8,128)(2,1)} %copy-done.10) | copy-start | bytes 10223620
  426.4 61.4 %collective-permute-start.5 = (bf16[1024,1024]{1,0:T(8,128)(2,1)}, bf16[1024,1024]{1,0:T(8,128)(2,1)}, u32[]{:S(2)}, u32[]{:S(2)}) collective-permute-start(bf16[1024,1024]{1,0:T(8,128)(2,1)} %slice.136), channel_id=1, source_target_pairs={{0,2},{1,3},{2,0},{3,1},{4,6},{5,7},{6,4},{7,5},{8,10},{9,11},{10,... | collective-permute-start | bytes 6291464 | tf_op jit(solution)/shard_map/ppermute | solution.py:178
  451.2 40.8 %copy-start.28 = (bf16[832,256]{1,0:T(8,128)(2,1)S(1)}, bf16[832,256]{1,0:T(8,128)(2,1)}, u32[]{:S(2)}) copy-start(bf16[832,256]{1,0:T(8,128)(2,1)} %get-tuple-element.73) | copy-start | bytes 1277956
  451.2 40.8 %copy-start.29 = (bf16[832,256]{1,0:T(8,128)(2,1)S(1)}, bf16[832,256]{1,0:T(8,128)(2,1)}, u32[]{:S(2)}) copy-start(bf16[832,256]{1,0:T(8,128)(2,1)} %get-tuple-element.76) | copy-start | bytes 1277956
  451.2 219.1 %reduce-scatter.9.cloned.1.call-start = ((), (), s32[]{:S(2)}) async-start(), calls=%async_computation.9 | async-start | bytes 2359296 | tf_op jit(solution)/shard_map/reduce_scatter | solution.py:193
  491.7 248.7 %reduce-scatter.11.cloned.1.call-start = ((), (), s32[]{:S(2)}) async-start(), calls=%async_computation.10 | async-start | bytes 2359296 | tf_op jit(solution)/shard_map/reduce_scatter | solution.py:193
  501.0 47.9 %copy-start.40 = (u32[32]{0:T(128)S(1)}, u32[32]{0:T(128)}, u32[]{:S(2)}) copy-start(u32[32]{0:T(128)} %constant.105) | copy-start | bytes 388
  501.0 46.2 %collective-permute-start.7 = (bf16[4096,256]{1,0:T(8,128)(2,1)S(1)}, bf16[4096,256]{1,0:T(8,128)(2,1)S(1)}, u32[]{:S(2)}, u32[]{:S(2)}) collective-permute-start(bf16[4096,256]{1,0:T(8,128)(2,1)S(1)} %slice.138), channel_id=1, source_target_pairs={{0,2},{1,3},{2,0},{3,1},{4,6},{5,7},{6,4},{7,5},{8,10},{9,11},{10,... | collective-permute-start | bytes 6291464 | tf_op jit(solution)/shard_map/ppermute | solution.py:178
  (36 other events, 265.7 us)
Sparse Core Ops, SparseCore 0:
  15.6 52.0 all-gather.2
  397.6 63.0 reduce-scatter.6
  464.5 63.8 reduce-scatter.4
  531.6 67.4 all-reduce.2
  602.5 67.8 reduce-scatter.8
  673.7 66.6 reduce-scatter.10

commit v2 on v1

v2 whole, which is shorter than its diff:
```python
import functools

import jax
import jax.numpy as jnp
from jax import lax
from jax.experimental import pallas as pl
from jax.experimental.pallas import tpu as pltpu
from jax.sharding import PartitionSpec as P

epsilon = 1e-05
HD = 64
NT = (((1,), (1,)), ((), ()))
NEG = -1e30
TILE = 256


def _bounds(len_ref, qb):
    l0 = len_ref[0, 0]
    e1 = l0 + len_ref[0, 1]

    def start_of(r):
        return jnp.where(r >= e1, e1, jnp.where(r >= l0, l0, 0))

    first = qb * TILE
    s_first, s_last = start_of(first), start_of(first + TILE - 1)
    kmin = s_first // TILE
    kmid = jnp.maximum(kmin, jnp.minimum(qb, (s_last + TILE - 1) // TILE))
    rows = first + lax.broadcasted_iota(jnp.int32, (1, TILE), 1)
    return kmin, kmid, rows, start_of(rows)


def _walk(len_ref, qb, step, carry, wide):
    kmin, kmid, rows, starts = _bounds(len_ref, qb)

    def masked(kb, carry):
        at = pl.multiple_of(kb * TILE, TILE)
        kpos = at + lax.broadcasted_iota(jnp.int32, (TILE, TILE), 0)
        return step(at, TILE, (kpos >= starts) & (kpos <= rows), carry)

    def plain(size):
        def run(kb, carry):
            return step(pl.multiple_of(kb * TILE, TILE), size * TILE, None, carry)

        return run

    carry = lax.fori_loop(kmin, kmid, masked, carry)
    at, left = kmid, qb - kmid
    for size in wide:
        count = left // size
        base = at
        carry = lax.fori_loop(0, count, lambda i, c, base=base, size=size: plain(size)(base + i * size, c), carry)
        at, left = at + count * size, left - count * size
    return masked(qb, carry)


def _fill_masked(dst, value, heads):
    lane = lax.broadcasted_iota(jnp.int32, value.shape, 1) // HD
    for h in range(heads):
        dst[pl.ds(h * TILE, TILE), :] = jnp.where(lane == h, value, jnp.zeros_like(value))


def fwd_kernel(len_ref, q_ref, k_ref, v_ref, o_ref, lse_ref, qm, acc, ps, vt, *, heads, wide):
    qb = pl.program_id(0)

    @pl.when(qb == 0)
    def _():
        vt[...] = v_ref[...].T

    _fill_masked(qm, q_ref[...] * jnp.bfloat16(0.125), heads)
    acc[...] = jnp.zeros_like(acc)

    def step(at, size, mask, carry):
        keys = pl.ds(at, size)
        scores = [
            lax.dot_general(k_ref[keys, :], qm[pl.ds(h * TILE, TILE), :], NT, preferred_element_type=jnp.float32)
            for h in range(heads)
        ]
        out, fades = [], []
        for h in range(heads):
            m, l = carry[h]
            s = scores[h]
            if mask is not None:
                s = jnp.where(mask, s, NEG)
            top = jnp.maximum(m, jnp.max(s, 0, keepdims=True))
            p = jnp.exp(s - top)
            if mask is not None:
                p = jnp.where(mask, p, 0.0)
            fade = jnp.exp(m - top)
            ps[pl.ds(0, size), pl.ds(h * TILE, TILE)] = p.astype(jnp.bfloat16)
            out.append((top, l * fade + jnp.sum(p, 0, keepdims=True)))
            fades.append(fade)
        for h in range(heads):
            lanes = pl.ds(h * HD, HD)
            part = jnp.dot(vt[lanes, keys], ps[pl.ds(0, size), pl.ds(h * TILE, TILE)], preferred_element_type=jnp.float32)
            acc[lanes, :] = acc[lanes, :] * fades[h] + part
        return tuple(out)

    carry = tuple((jnp.full((1, TILE), NEG, jnp.float32), jnp.zeros((1, TILE), jnp.float32)) for _ in range(heads))
    carry = _walk(len_ref, qb, step, carry, wide)
    for h in range(heads):
        m, l = carry[h]
        lse_ref[pl.ds(h, 1), :] = m + jnp.log(l)
        acc[pl.ds(h * HD, HD), :] = acc[pl.ds(h * HD, HD), :] / l
    o_ref[...] = acc[...].T.astype(jnp.bfloat16)


def attn_fwd(lengths, qkv, pair=0, lane=256, wide=(1,)):
    n = qkv.shape[0]
    heads = lane // HD
    return pl.pallas_call(
        functools.partial(fwd_kernel, heads=heads, wide=wide),
        grid_spec=pltpu.PrefetchScalarGridSpec(
            num_scalar_prefetch=1,
            grid=(n // TILE,),
            in_specs=[
                pl.BlockSpec((TILE, lane), lambda i, L: (i, 3 * pair)),
                pl.BlockSpec((n, lane), lambda i, L: (0, 3 * pair + 1)),
                pl.BlockSpec((n, lane), lambda i, L: (0, 3 * pair + 2)),
            ],
            out_specs=[pl.BlockSpec((TILE, lane), lambda i, L: (i, 0)), pl.BlockSpec((heads, TILE), lambda i, L: (0, i))],
            scratch_shapes=[
                pltpu.VMEM((heads * TILE, lane), jnp.bfloat16),
                pltpu.VMEM((lane, TILE), jnp.float32),
                pltpu.VMEM((wide[0] * TILE, heads * TILE), jnp.bfloat16),
                pltpu.VMEM((lane, n), jnp.bfloat16),
            ],
        ),
        out_shape=[jax.ShapeDtypeStruct((n, lane), jnp.bfloat16), jax.ShapeDtypeStruct((heads, n), jnp.float32)],
        compiler_params=pltpu.CompilerParams(vmem_limit_bytes=40 * 2**20),
        cost_estimate=pl.CostEstimate(flops=n * n * lane * 9, bytes_accessed=10 * n * lane, transcendentals=n * n * heads // 2),
        name="attn_fwd",
    )(lengths, qkv, qkv, qkv)


def bwd_kernel(len_ref, q_ref, do_ref, o_ref, lse_ref, k_ref, v_ref, d_ref, qm, dom, ps, ds, dqt, dk, dv, kt, *, heads, wide):
    qb = pl.program_id(0)
    c = heads * HD

    @pl.when(qb == 0)
    def _():
        dk[...] = jnp.zeros_like(dk)
        dv[...] = jnp.zeros_like(dv)
        kt[...] = k_ref[...].T

    _fill_masked(qm, q_ref[...] * jnp.bfloat16(0.125), heads)
    _fill_masked(dom, do_ref[...], heads)
    prod = (do_ref[...].astype(jnp.float32) * o_ref[...].astype(jnp.float32)).T
    delta = [jnp.sum(prod[h * HD : (h + 1) * HD], 0, keepdims=True) for h in range(heads)]
    dqt[...] = jnp.zeros_like(dqt)

    def step(at, size, mask, carry):
        keys = pl.ds(at, size)
        used = pl.ds(0, size)
        for h in range(heads):
            mine = pl.ds(h * TILE, TILE)
            s = lax.dot_general(k_ref[keys, :], qm[mine, :], NT, preferred_element_type=jnp.float32)
            p = jnp.exp(s - lse_ref[pl.ds(h, 1), :])
            if mask is not None:
                p = jnp.where(mask, p, 0.0)
            dp = lax.dot_general(v_ref[keys, :], dom[mine, :], NT, preferred_element_type=jnp.float32)
            ps[used, mine] = p.astype(jnp.bfloat16)
            ds[used, mine] = (p * (dp - delta[h])).astype(jnp.bfloat16)
        dv[keys, :] += jnp.dot(ps[used, :], dom[...], preferred_element_type=jnp.float32)
        dk[keys, :] += jnp.dot(ds[used, :], qm[...], preferred_element_type=jnp.float32)
        for h in range(heads):
            lanes = pl.ds(h * HD, HD)
            dqt[lanes, :] += jnp.dot(kt[lanes, keys], ds[used, pl.ds(h * TILE, TILE)], preferred_element_type=jnp.float32)
        return carry

    _walk(len_ref, qb, step, 0, wide)
    d_ref[pl.ds(pl.multiple_of(qb * TILE, TILE), TILE), pl.ds(0, c)] = (dqt[...] * 0.125).T.astype(jnp.bfloat16)

    @pl.when(qb == pl.num_programs(0) - 1)
    def _():
        d_ref[:, pl.ds(c, c)] = dk[...].astype(jnp.bfloat16)
        d_ref[:, pl.ds(2 * c, c)] = dv[...].astype(jnp.bfloat16)


def attn_bwd(lengths, qkv, do, o, lse, pair=0, lane=256, wide=(1,)):
    n = qkv.shape[0]
    heads = lane // HD
    row = lambda col: pl.BlockSpec((TILE, lane), lambda i, L: (i, col))
    whole = lambda col: pl.BlockSpec((n, lane), lambda i, L: (0, col))
    return pl.pallas_call(
        functools.partial(bwd_kernel, heads=heads, wide=wide),
        grid_spec=pltpu.PrefetchScalarGridSpec(
            num_scalar_prefetch=1,
            grid=(n // TILE,),
            in_specs=[
                row(3 * pair), row(pair), row(0), pl.BlockSpec((heads, TILE), lambda i, L: (0, i)),
                whole(3 * pair + 1), whole(3 * pair + 2),
            ],
            out_specs=pl.BlockSpec((n, 3 * lane), lambda i, L: (0, pair)),
            scratch_shapes=[
                pltpu.VMEM((heads * TILE, lane), jnp.bfloat16),
                pltpu.VMEM((heads * TILE, lane), jnp.bfloat16),
                pltpu.VMEM((wide[0] * TILE, heads * TILE), jnp.bfloat16),
                pltpu.VMEM((wide[0] * TILE, heads * TILE), jnp.bfloat16),
                pltpu.VMEM((lane, TILE), jnp.float32),
                pltpu.VMEM((n, lane), jnp.float32),
                pltpu.VMEM((n, lane), jnp.float32),
                pltpu.VMEM((lane, n), jnp.bfloat16),
            ],
        ),
        out_shape=jax.ShapeDtypeStruct(qkv.shape, jnp.bfloat16),
        compiler_params=pltpu.CompilerParams(vmem_limit_bytes=40 * 2**20),
        cost_estimate=pl.CostEstimate(flops=n * n * lane * 11, bytes_accessed=20 * n * lane, transcendentals=n * n * heads // 2),
        name="attn_bwd",
    )(lengths, qkv, do, o, lse, qkv, qkv)


def _stats(v):
    c = v - jnp.mean(v, -1, keepdims=True)
    r = lax.rsqrt(jnp.mean(c * c, -1, keepdims=True) + epsilon)
    return c * r, r


def _pull(n, r, e):
    return r * (e - jnp.mean(e, -1, keepdims=True) - n * jnp.mean(e * n, -1, keepdims=True))


def _fold(v):
    return jnp.sum(v.reshape(-1, 8, v.shape[-1]), 0)


def _each(total, size, fn):
    def body(i, carry):
        fn(pl.ds(pl.multiple_of(i * size, size), size))
        return carry

    lax.fori_loop(0, total // size, body, 0)


def ffn_kernel(
    order, places,
    x_ref, cot_ref, att_ref, wo_ref, up_ref, down_ref, gain_ref, shift_ref, bias_ref, fb_ref,
    mixed_ref, gmid_ref, gatt_ref, out_away, out_stay, up_away, up_stay, down_away, down_stay, small_ref, hid_ref,
    act, slope, second, second_t, turned, branch, ffn,
    sums, *, tiles, cut, strip,
):
    s = pl.program_id(0)
    rows, width = x_ref.shape
    own = width // 4
    f32 = jnp.float32
    hid = up_ref.shape[1]
    row = lambda ref, i: ref[pl.ds(i, 1), :]

    def turn_into(dst, value):
        flipped = value.T
        for b in range(4):
            dst[pl.ds(b * own, own), :] = dst_rows(flipped, b)

    def dst_rows(flipped, b):
        return flipped[b * own : (b + 1) * own, :]

    @pl.when(s == 0)
    def _():
        sums[...] = jnp.zeros_like(sums)
        for i in range(rows // cut):
            at = pl.ds(i * cut, cut)
            branch[at, :] = jnp.dot(att_ref[at, :], wo_ref[...], preferred_element_type=f32) + row(bias_ref, 2)

        def normed(at):
            n, _ = _stats(branch[at, :])
            m = x_ref[at, :].astype(f32) + n * row(gain_ref, 1) + row(shift_ref, 1)
            gmid_ref[at, :] = m
            n, _ = _stats(m)
            second[at, :] = (n * row(gain_ref, 2) + row(shift_ref, 2)).astype(jnp.bfloat16)

        _each(rows, strip, normed)
        second_t[...] = second[...].T

    @pl.when(s < tiles)
    def _():
        at_hid = pl.ds(pl.multiple_of(s * hid, hid), hid)
        for i in range(rows // cut):
            at = pl.ds(i * cut, cut)
            u = jnp.dot(second[at, :], up_ref[...], preferred_element_type=f32) + fb_ref[...]
            c1, c3 = 0.7978845608028654, 0.7978845608028654 * 0.044715
            sq = u * u
            t = jnp.tanh(u * (c1 + c3 * sq))
            half = 0.5 + 0.5 * t
            a = (u * half).astype(jnp.bfloat16)
            act[at, at_hid] = a
            slope[at, at_hid] = (half + (0.5 * u) * (1.0 - t * t) * (c1 + 3.0 * c3 * sq)).astype(jnp.bfloat16)
            part = jnp.dot(a, down_ref[...], preferred_element_type=f32)

            @pl.when(s == 0)
            def _():
                ffn[at, :] = part + row(bias_ref, 3)

            @pl.when(s > 0)
            def _():
                ffn[at, :] += part

    @pl.when(s == tiles - 1)
    def _():
        def normed(at):
            n, r = _stats(ffn[at, :])
            y = cot_ref[at, :].astype(f32)
            mixed_ref[at, :] = (gmid_ref[at, :] + n * row(gain_ref, 3) + row(shift_ref, 3)).astype(jnp.bfloat16)
            g = _pull(n, r, y * row(gain_ref, 3)).astype(jnp.bfloat16)
            second[at, :] = g
            sums[pl.ds(16, 8), :] += _fold(y * n)
            sums[pl.ds(40, 8), :] += _fold(y)
            sums[pl.ds(56, 8), :] += _fold(g.astype(f32))

        _each(rows, strip, normed)
        flipped = second[...].T
        for b in range(4):
            ffn_rows = pl.ds(pl.multiple_of(places[b] * own, own), own)
            turned[ffn_rows, :] = flipped[b * own : (b + 1) * own, :]

    @pl.when(s >= tiles)
    def _():
        at_hid = pl.ds(pl.multiple_of((s - tiles) * hid, hid), hid)
        pre = []
        for i in range(rows // cut):
            at = pl.ds(i * cut, cut)
            g = lax.dot_general(second[at, :], down_ref[...], NT, preferred_element_type=f32) * slope[at, at_hid].astype(f32)
            g = g.astype(jnp.bfloat16)
            slope[at, at_hid] = g
            pre.append(_fold(g.astype(f32)))
            part = lax.dot_general(g, up_ref[...], NT, preferred_element_type=f32)

            @pl.when(s == tiles)
            def _():
                ffn[at, :] = part

            @pl.when(s > tiles)
            def _():
                ffn[at, :] += part

        hid_ref[0] = jnp.sum(sum(pre), 0, keepdims=True)
        down_grad = jnp.dot(turned[...], act[:, at_hid], preferred_element_type=f32).astype(jnp.bfloat16)
        down_away[0] = down_grad[: width // 2]
        down_stay[0] = down_grad[width // 2 :]
        up_grad = jnp.dot(second_t[...], slope[:, at_hid], preferred_element_type=f32).astype(jnp.bfloat16)

        @pl.when(s < tiles + tiles // 2)
        def _():
            up_away[...] = up_grad.reshape(up_away.shape)

        @pl.when(s >= tiles + tiles // 2)
        def _():
            up_stay[...] = up_grad.reshape(up_stay.shape)

    @pl.when(s == 2 * tiles - 1)
    def _():
        def normed(at):
            n, r = _stats(gmid_ref[at, :])
            y = ffn[at, :]
            gm = cot_ref[at, :].astype(f32) + _pull(n, r, y * row(gain_ref, 2))
            gmid_ref[at, :] = gm
            sums[pl.ds(8, 8), :] += _fold(y * n)
            sums[pl.ds(32, 8), :] += _fold(y)
            n, r = _stats(branch[at, :])
            g = _pull(n, r, gm * row(gain_ref, 1)).astype(jnp.bfloat16)
            second[at, :] = g
            sums[pl.ds(0, 8), :] += _fold(gm * n)
            sums[pl.ds(24, 8), :] += _fold(gm)
            sums[pl.ds(48, 8), :] += _fold(g.astype(f32))

        _each(rows, strip, normed)
        flipped = second[...].T
        for b in range(4):
            at = pl.ds(pl.multiple_of(places[b] * own, own), own)
            turned[at, :] = flipped[b * own : (b + 1) * own, :]
        for i in range(rows // cut):
            at = pl.ds(i * cut, cut)
            gatt_ref[at, :] = lax.dot_general(second[at, :], wo_ref[...], NT, preferred_element_type=f32).astype(jnp.bfloat16)
        grad = jnp.dot(turned[...], att_ref[...], preferred_element_type=f32).astype(jnp.bfloat16)
        out_away[...] = grad[: width // 2]
        out_stay[...] = grad[width // 2 :]
        for i in range(8):
            small_ref[pl.ds(i, 1), :] = jnp.sum(sums[pl.ds(8 * i, 8), :], 0, keepdims=True)


def ffn_both(me, tokens, cotangent, attended, out_weight, up_weight, down_weight, norm_gain, norm_bias, proj_bias, ffn_bias):
    rows, width = tokens.shape
    hidden = up_weight.shape[1]
    tiles = 8
    hid = hidden // tiles
    half = tiles // 2
    bf16, f32 = jnp.bfloat16, jnp.float32
    blocks = jnp.stack([me ^ 3, me ^ 1, me ^ 2, me])
    order = (blocks[:, None] * 2 + jnp.arange(2)[None]).reshape(-1).astype(jnp.int32)
    spot = jnp.arange(4) ^ me
    places = jnp.where(spot == 3, 0, jnp.where(spot == 1, 1, jnp.where(spot == 2, 2, 3))).astype(jnp.int32)
    tile_of = lambda s: lax.rem(s, tiles)
    late = lambda s: jnp.maximum(s - tiles, 0)
    whole = lambda *shape: pl.BlockSpec(shape, lambda s, o, p: (0,) * len(shape))
    once = lambda *shape: pl.BlockSpec(shape, lambda s, o, p: (0,) * len(shape), pipeline_mode=pl.Buffered(1))
    return pl.pallas_call(
        functools.partial(ffn_kernel, tiles=tiles, cut=rows, strip=rows // 4),
        grid_spec=pltpu.PrefetchScalarGridSpec(
            num_scalar_prefetch=2,
            grid=(2 * tiles,),
            in_specs=[
                once(rows, width), once(rows, width), once(rows, width), once(width, width),
                pl.BlockSpec((width, hid), lambda s, o, p: (0, o[tile_of(s)])),
                pl.BlockSpec((hid, width), lambda s, o, p: (o[tile_of(s)], 0)),
                once(4, width), once(4, width), once(4, width),
                pl.BlockSpec((1, hid), lambda s, o, p: (0, o[tile_of(s)])),
            ],
            out_specs=[
                once(rows, width), once(rows, width), once(rows, width),
                once(width // 2, width), once(width // 2, width),
                pl.BlockSpec((8, 1, width // 8, hid), lambda s, o, p: (0, jnp.minimum(late(s), half - 1), 0, 0)),
                pl.BlockSpec((8, 1, width // 8, hid), lambda s, o, p: (0, jnp.maximum(late(s) - half, 0), 0, 0)),
                pl.BlockSpec((1, width // 2, hid), lambda s, o, p: (o[late(s)], 0, 0)),
                pl.BlockSpec((1, width // 2, hid), lambda s, o, p: (o[late(s)], 0, 0)),
                once(8, width),
                pl.BlockSpec((1, 1, hid), lambda s, o, p: (o[late(s)], 0, 0)),
            ],
            scratch_shapes=[
                pltpu.VMEM((rows, hidden), bf16), pltpu.VMEM((rows, hidden), bf16),
                pltpu.VMEM((rows, width), bf16), pltpu.VMEM((width, rows), bf16), pltpu.VMEM((width, rows), bf16),
                pltpu.VMEM((rows, width), f32), pltpu.VMEM((rows, width), f32),
                pltpu.VMEM((64, width), f32),
            ],
        ),
        out_shape=[
            jax.ShapeDtypeStruct((rows, width), bf16), jax.ShapeDtypeStruct((rows, width), f32), jax.ShapeDtypeStruct((rows, width), bf16),
            jax.ShapeDtypeStruct((width // 2, width), bf16), jax.ShapeDtypeStruct((width // 2, width), bf16),
            jax.ShapeDtypeStruct((8, half, width // 8, hid), bf16), jax.ShapeDtypeStruct((8, half, width // 8, hid), bf16),
            jax.ShapeDtypeStruct((tiles, width // 2, hid), bf16), jax.ShapeDtypeStruct((tiles, width // 2, hid), bf16),
            jax.ShapeDtypeStruct((8, width), f32), jax.ShapeDtypeStruct((tiles, 1, hid), f32),
        ],
        compiler_params=pltpu.CompilerParams(vmem_limit_bytes=60 * 2**20),
        cost_estimate=pl.CostEstimate(flops=50 * rows * width * width, bytes_accessed=80 * 2**20, transcendentals=rows * hidden),
        name="ffn_both",
    )(order, places, tokens, cotangent, attended, out_weight, up_weight, down_weight, norm_gain, norm_bias, proj_bias, ffn_bias.reshape(1, -1))


def project_kernel(x_ref, w_hbm, gain_ref, shift_ref, bias_ref, all_ref, qkv_ref, w_ref, w_sems, chip_send, chip_recv, core_send, core_recv, pass_send, pass_recv, *, pieces):
    me = lax.axis_index("blk")
    core = lax.rem(me, 2)
    twin, other, last = me + 1 - 2 * core, lax.rem(me + 2, 4), 3 - me
    rows, width = x_ref.shape
    own = width // 4
    size = rows // pieces
    barrier = pltpu.get_barrier_semaphore()
    for target in (twin, other):
        pl.semaphore_signal(barrier, inc=1, device_id={"blk": target}, device_id_type=pl.DeviceIdType.MESH)
    loads = []
    for third in range(3):
        columns = pl.ds(pl.multiple_of(third * width + me * own, own), own)
        load = pltpu.make_async_copy(w_hbm.at[:, columns], w_ref.at[:, pl.ds(third * own, own)], w_sems.at[third])
        load.start()
        loads.append(load)

    def at(block, i):
        return pl.ds(pl.multiple_of(block * rows + i * size, size), size)

    def send(block, i, target, sends, recvs):
        piece = all_ref.at[at(block, i), :]
        copy = pltpu.make_async_remote_copy(
            src_ref=piece, dst_ref=piece, send_sem=sends.at[i], recv_sem=recvs.at[i],
            device_id={"blk": target}, device_id_type=pl.DeviceIdType.MESH,
        )
        return copy

    def project(block, i):
        where = at(block, i)
        got = jnp.dot(all_ref[where, :], w_ref[...], preferred_element_type=jnp.float32) + bias_ref[...]
        qkv_ref[where, :] = got.astype(jnp.bfloat16)

    sent = []
    for i in range(pieces):
        n, _ = _stats(x_ref[pl.ds(i * size, size), :].astype(jnp.float32))
        all_ref[at(me, i), :] = (n * gain_ref[pl.ds(0, 1), :] + shift_ref[pl.ds(0, 1), :]).astype(jnp.bfloat16)
        if i == 0:
            pl.semaphore_wait(barrier, 2)
        for target, sends, recvs in ((other, chip_send, chip_recv), (twin, core_send, core_recv)):
            copy = send(me, i, target, sends, recvs)
            copy.start()
            sent.append(copy)
    for load in loads:
        load.wait()
    for i in range(pieces):
        project(me, i)
    for i in range(pieces):
        send(twin, i, twin, core_send, core_recv).wait_recv()
        project(twin, i)
    for i in range(pieces):
        send(other, i, other, chip_send, chip_recv).wait_recv()
        copy = send(other, i, twin, pass_send, pass_recv)
        copy.start()
        sent.append(copy)
        project(other, i)
        if i > 0:
            send(last, i - 1, twin, pass_send, pass_recv).wait_recv()
            project(last, i - 1)
    send(last, pieces - 1, twin, pass_send, pass_recv).wait_recv()
    project(last, pieces - 1)
    for copy in sent:
        copy.wait_send()


def gather_project(tokens, qkv_weight, norm_gain, norm_bias, bias):
    rows, width = tokens.shape
    pieces = 4
    vmem = pl.BlockSpec(memory_space=pltpu.VMEM)
    dma = pltpu.SemaphoreType.DMA((pieces,))
    return pl.pallas_call(
        functools.partial(project_kernel, pieces=pieces),
        in_specs=[vmem, pl.BlockSpec(memory_space=pl.ANY), vmem, vmem, vmem],
        out_specs=[vmem, vmem],
        out_shape=[jax.ShapeDtypeStruct((4 * rows, width), jnp.bfloat16), jax.ShapeDtypeStruct((4 * rows, 3 * width // 4), jnp.bfloat16)],
        scratch_shapes=[pltpu.VMEM((width, 3 * width // 4), jnp.bfloat16), pltpu.SemaphoreType.DMA((3,))] + [dma] * 6,
        compiler_params=pltpu.CompilerParams(collective_id=0, has_side_effects=True, vmem_limit_bytes=48 * 2**20),
        name="gather_project",
    )(tokens, qkv_weight, norm_gain, norm_bias, bias)


def outer_sum(left, right):
    return lax.dot_general(left, right, (((0,), (0,)), ((), ())), preferred_element_type=jnp.float32)


def times_transposed(left, right):
    return lax.dot_general(left, right, NT, preferred_element_type=jnp.float32)


def column_sums(values):
    return jnp.sum(values.astype(jnp.float32), 0)


def exchange(values, axis, bit):
    return lax.ppermute(values, axis, [(i, i ^ bit) for i in range(lax.axis_size(axis))])


def plus(left, right):
    return (left.astype(jnp.float32) + right.astype(jnp.float32)).astype(jnp.bfloat16)


def pick(values, index, axis):
    return lax.dynamic_index_in_dim(values, index, axis, False)


def sum_everywhere(values):
    for axis in ("blk", "dp"):
        bit = 1
        while bit < lax.axis_size(axis):
            values = values + exchange(values, axis, bit)
            bit *= 2
    return values


def far_sum(half):
    line = lax.axis_index("dp") // 2
    parts = lax.axis_size("dp")
    if parts > 8:
        groups = [[d for d in range(parts) if d % 2 == b] for b in range(2)]
        return jnp.sum(lax.all_to_all(half, "dp", 0, 0, axis_index_groups=groups).astype(jnp.float32), 0)
    got = [exchange(pick(half, line ^ step, 0), "dp", 2 * step) for step in range(1, parts // 2)]
    return pick(half, line, 0).astype(jnp.float32) + sum(piece.astype(jnp.float32) for piece in got)


def weight_sums(up, down, out):
    parts = lax.axis_size("dp")
    width, hidden = out.shape[1], down.shape[0] * down.shape[2]
    own = width // 4
    if parts == 8:
        thin = own // 4
        pieces = [
            up.reshape(8, 2, -1, hidden // 8),
            down.reshape(8, 2, -1, hidden // 8),
            out.reshape(2, 4, thin, 8, width // 8).transpose(3, 0, 2, 1, 4).reshape(8, 2, thin, width // 2),
        ]
        got = lax.psum_scatter(jnp.concatenate(pieces, 2), "dp", scatter_dimension=0, tiled=False)
        total = got[1].astype(jnp.float32) + exchange(got[0], "blk", 2).astype(jnp.float32)
        up_grad = total[:own].reshape(2, width // 8, -1).transpose(1, 0, 2).reshape(width // 8, -1)
        out_grad = total[2 * own :].reshape(thin, 4, -1).transpose(1, 0, 2).reshape(own, -1)
        return up_grad, total[own : 2 * own].T, out_grad.T
    pieces = [
        up.reshape(8, 2, 2, width // 8, -1).transpose(1, 0, 3, 2, 4).reshape(2, parts, -1),
        down.reshape(8, 2, own, -1).transpose(1, 2, 0, 3).reshape(2, own, parts, -1).transpose(0, 2, 1, 3).reshape(2, parts, -1),
        out.reshape(2, own, parts, -1).transpose(0, 2, 1, 3).reshape(2, parts, -1),
    ]
    ends = [pieces[0].shape[2], pieces[0].shape[2] + pieces[1].shape[2]]
    got = lax.psum_scatter(jnp.concatenate(pieces, 2).transpose(1, 0, 2), "dp", scatter_dimension=0, tiled=False)
    total = got[1].astype(jnp.float32) + exchange(got[0], "blk", 2).astype(jnp.float32)
    up_grad, down_grad, out_grad = total[: ends[0]], total[ends[0] : ends[1]], total[ends[1] :]
    return up_grad.reshape(width // parts, -1), down_grad.reshape(own, -1).T, out_grad.reshape(own, -1).T


def local(tokens, cotangent, lengths, qkv_weight, out_weight, up_weight, down_weight, norm_gain, norm_bias, proj_bias, ffn_bias):
    rows, width = tokens.shape
    blocks = lax.axis_size("blk")
    parts = lax.axis_size("dp")
    me = lax.axis_index("blk")
    core, chip = me % 2, me // 2
    own = width // blocks

    def own_columns(values, third):
        return lax.dynamic_slice_in_dim(values, third * width + me * own, own, values.ndim - 1)

    own_weight = jnp.concatenate([own_columns(qkv_weight, third) for third in range(3)], 1)
    query_bias = lax.dynamic_slice_in_dim(proj_bias[0], me * own, own)
    value_bias = lax.dynamic_slice_in_dim(proj_bias[1], me * own, own)
    own_bias = jnp.concatenate([query_bias, jnp.zeros_like(query_bias), value_bias]).reshape(1, -1)
    first_all, qkv = gather_project(tokens, qkv_weight, norm_gain, norm_bias, own_bias)
    attended_own, log_total = attn_fwd(lengths, qkv)
    attended = lax.all_to_all(attended_own, "blk", split_axis=0, concat_axis=1, tiled=True)

    (mixed, grad_middle, grad_attended, out_away, out_stay, up_away, up_stay, down_away, down_stay, sums, hidden_bias) = ffn_both(
        me, tokens, cotangent, attended, out_weight, up_weight, down_weight, norm_gain, norm_bias, proj_bias, ffn_bias
    )
    grad_own = lax.all_to_all(grad_attended, "blk", split_axis=1, concat_axis=0, tiled=True)
    up_half = plus(up_stay, exchange(up_away, "blk", 1))
    down_half = plus(down_stay, exchange(down_away, "blk", 1))
    out_half = plus(out_stay, exchange(out_away, "blk", 1))
    grad_own, up_half, down_half, out_half = lax.optimization_barrier((grad_own, up_half, down_half, out_half))
    up_grad, down_grad, out_grad = weight_sums(up_half, down_half, out_half)
    grads = attn_bwd(lengths, qkv, grad_own, attended_own, log_total)

    by_block = grads.reshape(2, 2, rows, 3 * own)
    away = times_transposed(pick(by_block, 1 - core, 1).reshape(2 * rows, 3 * own), own_weight).astype(jnp.bfloat16)
    got = exchange(away, "blk", 1)
    stay = times_transposed(pick(by_block, core, 1).reshape(2 * rows, 3 * own), own_weight)
    half = plus(stay, got).reshape(2, rows, width)
    half, grads = lax.optimization_barrier((half, grads))
    far = exchange(pick(half, 1 - chip, 0), "blk", 2)

    term = outer_sum(first_all, grads).astype(jnp.bfloat16).reshape(parts // 2, 2, width // parts, 3 * own)
    near = lax.rem(lax.axis_index("dp"), 2)
    term = plus(pick(term, near, 1), exchange(pick(term, 1 - near, 1), "dp", 1))
    qkv_term = far_sum(term).astype(jnp.bfloat16)
    qkv_blocks = lax.all_gather(qkv_term, "blk", axis=0)
    qkv_rows = qkv_blocks.reshape(blocks, -1, 3, own).transpose(1, 2, 0, 3).reshape(-1, 3 * width)
    qkv_grad = lax.dynamic_slice_in_dim(qkv_rows, me * 3 * own, 3 * own, 1).astype(jnp.float32)

    def spread(values):
        return lax.dynamic_update_slice_in_dim(jnp.zeros((width,), jnp.float32), values, me * own, 0)

    y = pick(half, chip, 0).astype(jnp.float32) + far.astype(jnp.float32)
    n, r = _stats(tokens.astype(jnp.float32))
    token_grad = (grad_middle + _pull(n, r, y * norm_gain[0])).astype(jnp.bfloat16)
    small = jnp.stack(
        [
            jnp.sum(y * n, 0), *sums[:3], jnp.sum(y, 0), *sums[3:6],
            spread(column_sums(grads[:, :own])), spread(column_sums(grads[:, 2 * own :])), *sums[6:],
            *hidden_bias.reshape(-1, width),
        ]
    )
    small = sum_everywhere(small)
    place = lax.axis_index("dp")
    chunk = width // parts
    small_own = lax.dynamic_slice_in_dim(small[:12], place * chunk, chunk, 1)
    hidden = lax.dynamic_slice_in_dim(small[12:].reshape(-1), place * 4 * chunk, 4 * chunk, 0)
    return (mixed, token_grad, qkv_grad, out_grad, up_grad, down_grad, small_own[:4], small_own[4:8], small_own[8:], hidden)


def solution(mesh):
    return jax.shard_map(
        local,
        mesh=mesh,
        in_specs=(P(("dp", "blk"), None), P(("dp", "blk"), None), P("dp", None)) + (P(),) * 8,
        out_specs=(P(("dp", "blk"), None), P(("dp", "blk"), None))
        + (P("dp", "blk"),) * 4
        + (P(None, "dp"),) * 3
        + (P("dp"),),
        check_vma=False,
    )
```

time: 761 us -> 511 us (0.67)
  waiting for transfers between devices: 339 us -> 89.1 us
  Pallas kernels: 111 us -> 247 us
  matrix products: 126 us -> 17.1 us
  starting transfers between devices: 8.41 us -> 41.5 us
  blocking collectives: 38 us -> 10.8 us
  other arithmetic: 55.2 us -> 39 us
  local copies, waits for them, and re-layouts: 56.5 us -> 43.4 us
    pallas_call x2 -> x4, Pallas kernels: 111 us -> 247 us  [the longest x1 91.8 us: ffn_both(): pl.pallas_call(functools.partial(ffn_kernel, tiles=tiles, cut=rows, strip...]
    reduce_scatter x4 -> x1, waiting for transfers between devices: 132 us -> 0.01 us  [weight_sums(): lax.psum_scatter(jnp.concatenate(pieces, 2), 'dp', scatter_dimension=0, t...]
    all_gather x1 -> x0, waiting for transfers between devices: 49.7 us -> none  [local(): first_all = lax.all_gather(first_normed, 'blk', axis=0, tiled=True)]
    ppermute x8 -> x15, waiting for transfers between devices: 106 us -> 65.9 us  [exchange(): lax.ppermute(values, axis, [(i, i ^ bit) for i in range(lax.axis_size(axi...]
    dot_general x4 -> x0, matrix products: 39.5 us -> none  [the longest x1 19 us: local(): jnp.dot(second_normed, up_weight, preferred_element_type=jnp.float32)]
    dot_general x4 -> x2, matrix products: 44.9 us -> 9.11 us  [times_transposed(): return lax.dot_general(left, right, NT, preferred_element_type=jnp.float32)]
    dot_general x7 -> x1, matrix products: 41.5 us -> 8 us  [outer_sum(): lax.dot_general(left, right, (((0,), (0,)), ((), ())), preferred_element_...]
    ppermute x8 -> x15, starting transfers between devices: 3.59 us -> 34.3 us  [exchange(): lax.ppermute(values, axis, [(i, i ^ bit) for i in range(lax.axis_size(axi...]
  transfers between devices with their start and end apart: 15 -> 18, of which waited for: 9 -> 12; matrix products, arithmetic and copies ran while one was open for 12% -> 15% of each run, Pallas kernels for 0% -> 11%
where the time goes in v2:
time: 511 us; the launch traced here: 502 us
  Pallas kernels  247 us (48%)
  waiting for transfers between devices  89.1 us (17%)
  local copies, waits for them, and re-layouts  43.4 us (8%)
  starting transfers between devices  41.5 us (8%)
  other arithmetic  39 us (8%)
  matrix products  17.1 us (3%)
  between operations  14.7 us (3%)
  blocking collectives  10.8 us (2%)
    pallas_call x1, Pallas kernels, ffn_both(): pl.pallas_call(functools.partial(ffn_kernel, tiles=tiles, cut=rows, strip...  91.8 us
    ppermute x15, waiting for transfers between devices, exchange(): lax.ppermute(values, axis, [(i, i ^ bit) for i in range(lax.axis_size(axi...  65.9 us
    pallas_call x1, Pallas kernels, attn_bwd(): pl.pallas_call(functools.partial(bwd_kernel, heads=heads, wide=wide), gri...  57.3 us
    pallas_call x1, Pallas kernels, attn_fwd(): pl.pallas_call(functools.partial(fwd_kernel, heads=heads, wide=wide), gri...  50.4 us
    pallas_call x1, Pallas kernels, gather_project(): pl.pallas_call(functools.partial(project_kernel, pieces=pieces), in_specs...  47.2 us
    ppermute x15, starting transfers between devices, exchange(): lax.ppermute(values, axis, [(i, i ^ bit) for i in range(lax.axis_size(axi...  34.3 us
    all_to_all x1, waiting for transfers between devices, local(): lax.all_to_all(attended_own, 'blk', split_axis=0, concat_axis=1, tiled=True)  20.3 us
    convert_element_type x4, other arithmetic, plus(): (left.astype(jnp.float32) + right.astype(jnp.float32)).astype(jnp.bfloat16)  16.2 us
  transfers between devices with their start and end apart: 18, of which 12 were waited for; matrix products, arithmetic and copies ran while one was open for 15% of the time, Pallas kernels for 11%

profile of v2, /device:TPU:0, one launch (start us, length us, event | category | flops | bytes accessed | tf_op | source)
XLA Modules:
  0.0 502.3 jit_solution(6827132790762568123)
XLA Ops:
  10.9 47.2 %gather_project.1 = (bf16[3328,1024]{1,0:T(8,128)(2,1)}, bf16[3328,768]{1,0:T(8,128)(2,1)}) custom-call(bf16[832,1024]{1,0:T(8,128)(2,1)S(1)} %copy-done, bf16[1024,3072]{1,0:T(8,128)(2,1)} %w_hbm.1, f32[4,1024]{1,0:T(4,128)S(1)} %copy-done.3, f32[4,1024]{1,0:T(4,128)S(1)} %copy-done.4, f32[1,768]{1,0:T(1,128)S(1)} %reshape.163.bias_ref), custom_call_target="tpu_custom_call" | custom-call | tf_op jit(solution)/shard_map/gather_project/pallas_call | solution.py:506
  60.6 50.4 %attn_fwd.1 = (bf16[3328,256]{1,0:T(8,128)(2,1)}, f32[4,3328]{1,0:T(4,128)S(1)}) custom-call(s32[1,3]{1,0:T(1,128)S(1)} %copy-done.7, bf16[3328,768]{1,0:T(8,128)(2,1)S(1)} %copy-done.5, bf16[3328,768]{1,0:T(8,128)(2,1)S(1)} %copy-done.5, bf16[3328,768]{1,0:T(8,128)(2,1)S(1)} %copy-done.5), custom_call_target="tpu_custom_call" | custom-call | flops 25518145536 | bytes 8519680 | tf_op jit(solution)/shard_map/attn_fwd/pallas_call | solution.py:110
  111.1 3.6 all-to-all-start
  115.8 20.3 %all-to-all-done = bf16[4,832,256]{2,1,0:T(8,128)(2,1)S(1)} async-done(((bf16[4,832,256]{2,1,0:T(8,128)(2,1)}), bf16[4,832,256]{2,1,0:T(8,128)(2,1)S(1)}, u32[]{:S(2)}, u32[]{:S(2)}) %all-to-all-start) | async-done | bytes 1703968 | tf_op jit(solution)/shard_map/all_to_all | solution.py:605
  137.5 91.8 %ffn_both.1 = (bf16[832,1024]{1,0:T(8,128)(2,1)}, f32[832,1024]{1,0:T(8,128)}, bf16[832,1024]{1,0:T(8,128)(2,1)}, bf16[512,1024]{1,0:T(8,128)(2,1)}, bf16[512,10...) custom-call(s32[8]{0:T(128)} %add.153.order, ...), custom_call_target="tpu_custom_call" | custom-call | flops 43620761600 | bytes 83886080 | tf_op jit(solution)/shard_map/ffn_both/pallas_call | solution.py:394
  232.7 3.6 all-to-all-start.1
  242.2 7.0 %add_convert_fusion = bf16[8,512,512]{2,1,0:T(8,128)(2,1)} fusion(bf16[8,512,512]{2,1,0:T(8,128)(2,1)} %collective-permute-done.1, bf16[8,512,512]{2,1,0:T(8,128)(2,1)} %get-tuple-element.38), kind=kLoop, calls=%fused_computation.1 | loop fusion | flops 8388608 | bytes 12582912 | tf_op jit(solution)/shard_map/convert_element_type | solution.py:534
  249.1 5.7 %add_convert_fusion.1 = bf16[8,4,128,512]{3,2,1,0:T(8,128)(2,1)} fusion(bf16[8,4,128,512]{3,2,1,0:T(8,128)(2,1)} %collective-permute-done, bf16[8,4,128,512]{3,2,1,0:T(8,128)(2,1)S(1)} %copy-done.10), kind=kLoop, calls=%fused_computation.2 | loop fusion | flops 8388608 | bytes 12582912 | tf_op jit(solution)/shard_map/convert_element_type | solution.py:534
  261.3 7.5 %pad_maximum_fusion = bf16[8,2,576,512]{3,2,1,0:T(8,128)(2,1)} fusion(bf16[8,2,64,512]{3,2,1,0:T(8,128)(2,1)S(1)} %reshape.175, bf16[8,2,256,512]{3,2,1,0:T(8,128)(2,1)} %bitcast.97, bf16[8,2,256,512]{3,2,1,0:T(8,128)(2,1)} %bitcast.98), kind=kLoop, calls=%fused_computation | loop fusion | flops 28311552 | bytes 18874368 | tf_op jit(solution)/shard_map/concatenate | solution.py:571
  272.8 57.3 %attn_bwd.1 = bf16[3328,768]{1,0:T(8,128)(2,1)S(1)} custom-call(s32[1,3]{1,0:T(1,128)S(1)} %copy-done.7, bf16[3328,768]{1,0:T(8,128)(2,1)S(1)} %copy-done.6, bf16[3328,256]{1,0:T(8,128)(2,1)S(1)} %bitcast.96, bf16[3328,256]{1,0:T(8,128)(2,1)} %get-tuple-element.32.o_ref, f32[4,3328]{1,0:T(4,128)S(1)} %get-tuple-element.43.lse_ref, ...), custom_call_target="tpu_custom_call" | custom-call | flops 31188844544 | bytes 17039360 | tf_op jit(solution)/shard_map/attn_bwd/pallas_call | solution.py:184
  333.1 4.4 convolution_convert_fusion
  338.4 5.4 %collective-permute-done.3 = bf16[1664,1024]{1,0:T(8,128)(2,1)} collective-permute-done((bf16[1664,1024]{1,0:T(8,128)(2,1)}, bf16[1664,1024]{1,0:T(8,128)(2,1)}, u32[]{:S(2)}, u32[]{:S(2)}) %collective-permute-start.3) | collective-permute-done | bytes 3407904 | tf_op jit(solution)/shard_map/ppermute | solution.py:530
  343.9 4.7 add_convert_fusion.2
  350.4 8.0 %convolution_convert_fusion.1 = bf16[1024,768]{1,0:T(8,128)(2,1)S(1)} fusion(bf16[3328,1024]{1,0:T(8,128)(2,1)} %get-tuple-element.45, bf16[3328,768]{1,0:T(8,128)(2,1)S(1)} %bitcast.95), kind=kOutput, calls=%fused_computation.28 | convolution fusion | flops 5235277824 | bytes 13500416 | tf_op jit(solution)/shard_map/dot_general | solution.py:518
  370.5 25.3 %collective-permute-done.5 = bf16[4,128,768]{1,2,0:T(8,128)(2,1)} collective-permute-done((bf16[4,128,768]{1,2,0:T(8,128)(2,1)}, bf16[4,128,768]{1,2,0:T(8,128)(2,1)}, u32[]{:S(2)}, u32[]{:S(2)}) %collective-permute-start.5) | collective-permute-done | bytes 786464 | tf_op jit(solution)/shard_map/ppermute | solution.py:530
  397.5 5.5 %collective-permute-start.6 = (bf16[128,768]{0,1:T(8,128)(2,1)S(1)}, bf16[128,768]{0,1:T(8,128)(2,1)S(1)}, u32[]{:S(2)}, u32[]{:S(2)}) collective-permute-start(bf16[128,768]{0,1:T(8,128)(2,1)S(1)} %get-tuple-element.97), channel_id=1, source_target_pairs={{0,8},{4,12},{8,0},{12,4},{16,24},{20,28},{24,16},{28,20},{1,9},{5... | collective-permute-start | bytes 589832 | tf_op jit(solution)/shard_map/ppermute | solution.py:530
  406.3 8.7 %collective-permute-done.6 = bf16[128,768]{0,1:T(8,128)(2,1)S(1)} collective-permute-done((bf16[128,768]{0,1:T(8,128)(2,1)S(1)}, bf16[128,768]{0,1:T(8,128)(2,1)S(1)}, u32[]{:S(2)}, u32[]{:S(2)}) %collective-permute-start.6) | collective-permute-done | bytes 196640 | tf_op jit(solution)/shard_map/ppermute | solution.py:530
  415.0 7.5 %collective-permute-done.7 = bf16[128,768]{0,1:T(8,128)(2,1)S(1)} collective-permute-done((bf16[128,768]{0,1:T(8,128)(2,1)S(1)}, bf16[128,768]{0,1:T(8,128)(2,1)S(1)}, u32[]{:S(2)}, u32[]{:S(2)}) %collective-permute-start.7) | collective-permute-done | bytes 196640 | tf_op jit(solution)/shard_map/ppermute | solution.py:530
  422.6 6.8 %collective-permute-done.8 = bf16[128,768]{0,1:T(8,128)(2,1)S(1)} collective-permute-done((bf16[128,768]{0,1:T(8,128)(2,1)S(1)}, bf16[128,768]{0,1:T(8,128)(2,1)S(1)}, u32[]{:S(2)}, u32[]{:S(2)}) %collective-permute-start.8) | collective-permute-done | bytes 196640 | tf_op jit(solution)/shard_map/ppermute | solution.py:530
  433.2 10.8 %all-gather = bf16[512,768]{0,1:T(8,128)(2,1)} all-gather(bf16[128,768]{0,1:T(8,128)(2,1)} %fusion.17), channel_id=2, replica_groups=mesh['dp'=8,'blk'=4] {'blk'}, dimensions={0}, use_global_device_ids=true | all-gather | bytes 983040 | tf_op jit(solution)/shard_map/all_gather | solution.py:630
  457.3 14.9 %collective-permute-start.13 = (f32[16,1024]{1,0:T(8,128)S(1)}, f32[16,1024]{1,0:T(8,128)S(1)}, u32[]{:S(2)}, u32[]{:S(2)}) collective-permute-start(f32[16,1024]{1,0:T(8,128)S(1)} %add.185), channel_id=1, source_target_pairs={{0,8},{4,12},{8,0},{12,4},{16,24},{20,28},{24,16},{28,20},{1,9},{5... | collective-permute-start | bytes 196616 | tf_op jit(solution)/shard_map/ppermute | solution.py:530
  474.5 4.6 collective-permute-start.14
  481.1 4.5 fusion.9
  486.9 5.3 %collective-permute-done.9 = bf16[576,512]{1,0:T(8,128)(2,1)S(1)} collective-permute-done((bf16[576,512]{1,0:T(8,128)(2,1)S(1)}, bf16[576,512]{1,0:T(8,128)(2,1)S(1)}, u32[]{:S(2)}, u32[]{:S(2)}) %collective-permute-start.9) | collective-permute-done | bytes 589856 | tf_op jit(solution)/shard_map/ppermute | solution.py:530
  (130 shorter events, 76.9 us)
Async XLA Ops:
  10.9 47.2 %copy-start.7 = (s32[1,3]{1,0:T(1,128)S(1)}, s32[1,3]{1,0:T(1,128)}, u32[]{:S(2)}) copy-start(s32[1,3]{1,0:T(1,128)} %len_ref.3) | copy-start | bytes 40
  111.1 25.0 %all-to-all-start = ((bf16[4,832,256]{2,1,0:T(8,128)(2,1)}), bf16[4,832,256]{2,1,0:T(8,128)(2,1)S(1)}, u32[]{:S(2)}, u32[]{:S(2)}) async-start(bf16[4,832,256]{2,1,0:T(8,128)(2,1)} %bitcast.6), calls=%async_computation | async-start | bytes 3407872 | tf_op jit(solution)/shard_map/all_to_all | solution.py:605
  229.3 12.8 %collective-permute-start.1 = (bf16[8,512,512]{2,1,0:T(8,128)(2,1)}, bf16[8,512,512]{2,1,0:T(8,128)(2,1)}, u32[]{:S(2)}, u32[]{:S(2)}) collective-permute-start(bf16[8,512,512]{2,1,0:T(8,128)(2,1)} %get-tuple-element.39), channel_id=1, source_target_pairs={{0,1},{1,0},{2,3},{3,2},{4,5},{5,4},{6,7},{7,6},{8,9},{9,8},{10,11... | collective-permute-start | bytes 12582920 | tf_op jit(solution)/shard_map/ppermute | solution.py:530
  229.4 19.7 %collective-permute-start = (bf16[8,4,128,512]{3,2,1,0:T(8,128)(2,1)}, bf16[8,4,128,512]{3,2,1,0:T(8,128)(2,1)}, u32[]{:S(2)}, u32[]{:S(2)}) collective-permute-start(bf16[8,4,128,512]{3,2,1,0:T(8,128)(2,1)} %get-tuple-element.37), channel_id=1, source_target_pairs={{0,1},{1,0},{2,3},{3,2},{4,5},{5,4},{6,7},{7,6},{8,9},{9,8},{10,11... | collective-permute-start | bytes 12582920 | tf_op jit(solution)/shard_map/ppermute | solution.py:530
  229.9 9.3 %collective-permute-start.2 = (bf16[512,1024]{1,0:T(8,128)(2,1)}, bf16[512,1024]{1,0:T(8,128)(2,1)S(1)}, u32[]{:S(2)}, u32[]{:S(2)}) collective-permute-start(bf16[512,1024]{1,0:T(8,128)(2,1)} %get-tuple-element.41), channel_id=1, source_target_pairs={{0,1},{1,0},{2,3},{3,2},{4,5},{5,4},{6,7},{7,6},{8,9},{9,8},{10,11... | collective-permute-start | bytes 3145736 | tf_op jit(solution)/shard_map/ppermute | solution.py:530
  232.7 25.0 %all-to-all-start.1 = ((bf16[832,4,256]{2,0,1:T(8,128)(2,1)}), bf16[832,4,256]{2,0,1:T(8,128)(2,1)S(1)}, u32[]{:S(2)}, u32[]{:S(2)}) async-start(bf16[832,4,256]{2,0,1:T(8,128)(2,1)} %bitcast.90), calls=%async_computation.1 | async-start | bytes 3407872 | tf_op jit(solution)/shard_map/all_to_all | solution.py:610
  236.3 242.7 %reduce-scatter.2.cloned.1.call-start = ((), (), s32[]{:S(2)}) async-start(), calls=%async_computation.3 | async-start | bytes 10616832 | tf_op jit(solution)/shard_map/reduce_scatter | solution.py:571
  337.5 6.4 %collective-permute-start.3 = (bf16[1664,1024]{1,0:T(8,128)(2,1)}, bf16[1664,1024]{1,0:T(8,128)(2,1)}, u32[]{:S(2)}, u32[]{:S(2)}) collective-permute-start(bf16[1664,1024]{1,0:T(8,128)(2,1)} %convolution_convert_fusion), channel_id=1, source_target_pairs={{0,1},{1,0},{2,3},{3,2},{4,5},{5,4},{6,7},{7,6},{8,9},{9,8},{10,11... | collective-permute-start | bytes 10223624 | tf_op jit(solution)/shard_map/ppermute | solution.py:530
  337.8 12.6 %slice-start = ((s8[5111808]{0:T(1024)(128)(4,1)}), s8[4194304]{0:T(1024)(128)(4,1)S(1)}, s32[]{:S(2)}) async-start(s8[5111808]{0:T(1024)(128)(4,1)} %bitcast.94), calls=%async_computation.4 | async-start | bytes 8388608
  350.0 80.1 %collective-permute-start.4 = (bf16[832,1024]{1,0:T(8,128)(2,1)}, bf16[832,1024]{1,0:T(8,128)(2,1)S(1)}, u32[]{:S(2)}, u32[]{:S(2)}) collective-permute-start(bf16[832,1024]{1,0:T(8,128)(2,1)} %dynamic-slice_bitcast_fusion), channel_id=1, source_target_pairs={{0,2},{1,3},{2,0},{3,1},{4,6},{5,7},{6,4},{7,5},{8,10},{9,11},{10,... | collective-permute-start | bytes 5111816 | tf_op jit(solution)/shard_map/ppermute | solution.py:530
  362.1 33.7 %collective-permute-start.5 = (bf16[4,128,768]{1,2,0:T(8,128)(2,1)}, bf16[4,128,768]{1,2,0:T(8,128)(2,1)}, u32[]{:S(2)}, u32[]{:S(2)}) collective-permute-start(bf16[4,128,768]{1,2,0:T(8,128)(2,1)} %bitcast.113), channel_id=1, source_target_pairs={{0,4},{4,0},{8,12},{12,8},{16,20},{20,16},{24,28},{28,24},{1,5},{5... | collective-permute-start | bytes 2359304 | tf_op jit(solution)/shard_map/ppermute | solution.py:530
  367.9 62.2 %copy-start.9 = (bf16[1664,1024]{1,0:T(8,128)(2,1)S(1)}, bf16[1664,1024]{1,0:T(8,128)(2,1)}, u32[]{:S(2)}) copy-start(bf16[1664,1024]{1,0:T(8,128)(2,1)} %copy-done.8) | copy-start | bytes 10223620
  397.4 34.9 %copy-start.15 = (f32[2,1024]{1,0:T(2,128)S(1)}, f32[2,1024]{1,0:T(2,128)}, u32[]{:S(2)}) copy-start(f32[2,1024]{1,0:T(2,128)} %unstack.36) | copy-start | bytes 24580
  397.4 34.9 %copy-start.17 = (f32[2,1,512]{2,1,0:T(1,128)S(1)}, f32[2,1,512]{2,1,0:T(1,128)}, u32[]{:S(2)}) copy-start(f32[2,1,512]{2,1,0:T(1,128)} %get-tuple-element.105) | copy-start | bytes 12292
  397.4 34.9 %copy-start.18 = (f32[2,1,512]{2,1,0:T(1,128)S(1)}, f32[2,1,512]{2,1,0:T(1,128)}, u32[]{:S(2)}) copy-start(f32[2,1,512]{2,1,0:T(1,128)} %get-tuple-element.106) | copy-start | bytes 12292
  397.5 17.5 %collective-permute-start.6 = (bf16[128,768]{0,1:T(8,128)(2,1)S(1)}, bf16[128,768]{0,1:T(8,128)(2,1)S(1)}, u32[]{:S(2)}, u32[]{:S(2)}) collective-permute-start(bf16[128,768]{0,1:T(8,128)(2,1)S(1)} %get-tuple-element.97), channel_id=1, source_target_pairs={{0,8},{4,12},{8,0},{12,4},{16,24},{20,28},{24,16},{28,20},{1,9},{5... | collective-permute-start | bytes 589832 | tf_op jit(solution)/shard_map/ppermute | solution.py:530
  403.0 19.5 %collective-permute-start.7 = (bf16[128,768]{0,1:T(8,128)(2,1)S(1)}, bf16[128,768]{0,1:T(8,128)(2,1)S(1)}, u32[]{:S(2)}, u32[]{:S(2)}) collective-permute-start(bf16[128,768]{0,1:T(8,128)(2,1)S(1)} %get-tuple-element.99), channel_id=1, source_target_pairs={{0,16},{4,20},{8,24},{12,28},{16,0},{20,4},{24,8},{28,12},{1,17},{... | collective-permute-start | bytes 589832 | tf_op jit(solution)/shard_map/ppermute | solution.py:530
  404.9 24.4 %collective-permute-start.8 = (bf16[128,768]{0,1:T(8,128)(2,1)S(1)}, bf16[128,768]{0,1:T(8,128)(2,1)S(1)}, u32[]{:S(2)}, u32[]{:S(2)}) collective-permute-start(bf16[128,768]{0,1:T(8,128)(2,1)S(1)} %get-tuple-element.98), channel_id=1, source_target_pairs={{0,24},{4,28},{8,16},{12,20},{16,8},{20,12},{24,0},{28,4},{1,25},{... | collective-permute-start | bytes 589832 | tf_op jit(solution)/shard_map/ppermute | solution.py:530
  433.1 14.6 %collective-permute-start.10 = (f32[16,1024]{1,0:T(8,128)S(1)}, f32[16,1024]{1,0:T(8,128)}, u32[]{:S(2)}, u32[]{:S(2)}) collective-permute-start(f32[16,1024]{1,0:T(8,128)S(1)} %stack.43), channel_id=1, source_target_pairs={{0,1},{1,0},{2,3},{3,2},{4,5},{5,4},{6,7},{7,6},{8,9},{9,8},{10,11... | collective-permute-start | bytes 196616 | tf_op jit(solution)/shard_map/ppermute | solution.py:530
  448.6 4.4 collective-permute-start.11
  453.0 4.3 collective-permute-start.12
  457.3 17.1 %collective-permute-start.13 = (f32[16,1024]{1,0:T(8,128)S(1)}, f32[16,1024]{1,0:T(8,128)S(1)}, u32[]{:S(2)}, u32[]{:S(2)}) collective-permute-start(f32[16,1024]{1,0:T(8,128)S(1)} %add.185), channel_id=1, source_target_pairs={{0,8},{4,12},{8,0},{12,4},{16,24},{20,28},{24,16},{28,20},{1,9},{5... | collective-permute-start | bytes 196616 | tf_op jit(solution)/shard_map/ppermute | solution.py:530
  474.5 11.1 %collective-permute-start.14 = (f32[16,1024]{1,0:T(8,128)S(1)}, f32[16,1024]{1,0:T(8,128)S(1)}, u32[]{:S(2)}, u32[]{:S(2)}) collective-permute-start(f32[16,1024]{1,0:T(8,128)S(1)} %add.186), channel_id=1, source_target_pairs={{0,16},{4,20},{8,24},{12,28},{16,0},{20,4},{24,8},{28,12},{1,17},{... | collective-permute-start | bytes 196616 | tf_op jit(solution)/shard_map/ppermute | solution.py:530
  480.1 12.1 %collective-permute-start.9 = (bf16[576,512]{1,0:T(8,128)(2,1)S(1)}, bf16[576,512]{1,0:T(8,128)(2,1)S(1)}, u32[]{:S(2)}, u32[]{:S(2)}) collective-permute-start(bf16[576,512]{1,0:T(8,128)(2,1)S(1)} %slice_bitcast_fusion), channel_id=1, source_target_pairs={{0,2},{1,3},{2,0},{3,1},{4,6},{5,7},{6,4},{7,5},{8,10},{9,11},{10,... | collective-permute-start | bytes 1769480 | tf_op jit(solution)/shard_map/ppermute | solution.py:530
  (15 other events, 69.7 us)
Sparse Core Ops, SparseCore 0:
  268.9 193.5 reduce-scatter.1

commit v3 on v2

--- a/solution.py
+++ b/solution.py
@@ -223,6 +223,10 @@
     return jnp.sum(v.reshape(-1, 8, v.shape[-1]), 0)
 
 
+def _row(ref, i):
+    return ref[pl.ds(i, 1), :]
+
+
 def _each(total, size, fn):
     def body(i, carry):
         fn(pl.ds(pl.multiple_of(i * size, size), size))
@@ -231,206 +235,360 @@
     lax.fori_loop(0, total // size, body, 0)
 
 
+def _turn_blocks(dst, value, core):
+    own = dst.shape[0] // 4
+    flipped = value.T
+    for b in range(4):
+        stays = 1 - lax.rem(core + b % 2, 2)
+        dst[pl.ds(pl.multiple_of((2 * stays + b // 2) * own, own), own), :] = flipped[b * own : (b + 1) * own, :]
+
+
 def ffn_kernel(
-    order, places,
     x_ref, cot_ref, att_ref, wo_ref, up_ref, down_ref, gain_ref, shift_ref, bias_ref, fb_ref,
-    mixed_ref, gmid_ref, gatt_ref, out_away, out_stay, up_away, up_stay, down_away, down_stay, small_ref, hid_ref,
-    act, slope, second, second_t, turned, branch, ffn,
-    sums, *, tiles, cut, strip,
+    mixed_ref, mid_ref, n_ref, r_ref, low_ref, turned_ref, second_t, act_ref, slope_ref, small_ref,
+    second, branch, ffn, sums, *, tiles, strip,
 ):
     s = pl.program_id(0)
     rows, width = x_ref.shape
-    own = width // 4
     f32 = jnp.float32
-    hid = up_ref.shape[1]
-    row = lambda ref, i: ref[pl.ds(i, 1), :]
-
-    def turn_into(dst, value):
-        flipped = value.T
-        for b in range(4):
-            dst[pl.ds(b * own, own), :] = dst_rows(flipped, b)
-
-    def dst_rows(flipped, b):
-        return flipped[b * own : (b + 1) * own, :]
 
     @pl.when(s == 0)
     def _():
         sums[...] = jnp.zeros_like(sums)
-        for i in range(rows // cut):
-            at = pl.ds(i * cut, cut)
-            branch[at, :] = jnp.dot(att_ref[at, :], wo_ref[...], preferred_element_type=f32) + row(bias_ref, 2)
+        branch[...] = jnp.dot(att_ref[...], wo_ref[...], preferred_element_type=f32) + _row(bias_ref, 2)
 
         def normed(at):
-            n, _ = _stats(branch[at, :])
-            m = x_ref[at, :].astype(f32) + n * row(gain_ref, 1) + row(shift_ref, 1)
-            gmid_ref[at, :] = m
+            n, r = _stats(branch[at, :])
+            n_ref[at, :] = n.astype(jnp.bfloat16)
+            r_ref[at, :] = r
+            m = x_ref[at, :].astype(f32) + n * _row(gain_ref, 1) + _row(shift_ref, 1)
+            mid_ref[at, :] = m
             n, _ = _stats(m)
-            second[at, :] = (n * row(gain_ref, 2) + row(shift_ref, 2)).astype(jnp.bfloat16)
+            second[at, :] = (n * _row(gain_ref, 2) + _row(shift_ref, 2)).astype(jnp.bfloat16)
 
         _each(rows, strip, normed)
         second_t[...] = second[...].T
 
-    @pl.when(s < tiles)
-    def _():
-        at_hid = pl.ds(pl.multiple_of(s * hid, hid), hid)
-        for i in range(rows // cut):
-            at = pl.ds(i * cut, cut)
-            u = jnp.dot(second[at, :], up_ref[...], preferred_element_type=f32) + fb_ref[...]
-            c1, c3 = 0.7978845608028654, 0.7978845608028654 * 0.044715
-            sq = u * u
-            t = jnp.tanh(u * (c1 + c3 * sq))
-            half = 0.5 + 0.5 * t
-            a = (u * half).astype(jnp.bfloat16)
-            act[at, at_hid] = a
-            slope[at, at_hid] = (half + (0.5 * u) * (1.0 - t * t) * (c1 + 3.0 * c3 * sq)).astype(jnp.bfloat16)
-            part = jnp.dot(a, down_ref[...], preferred_element_type=f32)
-
-            @pl.when(s == 0)
-            def _():
-                ffn[at, :] = part + row(bias_ref, 3)
-
-            @pl.when(s > 0)
-            def _():
-                ffn[at, :] += part
+    u = jnp.dot(second[...], up_ref[...], preferred_element_type=f32) + fb_ref[...]
+    c1, c3 = 0.7978845608028654, 0.7978845608028654 * 0.044715
+    sq = u * u
+    t = jnp.tanh(u * (c1 + c3 * sq))
+    half = 0.5 + 0.5 * t
+    a = (u * half).astype(jnp.bfloat16)
+    act_ref[...] = a
+    slope_ref[...] = (half + (0.5 * u) * (1.0 - t * t) * (c1 + 3.0 * c3 * sq)).astype(jnp.bfloat16)
+    part = jnp.dot(a, down_ref[...], preferred_element_type=f32)
+
+    @pl.when(s == 0)
+    def _():
+        ffn[...] = part + _row(bias_ref, 3)
+
+    @pl.when(s > 0)
+    def _():
+        ffn[...] += part
 
     @pl.when(s == tiles - 1)
     def _():
         def normed(at):
             n, r = _stats(ffn[at, :])
             y = cot_ref[at, :].astype(f32)
-            mixed_ref[at, :] = (gmid_ref[at, :] + n * row(gain_ref, 3) + row(shift_ref, 3)).astype(jnp.bfloat16)
-            g = _pull(n, r, y * row(gain_ref, 3)).astype(jnp.bfloat16)
-            second[at, :] = g
-            sums[pl.ds(16, 8), :] += _fold(y * n)
-            sums[pl.ds(40, 8), :] += _fold(y)
-            sums[pl.ds(56, 8), :] += _fold(g.astype(f32))
+            mixed_ref[at, :] = (mid_ref[at, :] + n * _row(gain_ref, 3) + _row(shift_ref, 3)).astype(jnp.bfloat16)
+            g = _pull(n, r, y * _row(gain_ref, 3)).astype(jnp.bfloat16)
+            low_ref[at, :] = g
+            sums[pl.ds(0, 8), :] += _fold(y * n)
+            sums[pl.ds(8, 8), :] += _fold(y)
+            sums[pl.ds(16, 8), :] += _fold(g.astype(f32))
 
         _each(rows, strip, normed)
-        flipped = second[...].T
-        for b in range(4):
-            ffn_rows = pl.ds(pl.multiple_of(places[b] * own, own), own)
-            turned[ffn_rows, :] = flipped[b * own : (b + 1) * own, :]
-
-    @pl.when(s >= tiles)
-    def _():
-        at_hid = pl.ds(pl.multiple_of((s - tiles) * hid, hid), hid)
-        pre = []
-        for i in range(rows // cut):
-            at = pl.ds(i * cut, cut)
-            g = lax.dot_general(second[at, :], down_ref[...], NT, preferred_element_type=f32) * slope[at, at_hid].astype(f32)
-            g = g.astype(jnp.bfloat16)
-            slope[at, at_hid] = g
-            pre.append(_fold(g.astype(f32)))
-            part = lax.dot_general(g, up_ref[...], NT, preferred_element_type=f32)
-
-            @pl.when(s == tiles)
-            def _():
-                ffn[at, :] = part
-
-            @pl.when(s > tiles)
-            def _():
-                ffn[at, :] += part
-
-        hid_ref[0] = jnp.sum(sum(pre), 0, keepdims=True)
-        down_grad = jnp.dot(turned[...], act[:, at_hid], preferred_element_type=f32).astype(jnp.bfloat16)
-        down_away[0] = down_grad[: width // 2]
-        down_stay[0] = down_grad[width // 2 :]
-        up_grad = jnp.dot(second_t[...], slope[:, at_hid], preferred_element_type=f32).astype(jnp.bfloat16)
-
-        @pl.when(s < tiles + tiles // 2)
-        def _():
-            up_away[...] = up_grad.reshape(up_away.shape)
-
-        @pl.when(s >= tiles + tiles // 2)
-        def _():
-            up_stay[...] = up_grad.reshape(up_stay.shape)
-
-    @pl.when(s == 2 * tiles - 1)
-    def _():
-        def normed(at):
-            n, r = _stats(gmid_ref[at, :])
-            y = ffn[at, :]
-            gm = cot_ref[at, :].astype(f32) + _pull(n, r, y * row(gain_ref, 2))
-            gmid_ref[at, :] = gm
-            sums[pl.ds(8, 8), :] += _fold(y * n)
-            sums[pl.ds(32, 8), :] += _fold(y)
-            n, r = _stats(branch[at, :])
-            g = _pull(n, r, gm * row(gain_ref, 1)).astype(jnp.bfloat16)
-            second[at, :] = g
-            sums[pl.ds(0, 8), :] += _fold(gm * n)
-            sums[pl.ds(24, 8), :] += _fold(gm)
-            sums[pl.ds(48, 8), :] += _fold(g.astype(f32))
-
-        _each(rows, strip, normed)
-        flipped = second[...].T
-        for b in range(4):
-            at = pl.ds(pl.multiple_of(places[b] * own, own), own)
-            turned[at, :] = flipped[b * own : (b + 1) * own, :]
-        for i in range(rows // cut):
-            at = pl.ds(i * cut, cut)
-            gatt_ref[at, :] = lax.dot_general(second[at, :], wo_ref[...], NT, preferred_element_type=f32).astype(jnp.bfloat16)
-        grad = jnp.dot(turned[...], att_ref[...], preferred_element_type=f32).astype(jnp.bfloat16)
-        out_away[...] = grad[: width // 2]
-        out_stay[...] = grad[width // 2 :]
-        for i in range(8):
+        _turn_blocks(turned_ref, low_ref[...], lax.rem(lax.axis_index("blk"), 2))
+        for i in range(3):
             small_ref[pl.ds(i, 1), :] = jnp.sum(sums[pl.ds(8 * i, 8), :], 0, keepdims=True)
 
 
-def ffn_both(me, tokens, cotangent, attended, out_weight, up_weight, down_weight, norm_gain, norm_bias, proj_bias, ffn_bias):
+def _once(*shape):
+    return pl.BlockSpec(shape, lambda s: (0,) * len(shape), pipeline_mode=pl.Buffered(1))
+
+
+def ffn_forward(tokens, cotangent, attended, out_weight, up_weight, down_weight, norm_gain, norm_bias, proj_bias, ffn_bias):
     rows, width = tokens.shape
     hidden = up_weight.shape[1]
     tiles = 8
     hid = hidden // tiles
+    bf16, f32 = jnp.bfloat16, jnp.float32
+    shape = jax.ShapeDtypeStruct
+    return pl.pallas_call(
+        functools.partial(ffn_kernel, tiles=tiles, strip=rows // 4),
+        grid=(tiles,),
+        in_specs=[
+            _once(rows, width), _once(rows, width), _once(rows, width), _once(width, width),
+            pl.BlockSpec((width, hid), lambda s: (0, s)), pl.BlockSpec((hid, width), lambda s: (s, 0)),
+            _once(4, width), _once(4, width), _once(4, width), pl.BlockSpec((1, hid), lambda s: (0, s)),
+        ],
+        out_specs=[
+            _once(rows, width), _once(rows, width), _once(rows, width), _once(rows, 1), _once(rows, width),
+            _once(width, rows), _once(width, rows),
+            pl.BlockSpec((rows, hid), lambda s: (0, s)), pl.BlockSpec((rows, hid), lambda s: (0, s)), _once(8, width),
+        ],
+        out_shape=[
+            shape((rows, width), bf16), shape((rows, width), f32), shape((rows, width), bf16), shape((rows, 1), f32),
+            shape((rows, width), bf16), shape((width, rows), bf16), shape((width, rows), bf16),
+            shape((rows, hidden), bf16), shape((rows, hidden), bf16), shape((8, width), f32),
+        ],
+        scratch_shapes=[pltpu.VMEM((rows, width), bf16), pltpu.VMEM((rows, width), f32), pltpu.VMEM((rows, width), f32), pltpu.VMEM((24, width), f32)],
+        compiler_params=pltpu.CompilerParams(vmem_limit_bytes=52 * 2**20),
+        cost_estimate=pl.CostEstimate(flops=18 * rows * width * width, bytes_accessed=50 * 2**20, transcendentals=rows * hidden),
+        name="ffn_forward",
+    )(tokens, cotangent, attended, out_weight, up_weight, down_weight, norm_gain, norm_bias, proj_bias, ffn_bias.reshape(1, -1))
+
+
+def grads_kernel(
+    low_ref, turned_ref, second_t, act_ref, slope_ref, up_ref, down_ref, mid_hbm, n_hbm, r_ref, cot_ref, att_ref, wo_ref, gain_ref,
+    gmid_ref, small_ref, hid_ref, up_out, down_out, out_out, gown_out,
+    pre, gs, low, turned, gatt, sums, up_buf, up_in, up_y, down_send, down_keep, down_in, down_x,
+    up_core, up_core_in, up_far, up_far_in, down_core, down_core_in, down_far, down_far_in, up_done, down_done, own_sems, gatt_sends, gatt_recvs, *, tiles, strip, fold,
+):
+    s = pl.program_id(0)
+    rows, width = low_ref.shape
+    own = width // 4
+    f32, bf16 = jnp.float32, jnp.bfloat16
+    pair, side = s // 2, lax.rem(s, 2)
+    me, place = lax.axis_index("blk"), lax.axis_index("dp")
+    core, chip, near = lax.rem(me, 2), me // 2, lax.rem(place, 2)
+    twin, other, beside = {"blk": me + 1 - 2 * core}, {"blk": lax.rem(me + 2, 4)}, {"dp": place + 1 - 2 * near}
+    last = {"blk": 3 - me}
     half = tiles // 2
+    mesh_ids = pl.DeviceIdType.MESH
+
+    def remote(src, dst, sends, recvs, i, target):
+        return pltpu.make_async_remote_copy(
+            src_ref=src, dst_ref=dst, send_sem=sends.at[i], recv_sem=recvs.at[i], device_id=target, device_id_type=mesh_ids
+        )
+
+    def up_to_twin(p):
+        return remote(up_buf.at[0], up_in.at[p], up_core, up_core_in, p, twin)
+
+    def up_to_beside(p):
+        return remote(up_in.at[p, :, 1 - near], up_y.at[p], up_far, up_far_in, p, beside)
+
+    def down_to_twin(u, slot):
+        return remote(down_send.at[slot], down_in.at[lax.rem(u, 4)], down_core, down_core_in, u, twin)
+
+    def down_to_other(u):
+        return remote(down_keep.at[u, 1 - chip], down_x.at[u], down_far, down_far_in, u, other)
+
+    def up_result(p):
+        return pltpu.make_async_copy(up_y.at[p], up_out.at[:, p], up_done.at[p])
+
+    def down_result(u):
+        tile = 4 * (u // 4) + 2 * lax.rem(u, 2) + lax.rem(u // 2, 2)
+        return pltpu.make_async_copy(down_x.at[u], down_out.at[tile], down_done.at[u])
+
+    def saved(i):
+        return pltpu.make_async_copy((mid_hbm, n_hbm)[i], (gmid_ref, low)[i], own_sems.at[i])
+
+    def out_result(i):
+        return pltpu.make_async_copy(up_buf.at[i], out_out.at[i], own_sems.at[2 + i])
+
+    def columns_to(i):
+        target = (last, other, twin)[i]
+        block = target["blk"]
+        src = gatt.at[:, pl.ds(pl.multiple_of(block * own, own), own)]
+        dst = gown_out.at[pl.ds(pl.multiple_of(me * rows, rows), rows), :]
+        return remote(src, dst, gatt_sends, gatt_recvs, i, target)
+
+    def columns_here():
+        src = gatt.at[:, pl.ds(pl.multiple_of(me * own, own), own)]
+        return pltpu.make_async_copy(src, gown_out.at[pl.ds(pl.multiple_of(me * rows, rows), rows), :], own_sems.at[4])
+
+    def join_up(p):
+        up_to_twin(p).wait_recv()
+        up_in[p] = (up_in[p].astype(f32) + up_buf[1].astype(f32)).astype(bf16)
+        up_to_beside(p).start()
+
+    def join_far_up(p):
+        up_to_beside(p).wait_recv()
+        up_y[p] = (up_y[p].astype(f32) + up_in[p, :, near].astype(f32)).astype(bf16)
+        up_result(p).start()
+
+    def join_cores(p):
+        join_up(p)
+        for c in range(2):
+            u = 2 * p + c
+            down_to_twin(u, c).wait_recv()
+            down_keep[u] = (down_keep[u].astype(f32) + down_in[lax.rem(u, 4)].astype(f32)).astype(bf16)
+            down_to_other(u).start()
+
+    def join_far(p):
+        join_far_up(p)
+        for c in range(2):
+            u = 2 * p + c
+            down_to_other(u).wait_recv()
+            down_x[u] = (down_x[u].astype(f32) + down_keep[u, chip].astype(f32)).astype(bf16)
+            down_result(u).start()
+
+    @pl.when(s == 0)
+    def _():
+        barrier = pltpu.get_barrier_semaphore()
+        for target in (twin, other, beside, last):
+            pl.semaphore_signal(barrier, inc=1, device_id=target, device_id_type=mesh_ids)
+        sums[...] = jnp.zeros_like(sums)
+        saved(0).start()
+        saved(1).start()
+        pl.semaphore_wait(barrier, 4)
+
+    @pl.when((side == 0) & (s > 0))
+    def _():
+        join_cores(pair - 1)
+
+    @pl.when(s == 6)
+    def _():
+        join_far(0)
+
+    g = lax.dot_general(low_ref[...], down_ref[...], NT, preferred_element_type=f32) * slope_ref[...].astype(f32)
+    g = g.astype(bf16)
+    pre[...] = g
+    hid_ref[pl.ds(s, 1)] = jnp.sum(g.astype(f32), 0, keepdims=True)[None]
+    part = lax.dot_general(g, up_ref[...], NT, preferred_element_type=f32)
+
+    @pl.when(s == 0)
+    def _():
+        gs[...] = part
+
+    @pl.when(s > 0)
+    def _():
+        gs[...] += part
+
+    down_grad = jnp.dot(turned_ref[...], act_ref[...], preferred_element_type=f32).astype(bf16)
+
+    @pl.when(s >= 2)
+    def _():
+        down_to_twin(s - 2, side).wait_send()
+
+    down_send[side] = down_grad[: width // 2].reshape(2, own, -1)
+    down_to_twin(s, side).start()
+    down_keep[s] = down_grad[width // 2 :].reshape(2, own, -1)
+    up_grad = jnp.dot(second_t[...], pre[...], preferred_element_type=f32).astype(bf16).reshape(up_buf.shape[1:])
+
+    @pl.when(side == core)
+    def _():
+        up_buf[1] = up_grad
+
+    @pl.when(side != core)
+    def _():
+        @pl.when(pair > 0)
+        def _():
+            up_to_twin(pair - 1).wait_send()
+
+        up_buf[0] = up_grad
+        up_to_twin(pair).start()
+
+    @pl.when(s == tiles - 1)
+    def _():
+        def normed(at):
+            n, r = _stats(gmid_ref[at, :])
+            y = gs[at, :]
+            gm = cot_ref[at, :].astype(f32) + _pull(n, r, y * _row(gain_ref, 2))
+            gmid_ref[at, :] = gm
+            sums[pl.ds(8, 8), :] += _fold(y * n)
+            sums[pl.ds(24, 8), :] += _fold(y)
+            n, r = low[at, :].astype(f32), r_ref[at, :]
+            g = _pull(n, r, gm * _row(gain_ref, 1)).astype(bf16)
+            low[at, :] = g
+            sums[pl.ds(0, 8), :] += _fold(gm * n)
+            sums[pl.ds(16, 8), :] += _fold(gm)
+            sums[pl.ds(32, 8), :] += _fold(g.astype(f32))
+
+        join_cores(tiles // 2 - 1)
+        saved(0).wait()
+        saved(1).wait()
+        _each(rows, strip, normed)
+        gatt[...] = lax.dot_general(low[...], wo_ref[...], NT, preferred_element_type=f32).astype(bf16)
+        for i in range(3):
+            columns_to(i).start()
+        columns_here().start()
+        _turn_blocks(turned, low[...], core)
+        grad = jnp.dot(turned[...], att_ref[...], preferred_element_type=f32).astype(bf16)
+        up_to_twin(half - 1).wait_send()
+        if fold:
+            thin = width // 8
+            for d in range(8):
+                for b in range(8):
+                    piece = grad[b * thin : (b + 1) * thin, d * thin : (d + 1) * thin]
+                    up_buf[b // 4, d // 2, d % 2, :, pl.ds(b % 4 * thin, thin)] = piece
+            up_to_twin(half).start()
+        else:
+            for i in range(2):
+                up_buf[i] = grad[:, i * width // 2 : (i + 1) * width // 2].reshape(up_buf.shape[1:])
+                out_result(i).start()
+        for i in range(5):
+            small_ref[pl.ds(i, 1), :] = jnp.sum(sums[pl.ds(8 * i, 8), :], 0, keepdims=True)
+        if fold:
+            join_up(half)
+        for p in range(1, half):
+            join_far(p)
+        if fold:
+            join_far_up(half)
+        down_to_twin(tiles - 2, 0).wait_send()
+        down_to_twin(tiles - 1, 1).wait_send()
+        if fold:
+            up_to_twin(half).wait_send()
+        else:
+            out_result(0).wait()
+            out_result(1).wait()
+        for p in range(half + fold):
+            up_to_beside(p).wait_send()
+            up_result(p).wait()
+        for u in range(tiles):
+            down_to_other(u).wait_send()
+            down_result(u).wait()
+        for i in range(3):
+            columns_to(i).wait_send()
+            columns_to(i).wait_recv()
+        columns_here().wait()
+
+
+def ffn_backward(parts, low, turned, second_t, act, slope, up_weight, down_weight, mid, n_one, r_one, cotangent, attended, out_weight, norm_gain):
+    rows, width = low.shape
+    hidden = up_weight.shape[1]
+    tiles, own = 8, width // 4
+    hid = hidden // tiles
     bf16, f32 = jnp.bfloat16, jnp.float32
-    blocks = jnp.stack([me ^ 3, me ^ 1, me ^ 2, me])
-    order = (blocks[:, None] * 2 + jnp.arange(2)[None]).reshape(-1).astype(jnp.int32)
-    spot = jnp.arange(4) ^ me
-    places = jnp.where(spot == 3, 0, jnp.where(spot == 1, 1, jnp.where(spot == 2, 2, 3))).astype(jnp.int32)
-    tile_of = lambda s: lax.rem(s, tiles)
-    late = lambda s: jnp.maximum(s - tiles, 0)
-    whole = lambda *shape: pl.BlockSpec(shape, lambda s, o, p: (0,) * len(shape))
-    once = lambda *shape: pl.BlockSpec(shape, lambda s, o, p: (0,) * len(shape), pipeline_mode=pl.Buffered(1))
+    shape = jax.ShapeDtypeStruct
+    tile_of = lambda s: 4 * (s // 4) + 2 * lax.rem(s, 2) + lax.rem(s // 2, 2)
+    thin = (parts // 2, 2, width // parts, hid)
+    dma = pltpu.SemaphoreType.DMA
+    half = tiles // 2
+    fold = int(parts == 8)
     return pl.pallas_call(
-        functools.partial(ffn_kernel, tiles=tiles, cut=rows, strip=rows // 4),
-        grid_spec=pltpu.PrefetchScalarGridSpec(
-            num_scalar_prefetch=2,
-            grid=(2 * tiles,),
-            in_specs=[
-                once(rows, width), once(rows, width), once(rows, width), once(width, width),
-                pl.BlockSpec((width, hid), lambda s, o, p: (0, o[tile_of(s)])),
-                pl.BlockSpec((hid, width), lambda s, o, p: (o[tile_of(s)], 0)),
-                once(4, width), once(4, width), once(4, width),
-                pl.BlockSpec((1, hid), lambda s, o, p: (0, o[tile_of(s)])),
-            ],
-            out_specs=[
-                once(rows, width), once(rows, width), once(rows, width),
-                once(width // 2, width), once(width // 2, width),
-                pl.BlockSpec((8, 1, width // 8, hid), lambda s, o, p: (0, jnp.minimum(late(s), half - 1), 0, 0)),
-                pl.BlockSpec((8, 1, width // 8, hid), lambda s, o, p: (0, jnp.maximum(late(s) - half, 0), 0, 0)),
-                pl.BlockSpec((1, width // 2, hid), lambda s, o, p: (o[late(s)], 0, 0)),
-                pl.BlockSpec((1, width // 2, hid), lambda s, o, p: (o[late(s)], 0, 0)),
-                once(8, width),
-                pl.BlockSpec((1, 1, hid), lambda s, o, p: (o[late(s)], 0, 0)),
-            ],
-            scratch_shapes=[
-                pltpu.VMEM((rows, hidden), bf16), pltpu.VMEM((rows, hidden), bf16),
-                pltpu.VMEM((rows, width), bf16), pltpu.VMEM((width, rows), bf16), pltpu.VMEM((width, rows), bf16),
-                pltpu.VMEM((rows, width), f32), pltpu.VMEM((rows, width), f32),
-                pltpu.VMEM((64, width), f32),
-            ],
-        ),
+        functools.partial(grads_kernel, tiles=tiles, strip=rows // 4, fold=fold),
+        grid=(tiles,),
+        in_specs=[
+            _once(rows, width), _once(width, rows), _once(width, rows),
+            pl.BlockSpec((rows, hid), lambda s: (0, tile_of(s))), pl.BlockSpec((rows, hid), lambda s: (0, tile_of(s))),
+            pl.BlockSpec((width, hid), lambda s: (0, tile_of(s))), pl.BlockSpec((hid, width), lambda s: (tile_of(s), 0)),
+            pl.BlockSpec(memory_space=pl.ANY), pl.BlockSpec(memory_space=pl.ANY), _once(rows, 1), _once(rows, width), _once(rows, width), _once(width, width), _once(4, width),
+        ],
+        out_specs=[
+            _once(rows, width), _once(8, width), _once(tiles, 1, hid),
+            pl.BlockSpec(memory_space=pl.ANY), pl.BlockSpec(memory_space=pl.ANY), pl.BlockSpec(memory_space=pl.ANY), pl.BlockSpec(memory_space=pl.ANY),
+        ],
         out_shape=[
-            jax.ShapeDtypeStruct((rows, width), bf16), jax.ShapeDtypeStruct((rows, width), f32), jax.ShapeDtypeStruct((rows, width), bf16),
-            jax.ShapeDtypeStruct((width // 2, width), bf16), jax.ShapeDtypeStruct((width // 2, width), bf16),
-            jax.ShapeDtypeStruct((8, half, width // 8, hid), bf16), jax.ShapeDtypeStruct((8, half, width // 8, hid), bf16),
-            jax.ShapeDtypeStruct((tiles, width // 2, hid), bf16), jax.ShapeDtypeStruct((tiles, width // 2, hid), bf16),
-            jax.ShapeDtypeStruct((8, width), f32), jax.ShapeDtypeStruct((tiles, 1, hid), f32),
+            shape((rows, width), f32),
+            shape((8, width), f32), shape((tiles, 1, hid), f32),
+            shape((parts // 2, half + fold, width // parts, hid), bf16), shape((tiles, own, hid), bf16), shape((2,) + thin, bf16),
+            shape((4 * rows, own), bf16),
         ],
-        compiler_params=pltpu.CompilerParams(vmem_limit_bytes=60 * 2**20),
-        cost_estimate=pl.CostEstimate(flops=50 * rows * width * width, bytes_accessed=80 * 2**20, transcendentals=rows * hidden),
-        name="ffn_both",
-    )(order, places, tokens, cotangent, attended, out_weight, up_weight, down_weight, norm_gain, norm_bias, proj_bias, ffn_bias.reshape(1, -1))
+        scratch_shapes=[
+            pltpu.VMEM((rows, hid), bf16), pltpu.VMEM((rows, width), f32), pltpu.VMEM((rows, width), bf16), pltpu.VMEM((width, rows), bf16), pltpu.VMEM((rows, width), bf16),
+            pltpu.VMEM((40, width), f32),
+            pltpu.VMEM((2,) + thin, bf16), pltpu.VMEM((half + fold,) + thin, bf16), pltpu.VMEM((half + fold, parts // 2, width // parts, hid), bf16),
+            pltpu.VMEM((2, 2, own, hid), bf16), pltpu.VMEM((tiles, 2, own, hid), bf16), pltpu.VMEM((4, 2, own, hid), bf16),
+            pltpu.VMEM((tiles, own, hid), bf16),
+            *[dma((half + fold,))] * 4, *[dma((tiles,))] * 4, dma((half + fold,)), dma((tiles,)), dma((5,)), dma((3,)), dma((3,)),
+        ],
+        compiler_params=pltpu.CompilerParams(collective_id=1, has_side_effects=True, vmem_limit_bytes=60 * 2**20),
+        name="ffn_backward",
+    )(low, turned, second_t, act, slope, up_weight, down_weight, mid, n_one, r_one, cotangent, attended, out_weight, norm_gain)
 
 
 def project_kernel(x_ref, w_hbm, gain_ref, shift_ref, bias_ref, all_ref, qkv_ref, w_ref, w_sems, chip_send, chip_recv, core_send, core_recv, pass_send, pass_recv, *, pieces):
@@ -557,32 +715,26 @@
     return pick(half, line, 0).astype(jnp.float32) + sum(piece.astype(jnp.float32) for piece in got)
 
 
-def weight_sums(up, down, out):
+def weight_sums(up, down, out, own):
     parts = lax.axis_size("dp")
-    width, hidden = out.shape[1], down.shape[0] * down.shape[2]
-    own = width // 4
+    chip = lax.axis_index("blk") // 2
+    width = 4 * own
+    groups = [[d for d in range(parts) if d % 2 == b] for b in range(2)]
+    up = lax.psum_scatter(up, "dp", scatter_dimension=0, axis_index_groups=groups, tiled=False)
+    halves = up[:4].reshape((2, 2) + up.shape[1:]).transpose(0, 2, 1, 3).reshape(2, up.shape[1], -1)
     if parts == 8:
-        thin = own // 4
-        pieces = [
-            up.reshape(8, 2, -1, hidden // 8),
-            down.reshape(8, 2, -1, hidden // 8),
-            out.reshape(2, 4, thin, 8, width // 8).transpose(3, 0, 2, 1, 4).reshape(8, 2, thin, width // 2),
-        ]
-        got = lax.psum_scatter(jnp.concatenate(pieces, 2), "dp", scatter_dimension=0, tiled=False)
-        total = got[1].astype(jnp.float32) + exchange(got[0], "blk", 2).astype(jnp.float32)
-        up_grad = total[:own].reshape(2, width // 8, -1).transpose(1, 0, 2).reshape(width // 8, -1)
-        out_grad = total[2 * own :].reshape(thin, 4, -1).transpose(1, 0, 2).reshape(own, -1)
-        return up_grad, total[own : 2 * own].T, out_grad.T
-    pieces = [
-        up.reshape(8, 2, 2, width // 8, -1).transpose(1, 0, 3, 2, 4).reshape(2, parts, -1),
-        down.reshape(8, 2, own, -1).transpose(1, 2, 0, 3).reshape(2, own, parts, -1).transpose(0, 2, 1, 3).reshape(2, parts, -1),
-        out.reshape(2, own, parts, -1).transpose(0, 2, 1, 3).reshape(2, parts, -1),
-    ]
-    ends = [pieces[0].shape[2], pieces[0].shape[2] + pieces[1].shape[2]]
-    got = lax.psum_scatter(jnp.concatenate(pieces, 2).transpose(1, 0, 2), "dp", scatter_dimension=0, tiled=False)
-    total = got[1].astype(jnp.float32) + exchange(got[0], "blk", 2).astype(jnp.float32)
-    up_grad, down_grad, out_grad = total[: ends[0]], total[ends[0] : ends[1]], total[ends[1] :]
-    return up_grad.reshape(width // parts, -1), down_grad.reshape(own, -1).T, out_grad.reshape(own, -1).T
+        thin = up.shape[1]
+        halves = jnp.concatenate([halves, up[4].reshape(thin, 2, -1).transpose(1, 0, 2)], 2)
+    total = pick(halves, chip, 0).astype(jnp.float32) + exchange(pick(halves, 1 - chip, 0), "blk", 2).astype(jnp.float32)
+    if parts == 8:
+        out_grad = total[:, width:].reshape(thin, 2, thin).transpose(1, 0, 2).reshape(own, thin).T
+        down_grad = lax.psum_scatter(down, "dp", scatter_dimension=0, tiled=False).astype(jnp.float32).T
+    else:
+        down = down.transpose(1, 0, 2).reshape(own, parts, -1).transpose(1, 0, 2)
+        out = out.reshape(own, parts, width // parts).transpose(1, 0, 2)
+        both = lax.psum_scatter(jnp.concatenate([down, out], 2), "dp", scatter_dimension=0, tiled=False).astype(jnp.float32)
+        down_grad, out_grad = both[:, : down.shape[2]].T, both[:, down.shape[2] :].T
+    return total[:, :width], down_grad, out_grad
 
 
 def local(tokens, cotangent, lengths, qkv_weight, out_weight, up_weight, down_weight, norm_gain, norm_bias, proj_bias, ffn_bias):
@@ -604,15 +756,19 @@
     attended_own, log_total = attn_fwd(lengths, qkv)
     attended = lax.all_to_all(attended_own, "blk", split_axis=0, concat_axis=1, tiled=True)
 
-    (mixed, grad_middle, grad_attended, out_away, out_stay, up_away, up_stay, down_away, down_stay, sums, hidden_bias) = ffn_both(
-        me, tokens, cotangent, attended, out_weight, up_weight, down_weight, norm_gain, norm_bias, proj_bias, ffn_bias
+    mixed, mid, n_one, r_one, low, turned, second_t, act, slope, sums_three = ffn_forward(
+        tokens, cotangent, attended, out_weight, up_weight, down_weight, norm_gain, norm_bias, proj_bias, ffn_bias
     )
-    grad_own = lax.all_to_all(grad_attended, "blk", split_axis=1, concat_axis=0, tiled=True)
-    up_half = plus(up_stay, exchange(up_away, "blk", 1))
-    down_half = plus(down_stay, exchange(down_away, "blk", 1))
-    out_half = plus(out_stay, exchange(out_away, "blk", 1))
-    grad_own, up_half, down_half, out_half = lax.optimization_barrier((grad_own, up_half, down_half, out_half))
-    up_grad, down_grad, out_grad = weight_sums(up_half, down_half, out_half)
+    grad_middle, sums, hidden_bias, up_sum, down_sum, out_term, grad_own = ffn_backward(
+        parts, low, turned, second_t, act, slope, up_weight, down_weight, mid, n_one, r_one, cotangent, attended, out_weight, norm_gain
+    )
+    hidden_bias = hidden_bias.reshape(2, 2, 2, -1).transpose(0, 2, 1, 3)
+    out_sum = None
+    if parts != 8:
+        out_term = out_term.reshape(2, 2, width // 2, width // 2).transpose(1, 2, 0, 3).reshape(2, 2, own, width)
+        out_half = plus(out_term[1], exchange(out_term[0], "blk", 1))
+        out_sum = plus(pick(out_half, chip, 0), exchange(pick(out_half, 1 - chip, 0), "blk", 2))
+    up_grad, down_grad, out_grad = weight_sums(up_sum, down_sum, out_sum, own)
     grads = attn_bwd(lengths, qkv, grad_own, attended_own, log_total)
 
     by_block = grads.reshape(2, 2, rows, 3 * own)
@@ -639,8 +795,8 @@
     token_grad = (grad_middle + _pull(n, r, y * norm_gain[0])).astype(jnp.bfloat16)
     small = jnp.stack(
         [
-            jnp.sum(y * n, 0), *sums[:3], jnp.sum(y, 0), *sums[3:6],
-            spread(column_sums(grads[:, :own])), spread(column_sums(grads[:, 2 * own :])), *sums[6:],
+            jnp.sum(y * n, 0), sums[0], sums[1], sums_three[0], jnp.sum(y, 0), sums[2], sums[3], sums_three[1],
+            spread(column_sums(grads[:, :own])), spread(column_sums(grads[:, 2 * own :])), sums[4], sums_three[2],
             *hidden_bias.reshape(-1, width),
         ]
     )

time: 511 us -> 475 us (0.930)
  Pallas kernels: 247 us -> 290 us
  waiting for transfers between devices: 89.1 us -> 60.4 us
  other arithmetic: 39 us -> 15.5 us
  starting transfers between devices: 41.5 us -> 25.8 us
  local copies, waits for them, and re-layouts: 43.4 us -> 31.4 us
    pallas_call x1 -> x2, Pallas kernels: 91.8 us -> 132 us  [the longest x1 90.2 us: ffn_backward(): pl.pallas_call(functools.partial(grads_kernel, tiles=tiles, strip=rows //...]
    ppermute x15 -> x12, waiting for transfers between devices: 65.9 us -> 41.8 us  [exchange(): lax.ppermute(values, axis, [(i, i ^ bit) for i in range(lax.axis_size(axi...]
    convert_element_type x4 -> x1, other arithmetic: 16.2 us -> 1.34 us  [plus(): (left.astype(jnp.float32) + right.astype(jnp.float32)).astype(jnp.bfloat16)]
    ppermute x15 -> x12, starting transfers between devices: 34.3 us -> 22 us  [exchange(): lax.ppermute(values, axis, [(i, i ^ bit) for i in range(lax.axis_size(axi...]
    concatenate x1 -> x0, other arithmetic: 7.46 us -> none  [weight_sums(): jnp.concatenate(pieces, 2)]
  transfers between devices with their start and end apart: 18 -> 15, of which waited for: 12 -> 9; matrix products, arithmetic and copies ran while one was open for 15% -> 11% of each run, Pallas kernels for 11% -> 13%
where the time goes in v3:
time: 475 us; the launch traced here: 467 us
  Pallas kernels  290 us (61%)
  waiting for transfers between devices  60.4 us (13%)
  local copies, waits for them, and re-layouts  31.4 us (7%)
  starting transfers between devices  25.8 us (5%)
  matrix products  20.2 us (4%)
  other arithmetic  15.5 us (3%)
  between operations  14.8 us (3%)
  blocking collectives  8.59 us (2%)
    pallas_call x1, Pallas kernels, ffn_backward(): pl.pallas_call(functools.partial(grads_kernel, tiles=tiles, strip=rows //...  90.2 us
    pallas_call x1, Pallas kernels, attn_bwd(): pl.pallas_call(functools.partial(bwd_kernel, heads=heads, wide=wide), gri...  59 us
    pallas_call x1, Pallas kernels, attn_fwd(): pl.pallas_call(functools.partial(fwd_kernel, heads=heads, wide=wide), gri...  51.7 us
    pallas_call x1, Pallas kernels, gather_project(): pl.pallas_call(functools.partial(project_kernel, pieces=pieces), in_specs...  47.4 us
    ppermute x12, waiting for transfers between devices, exchange(): lax.ppermute(values, axis, [(i, i ^ bit) for i in range(lax.axis_size(axi...  41.8 us
    pallas_call x1, Pallas kernels, ffn_forward(): pl.pallas_call(functools.partial(ffn_kernel, tiles=tiles, strip=rows // 4...  41.4 us
    ppermute x12, starting transfers between devices, exchange(): lax.ppermute(values, axis, [(i, i ^ bit) for i in range(lax.axis_size(axi...  22 us
    all_to_all x1, waiting for transfers between devices, local(): lax.all_to_all(attended_own, 'blk', split_axis=0, concat_axis=1, tiled=True)  18.6 us
  transfers between devices with their start and end apart: 15, of which 9 were waited for; matrix products, arithmetic and copies ran while one was open for 11% of the time, Pallas kernels for 13%

profile of v3, /device:TPU:0, one launch (start us, length us, event | category | flops | bytes accessed | tf_op | source)
XLA Modules:
  0.0 466.5 jit_solution(11170371761021872704)
XLA Ops:
  10.9 47.4 %gather_project.1 = (bf16[3328,1024]{1,0:T(8,128)(2,1)}, bf16[3328,768]{1,0:T(8,128)(2,1)}) custom-call(bf16[832,1024]{1,0:T(8,128)(2,1)S(1)} %copy-done, bf16[1024,3072]{1,0:T(8,128)(2,1)} %w_hbm.1, f32[4,1024]{1,0:T(4,128)S(1)} %copy-done.4, f32[4,1024]{1,0:T(4,128)S(1)} %copy-done.6, f32[1,768]{1,0:T(1,128)S(1)} %reshape.113.bias_ref), custom_call_target="tpu_custom_call" | custom-call | tf_op jit(solution)/shard_map/gather_project/pallas_call | solution.py:664
  60.9 51.7 %attn_fwd.1 = (bf16[3328,256]{1,0:T(8,128)(2,1)}, f32[4,3328]{1,0:T(4,128)S(1)}) custom-call(s32[1,3]{1,0:T(1,128)S(1)} %copy-done.13, bf16[3328,768]{1,0:T(8,128)(2,1)S(1)} %copy-done.9, bf16[3328,768]{1,0:T(8,128)(2,1)S(1)} %copy-done.9, bf16[3328,768]{1,0:T(8,128)(2,1)S(1)} %copy-done.9), custom_call_target="tpu_custom_call" | custom-call | flops 25518145536 | bytes 8519680 | tf_op jit(solution)/shard_map/attn_fwd/pallas_call | solution.py:110
  112.6 3.6 all-to-all-start
  119.1 18.6 %all-to-all-done = bf16[4,832,256]{2,1,0:T(8,128)(2,1)S(1)} async-done(((bf16[4,832,256]{2,1,0:T(8,128)(2,1)}), bf16[4,832,256]{2,1,0:T(8,128)(2,1)S(1)}, u32[]{:S(2)}, u32[]{:S(2)}) %all-to-all-start) | async-done | bytes 1703968 | tf_op jit(solution)/shard_map/all_to_all | solution.py:757
  139.1 41.4 %ffn_forward.1 = (bf16[832,1024]{1,0:T(8,128)(2,1)}, f32[832,1024]{1,0:T(8,128)}, bf16[832,1024]{1,0:T(8,128)(2,1)}, f32[832,1]{1,0:T(8,128)S(1)}, bf16[832,1024...) custom-call(bf16[832,1024]{1,0:T(8,128)(2,1)} %x_ref.3, ...), custom_call_target="tpu_custom_call" | custom-call | flops 15703474176 | bytes 52428800 | tf_op jit(solution)/shard_map/ffn_forward/pallas_call | solution.py:319
  181.2 90.2 %ffn_backward.1 = (f32[832,1024]{1,0:T(8,128)}, f32[8,1024]{1,0:T(8,128)}, f32[8,1,512]{2,1,0:T(1,128)}, bf16[4,5,128,512]{3,2,1,0:T(8,128)(2,1)}, bf16[8,256,51...) custom-call(bf16[832,1024]{1,0:T(8,128)(2,1)} %get-tuple-element.35.low_ref, ...), custom_call_target="tpu_custom_call" | custom-call | tf_op jit(solution)/shard_map/ffn_backward/pallas_call | solution.py:562
  275.4 59.0 %attn_bwd.1 = bf16[3328,768]{1,0:T(8,128)(2,1)S(1)} custom-call(s32[1,3]{1,0:T(1,128)S(1)} %copy-done.13, bf16[3328,768]{1,0:T(8,128)(2,1)S(1)} %copy-done.10, bf16[3328,256]{1,0:T(8,128)(2,1)S(1)} %copy-done.11, bf16[3328,256]{1,0:T(8,128)(2,1)} %get-tuple-element.33.o_ref, f32[4,3328]{1,0:T(4,128)S(1)} %get-tuple-element.45.lse_ref, ...), custom_call_target="tpu_custom_call" | custom-call | flops 31188844544 | bytes 17039360 | tf_op jit(solution)/shard_map/attn_bwd/pallas_call | solution.py:184
  337.5 4.4 convolution_convert_fusion
  345.1 4.3 collective-permute-done
  349.4 7.8 %add_convert_fusion = bf16[1664,1024]{1,0:T(8,128)(2,1)} fusion(bf16[1664,1024]{1,0:T(8,128)(2,1)} %collective-permute-done, bf16[1664,768]{1,0:T(8,128)(2,1)} %bitcast.102, bf16[1024,256]{1,0:T(8,128)(2,1)} %get-tuple-element.101, bf16[1024,256]{1,0:T(8,128)(2,1)} %get-tuple-element.102, bf16[1024,256]{1,0:T(8,128)(2,1)S(1)} %copy-done.14), kind=kOutput, calls=%fused_computation | convolution fusion | flops 2627076096 | bytes 10944512 | tf_op jit(solution)/shard_map/dot_general | solution.py:680
  357.2 7.9 %convolution_convert_fusion.1 = bf16[1024,768]{1,0:T(8,128)(2,1)S(1)} fusion(bf16[3328,1024]{1,0:T(8,128)(2,1)} %get-tuple-element.47, bf16[3328,768]{1,0:T(8,128)(2,1)S(1)} %bitcast.91), kind=kOutput, calls=%fused_computation.23 | convolution fusion | flops 5235277824 | bytes 13500416 | tf_op jit(solution)/shard_map/dot_general | solution.py:676
  366.5 7.7 %collective-permute-start.2 = (bf16[4,128,768]{1,2,0:T(8,128)(2,1)}, bf16[4,128,768]{1,2,0:T(8,128)(2,1)}, u32[]{:S(2)}, u32[]{:S(2)}) collective-permute-start(bf16[4,128,768]{1,2,0:T(8,128)(2,1)} %bitcast.109), channel_id=1, source_target_pairs={{0,4},{4,0},{8,12},{12,8},{16,20},{20,16},{24,28},{28,24},{1,5},{5... | collective-permute-start | bytes 2359304 | tf_op jit(solution)/shard_map/ppermute | solution.py:688
  374.2 2.8 dynamic-slice_bitcast_fusion
  380.5 12.1 %collective-permute-done.2 = bf16[4,128,768]{1,2,0:T(8,128)(2,1)} collective-permute-done((bf16[4,128,768]{1,2,0:T(8,128)(2,1)}, bf16[4,128,768]{1,2,0:T(8,128)(2,1)}, u32[]{:S(2)}, u32[]{:S(2)}) %collective-permute-start.2) | collective-permute-done | bytes 786464 | tf_op jit(solution)/shard_map/ppermute | solution.py:688
  394.7 4.4 collective-permute-start.4
  401.1 7.7 %collective-permute-done.3 = bf16[128,768]{0,1:T(8,128)(2,1)S(1)} collective-permute-done((bf16[128,768]{0,1:T(8,128)(2,1)}, bf16[128,768]{0,1:T(8,128)(2,1)S(1)}, u32[]{:S(2)}, u32[]{:S(2)}) %collective-permute-start.3) | collective-permute-done | bytes 196640 | tf_op jit(solution)/shard_map/ppermute | solution.py:688
  408.9 6.7 %collective-permute-done.5 = bf16[128,768]{0,1:T(8,128)(2,1)} collective-permute-done((bf16[128,768]{0,1:T(8,128)(2,1)S(1)}, bf16[128,768]{0,1:T(8,128)(2,1)}, u32[]{:S(2)}, u32[]{:S(2)}) %collective-permute-start.5) | collective-permute-done | bytes 196640 | tf_op jit(solution)/shard_map/ppermute | solution.py:688
  416.7 8.6 %all-gather = bf16[512,768]{0,1:T(8,128)(2,1)S(1)} all-gather(bf16[128,768]{0,1:T(8,128)(2,1)S(1)} %fusion.17), channel_id=2, replica_groups=mesh['dp'=8,'blk'=4] {'blk'}, dimensions={0}, use_global_device_ids=true | all-gather | bytes 983040 | tf_op jit(solution)/shard_map/all_gather | solution.py:786
  425.7 3.7 fusion.10
  432.0 3.3 collective-permute-done.8
  436.8 2.8 collective-permute-done.9
  439.6 3.3 collective-permute-start.10
  442.9 4.7 fusion.9
  451.4 3.7 collective-permute-done.11
  (124 shorter events, 43.7 us)
Async XLA Ops:
  10.9 47.5 %copy-start.13 = (s32[1,3]{1,0:T(1,128)S(1)}, s32[1,3]{1,0:T(1,128)}, u32[]{:S(2)}) copy-start(s32[1,3]{1,0:T(1,128)} %len_ref.3) | copy-start | bytes 40
  112.6 25.0 %all-to-all-start = ((bf16[4,832,256]{2,1,0:T(8,128)(2,1)}), bf16[4,832,256]{2,1,0:T(8,128)(2,1)S(1)}, u32[]{:S(2)}, u32[]{:S(2)}) async-start(bf16[4,832,256]{2,1,0:T(8,128)(2,1)} %bitcast.2), calls=%async_computation | async-start | bytes 3407872 | tf_op jit(solution)/shard_map/all_to_all | solution.py:757
  116.2 22.9 %copy-start.5 = (f32[4,1024]{1,0:T(4,128)S(1)}, f32[4,1024]{1,0:T(4,128)}, u32[]{:S(2)}) copy-start(f32[4,1024]{1,0:T(4,128)} %gain_ref.5) | copy-start | bytes 49156
  116.2 22.9 %copy-start.7 = (f32[4,1024]{1,0:T(4,128)S(1)}, f32[4,1024]{1,0:T(4,128)}, u32[]{:S(2)}) copy-start(f32[4,1024]{1,0:T(4,128)} %shift_ref.3) | copy-start | bytes 49156
  116.2 22.9 %copy-start.8 = (f32[4,1024]{1,0:T(4,128)S(1)}, f32[4,1024]{1,0:T(4,128)}, u32[]{:S(2)}) copy-start(f32[4,1024]{1,0:T(4,128)} %bias_ref.1) | copy-start | bytes 49156
  116.2 22.9 %copy-start.12 = (f32[4096]{0:T(1024)S(1)}, f32[4096]{0:T(1024)}, u32[]{:S(2)}) copy-start(f32[4096]{0:T(1024)} %param.21) | copy-start | bytes 49156
  116.2 282.9 %reduce-scatter.5.cloned.1.call-start = ((), (), s32[]{:S(2)}) async-start(), calls=%async_computation.4 | async-start | bytes 2359296 | tf_op jit(solution)/shard_map/reduce_scatter | solution.py:731
  271.4 176.2 %reduce-scatter.3.cloned.1.call-start = ((), (), s32[]{:S(2)}) async-start(), calls=%async_computation.3 | async-start | bytes 3276800 | tf_op jit(solution)/shard_map/reduce_scatter | solution.py:723
  337.5 6.6 %copy-start.1 = (bf16[832,1024]{1,0:T(8,128)(2,1)S(1)}, bf16[832,1024]{1,0:T(8,128)(2,1)}, u32[]{:S(2)}) copy-start(bf16[832,1024]{1,0:T(8,128)(2,1)} %x_ref.3) | copy-start | bytes 5111812
  342.0 7.5 %collective-permute-start = (bf16[1664,1024]{1,0:T(8,128)(2,1)}, bf16[1664,1024]{1,0:T(8,128)(2,1)}, u32[]{:S(2)}, u32[]{:S(2)}) collective-permute-start(bf16[1664,1024]{1,0:T(8,128)(2,1)} %convolution_convert_fusion), channel_id=1, source_target_pairs={{0,1},{1,0},{2,3},{3,2},{4,5},{5,4},{6,7},{7,6},{8,9},{9,8},{10,11... | collective-permute-start | bytes 10223624 | tf_op jit(solution)/shard_map/ppermute | solution.py:688
  345.1 12.2 %slice-start = ((s8[5111808]{0:T(1024)(128)(4,1)}), s8[917504]{0:T(1024)(128)(4,1)S(1)}, s32[]{:S(2)}) async-start(s8[5111808]{0:T(1024)(128)(4,1)} %bitcast.90), calls=%async_computation.5 | async-start | bytes 1835008
  349.4 7.8 %slice-start.1 = ((s8[5111808]{0:T(1024)(128)(4,1)}), s8[4194304]{0:T(1024)(128)(4,1)S(1)}, s32[]{:S(2)}) async-start(s8[5111808]{0:T(1024)(128)(4,1)} %bitcast.90), calls=%async_computation.6 | async-start | bytes 8388608
  365.2 12.2 %copy-start.17 = (f32[8,1,512]{2,1,0:T(1,128)S(1)}, f32[8,1,512]{2,1,0:T(1,128)}, u32[]{:S(2)}) copy-start(f32[8,1,512]{2,1,0:T(1,128)} %get-tuple-element.53) | copy-start | bytes 49156
  366.5 26.1 %collective-permute-start.2 = (bf16[4,128,768]{1,2,0:T(8,128)(2,1)}, bf16[4,128,768]{1,2,0:T(8,128)(2,1)}, u32[]{:S(2)}, u32[]{:S(2)}) collective-permute-start(bf16[4,128,768]{1,2,0:T(8,128)(2,1)} %bitcast.109), channel_id=1, source_target_pairs={{0,4},{4,0},{8,12},{12,8},{16,20},{20,16},{24,28},{28,24},{1,5},{5... | collective-permute-start | bytes 2359304 | tf_op jit(solution)/shard_map/ppermute | solution.py:688
  377.0 48.6 %collective-permute-start.1 = (bf16[832,1024]{1,0:T(8,128)(2,1)}, bf16[832,1024]{1,0:T(8,128)(2,1)}, u32[]{:S(2)}, u32[]{:S(2)}) collective-permute-start(bf16[832,1024]{1,0:T(8,128)(2,1)} %dynamic-slice_bitcast_fusion), channel_id=1, source_target_pairs={{0,2},{1,3},{2,0},{3,1},{4,6},{5,7},{6,4},{7,5},{8,10},{9,11},{10,... | collective-permute-start | bytes 5111816 | tf_op jit(solution)/shard_map/ppermute | solution.py:688
  394.7 14.1 %collective-permute-start.3 = (bf16[128,768]{0,1:T(8,128)(2,1)}, bf16[128,768]{0,1:T(8,128)(2,1)S(1)}, u32[]{:S(2)}, u32[]{:S(2)}) collective-permute-start(bf16[128,768]{0,1:T(8,128)(2,1)} %get-tuple-element.107), channel_id=1, source_target_pairs={{0,8},{4,12},{8,0},{12,4},{16,24},{20,28},{24,16},{28,20},{1,9},{5... | collective-permute-start | bytes 589832 | tf_op jit(solution)/shard_map/ppermute | solution.py:688
  394.7 14.1 %collective-permute-start.4 = (bf16[128,768]{0,1:T(8,128)(2,1)}, bf16[128,768]{0,1:T(8,128)(2,1)}, u32[]{:S(2)}, u32[]{:S(2)}) collective-permute-start(bf16[128,768]{0,1:T(8,128)(2,1)} %get-tuple-element.109), channel_id=1, source_target_pairs={{0,16},{4,20},{8,24},{12,28},{16,0},{20,4},{24,8},{28,12},{1,17},{... | collective-permute-start | bytes 589832 | tf_op jit(solution)/shard_map/ppermute | solution.py:688
  399.1 16.5 %collective-permute-start.5 = (bf16[128,768]{0,1:T(8,128)(2,1)S(1)}, bf16[128,768]{0,1:T(8,128)(2,1)}, u32[]{:S(2)}, u32[]{:S(2)}) collective-permute-start(bf16[128,768]{0,1:T(8,128)(2,1)S(1)} %get-tuple-element.108), channel_id=1, source_target_pairs={{0,24},{4,28},{8,16},{12,20},{16,8},{20,12},{24,0},{28,4},{1,25},{... | collective-permute-start | bytes 589832 | tf_op jit(solution)/shard_map/ppermute | solution.py:688
  429.5 1.4 collective-permute-start.7
  430.9 4.4 collective-permute-start.8
  435.3 4.3 collective-permute-start.9
  439.6 10.1 %collective-permute-start.10 = (f32[16,1024]{1,0:T(8,128)S(1)}, f32[16,1024]{1,0:T(8,128)S(1)}, u32[]{:S(2)}, u32[]{:S(2)}) collective-permute-start(f32[16,1024]{1,0:T(8,128)S(1)} %add.157), channel_id=1, source_target_pairs={{0,8},{4,12},{8,0},{12,4},{16,24},{20,28},{24,16},{28,20},{1,9},{5... | collective-permute-start | bytes 196616 | tf_op jit(solution)/shard_map/ppermute | solution.py:688
  449.8 5.4 %collective-permute-start.11 = (f32[16,1024]{1,0:T(8,128)S(1)}, f32[16,1024]{1,0:T(8,128)S(1)}, u32[]{:S(2)}, u32[]{:S(2)}) collective-permute-start(f32[16,1024]{1,0:T(8,128)S(1)} %add.158), channel_id=1, source_target_pairs={{0,16},{4,20},{8,24},{12,28},{16,0},{20,4},{24,8},{28,12},{1,17},{... | collective-permute-start | bytes 196616 | tf_op jit(solution)/shard_map/ppermute | solution.py:688
  449.9 7.7 %collective-permute-start.6 = (bf16[128,1280]{1,0:T(8,128)(2,1)S(1)}, bf16[128,1280]{1,0:T(8,128)(2,1)S(1)}, u32[]{:S(2)}, u32[]{:S(2)}) collective-permute-start(bf16[128,1280]{1,0:T(8,128)(2,1)S(1)} %fusion.19), channel_id=1, source_target_pairs={{0,2},{1,3},{2,0},{3,1},{4,6},{5,7},{6,4},{7,5},{8,10},{9,11},{10,... | collective-permute-start | bytes 983048 | tf_op jit(solution)/shard_map/ppermute | solution.py:688
  (12 other events, 25.5 us)
Sparse Core Ops, SparseCore 0:
  271.5 69.1 reduce-scatter.4
  345.2 58.5 reduce-scatter.2

commit v4 on v3

--- a/solution.py
+++ b/solution.py
@@ -59,7 +59,58 @@
         dst[pl.ds(h * TILE, TILE), :] = jnp.where(lane == h, value, jnp.zeros_like(value))
 
 
-def fwd_kernel(len_ref, q_ref, k_ref, v_ref, o_ref, lse_ref, qm, acc, ps, vt, *, heads, wide):
+def _span(len_ref, qb):
+    l0 = len_ref[0, 0]
+    e1 = l0 + len_ref[0, 1]
+
+    def start_of(r):
+        return jnp.where(r >= e1, e1, jnp.where(r >= l0, l0, 0))
+
+    rows = qb * TILE + lax.broadcasted_iota(jnp.int32, (1, TILE), 1)
+    kmin = start_of(qb * TILE) // TILE
+    return kmin, qb + 1 - kmin, rows, start_of(rows)
+
+
+def _at(kb):
+    return pl.ds(pl.multiple_of(kb * TILE, TILE), TILE)
+
+
+def _mask(kb, rows, starts):
+    kpos = kb * TILE + lax.broadcasted_iota(jnp.int32, (TILE, TILE), 0)
+    return (kpos >= starts) & (kpos <= rows)
+
+
+def _pipeline(kmin, count, load, work, use):
+    odd = lax.rem(count, 2)
+    end = kmin + count - 1
+
+    @pl.when(odd == 1)
+    def _():
+        load(kmin, 0)
+        load(jnp.minimum(kmin + 1, end), 1)
+        work(kmin, 0)
+
+    @pl.when(odd == 0)
+    def _():
+        load(kmin, 1)
+
+    first = kmin + odd
+
+    def two(i, carry):
+        kb = first + 2 * i
+        load(jnp.minimum(kb + 1, end), 0)
+        work(kb, 1)
+        use(jnp.maximum(kb - 1, kmin), 0)
+        load(jnp.minimum(kb + 2, end), 1)
+        work(kb + 1, 0)
+        use(kb, 1)
+        return carry
+
+    lax.fori_loop(0, count // 2, two, 0)
+    use(end, 0)
+
+
+def fwd_kernel(len_ref, q_ref, k_ref, v_ref, o_ref, lse_ref, qm, acc, s_one, s_two, p_one, p_two, fade_one, fade_two, top, norm, vt, *, heads):
     qb = pl.program_id(0)
 
     @pl.when(qb == 0)
@@ -68,65 +119,71 @@
 
     _fill_masked(qm, q_ref[...] * jnp.bfloat16(0.125), heads)
     acc[...] = jnp.zeros_like(acc)
-
-    def step(at, size, mask, carry):
-        keys = pl.ds(at, size)
-        scores = [
-            lax.dot_general(k_ref[keys, :], qm[pl.ds(h * TILE, TILE), :], NT, preferred_element_type=jnp.float32)
-            for h in range(heads)
-        ]
-        out, fades = [], []
+    p_one[...] = jnp.zeros_like(p_one)
+    fade_one[...] = jnp.zeros_like(fade_one)
+    top[...] = jnp.full(top.shape, 0.1 * NEG, jnp.float32)
+    norm[...] = jnp.zeros_like(norm)
+    kmin, count, rows, starts = _span(len_ref, qb)
+    scores, probs, fades = (s_one, s_two), (p_one, p_two), (fade_one, fade_two)
+
+    def load(kb, slot):
         for h in range(heads):
-            m, l = carry[h]
-            s = scores[h]
-            if mask is not None:
-                s = jnp.where(mask, s, NEG)
-            top = jnp.maximum(m, jnp.max(s, 0, keepdims=True))
-            p = jnp.exp(s - top)
-            if mask is not None:
-                p = jnp.where(mask, p, 0.0)
-            fade = jnp.exp(m - top)
-            ps[pl.ds(0, size), pl.ds(h * TILE, TILE)] = p.astype(jnp.bfloat16)
-            out.append((top, l * fade + jnp.sum(p, 0, keepdims=True)))
-            fades.append(fade)
+            mine = pl.ds(h * TILE, TILE)
+            scores[slot][:, mine] = lax.dot_general(k_ref[_at(kb), :], qm[mine, :], NT, preferred_element_type=jnp.float32)
+
+    def work(kb, slot):
+        mask = _mask(kb, rows, starts)
+        for h in range(heads):
+            mine, row = pl.ds(h * TILE, TILE), pl.ds(h, 1)
+            s = jnp.where(mask, scores[slot][:, mine], NEG)
+            m = top[row, :]
+            new = jnp.maximum(m, jnp.max(s, 0, keepdims=True))
+            p = jnp.exp(s - new)
+            fade = jnp.exp(m - new)
+            top[row, :] = new
+            norm[row, :] = norm[row, :] * fade + jnp.sum(p, 0, keepdims=True)
+            fades[slot][row, :] = fade
+            probs[slot][:, mine] = p.astype(jnp.bfloat16)
+
+    def use(kb, slot):
         for h in range(heads):
             lanes = pl.ds(h * HD, HD)
-            part = jnp.dot(vt[lanes, keys], ps[pl.ds(0, size), pl.ds(h * TILE, TILE)], preferred_element_type=jnp.float32)
-            acc[lanes, :] = acc[lanes, :] * fades[h] + part
-        return tuple(out)
-
-    carry = tuple((jnp.full((1, TILE), NEG, jnp.float32), jnp.zeros((1, TILE), jnp.float32)) for _ in range(heads))
-    carry = _walk(len_ref, qb, step, carry, wide)
+            part = jnp.dot(vt[lanes, _at(kb)], probs[slot][:, pl.ds(h * TILE, TILE)], preferred_element_type=jnp.float32)
+            acc[lanes, :] = acc[lanes, :] * fades[slot][pl.ds(h, 1), :] + part
+
+    _pipeline(kmin, count, load, work, use)
     for h in range(heads):
-        m, l = carry[h]
-        lse_ref[pl.ds(h, 1), :] = m + jnp.log(l)
-        acc[pl.ds(h * HD, HD), :] = acc[pl.ds(h * HD, HD), :] / l
+        row, lanes = pl.ds(h, 1), pl.ds(h * HD, HD)
+        lse_ref[row, :] = top[row, :] + jnp.log(norm[row, :])
+        acc[lanes, :] = acc[lanes, :] / norm[row, :]
     o_ref[...] = acc[...].T.astype(jnp.bfloat16)
 
 
-def attn_fwd(lengths, qkv, pair=0, lane=256, wide=(1,)):
-    n = qkv.shape[0]
+def attn_fwd(lengths, qkv):
+    n, lane = qkv.shape[0], qkv.shape[1] // 3
     heads = lane // HD
+    wide = heads * TILE
+    f32, bf16 = jnp.float32, jnp.bfloat16
     return pl.pallas_call(
-        functools.partial(fwd_kernel, heads=heads, wide=wide),
+        functools.partial(fwd_kernel, heads=heads),
         grid_spec=pltpu.PrefetchScalarGridSpec(
             num_scalar_prefetch=1,
             grid=(n // TILE,),
             in_specs=[
-                pl.BlockSpec((TILE, lane), lambda i, L: (i, 3 * pair)),
-                pl.BlockSpec((n, lane), lambda i, L: (0, 3 * pair + 1)),
-                pl.BlockSpec((n, lane), lambda i, L: (0, 3 * pair + 2)),
+                pl.BlockSpec((TILE, lane), lambda i, L: (i, 0)),
+                pl.BlockSpec((n, lane), lambda i, L: (0, 1)),
+                pl.BlockSpec((n, lane), lambda i, L: (0, 2)),
             ],
             out_specs=[pl.BlockSpec((TILE, lane), lambda i, L: (i, 0)), pl.BlockSpec((heads, TILE), lambda i, L: (0, i))],
             scratch_shapes=[
-                pltpu.VMEM((heads * TILE, lane), jnp.bfloat16),
-                pltpu.VMEM((lane, TILE), jnp.float32),
-                pltpu.VMEM((wide[0] * TILE, heads * TILE), jnp.bfloat16),
-                pltpu.VMEM((lane, n), jnp.bfloat16),
+                pltpu.VMEM((wide, lane), bf16), pltpu.VMEM((lane, TILE), f32),
+                pltpu.VMEM((TILE, wide), f32), pltpu.VMEM((TILE, wide), f32), pltpu.VMEM((TILE, wide), bf16), pltpu.VMEM((TILE, wide), bf16),
+                pltpu.VMEM((heads, TILE), f32), pltpu.VMEM((heads, TILE), f32), pltpu.VMEM((heads, TILE), f32), pltpu.VMEM((heads, TILE), f32),
+                pltpu.VMEM((lane, n), bf16),
             ],
         ),
-        out_shape=[jax.ShapeDtypeStruct((n, lane), jnp.bfloat16), jax.ShapeDtypeStruct((heads, n), jnp.float32)],
-        compiler_params=pltpu.CompilerParams(vmem_limit_bytes=40 * 2**20),
+        out_shape=[jax.ShapeDtypeStruct((n, lane), bf16), jax.ShapeDtypeStruct((heads, n), f32)],
+        compiler_params=pltpu.CompilerParams(vmem_limit_bytes=58 * 2**20),
         cost_estimate=pl.CostEstimate(flops=n * n * lane * 9, bytes_accessed=10 * n * lane, transcendentals=n * n * heads // 2),
         name="attn_fwd",
     )(lengths, qkv, qkv, qkv)
@@ -203,7 +260,7 @@
             ],
         ),
         out_shape=jax.ShapeDtypeStruct(qkv.shape, jnp.bfloat16),
-        compiler_params=pltpu.CompilerParams(vmem_limit_bytes=40 * 2**20),
+        compiler_params=pltpu.CompilerParams(vmem_limit_bytes=58 * 2**20),
         cost_estimate=pl.CostEstimate(flops=n * n * lane * 11, bytes_accessed=20 * n * lane, transcendentals=n * n * heads // 2),
         name="attn_bwd",
     )(lengths, qkv, do, o, lse, qkv, qkv)
@@ -244,17 +301,57 @@
 
 
 def ffn_kernel(
-    x_ref, cot_ref, att_ref, wo_ref, up_ref, down_ref, gain_ref, shift_ref, bias_ref, fb_ref,
-    mixed_ref, mid_ref, n_ref, r_ref, low_ref, turned_ref, second_t, act_ref, slope_ref, small_ref,
-    second, branch, ffn, sums, *, tiles, strip,
+    x_hbm, cot_hbm, own_hbm, wo_hbm, up_ref, down_ref, gain_ref, shift_ref, bias_ref, fb_ref,
+    mixed_ref, mid_out, n_out, r_ref, low_ref, turned_ref, second_out, act_ref, slope_ref, small_ref, att_out,
+    x_ref, cot_ref, wo_ref, mid_ref, n_ref, second_t, att_ref, second, branch, ffn, sums, sends, recvs, own_sem, load_sems, save_sems, *, tiles, strip,
 ):
     s = pl.program_id(0)
     rows, width = x_ref.shape
     f32 = jnp.float32
 
+    def loaded(i):
+        return pltpu.make_async_copy((x_hbm, cot_hbm, wo_hbm)[i], (x_ref, cot_ref, wo_ref)[i], load_sems.at[i])
+
+    def saved(i):
+        pairs = ((mid_ref, mid_out), (n_ref, n_out), (second_t, second_out), (att_ref, att_out))
+        return pltpu.make_async_copy(*pairs[i], save_sems.at[i])
+
     @pl.when(s == 0)
     def _():
+        me = lax.axis_index("blk")
+        own = width // 4
+        peers = (me + 1 - 2 * lax.rem(me, 2), lax.rem(me + 2, 4), 3 - me)
+        mesh_ids = pl.DeviceIdType.MESH
+        barrier = pltpu.get_barrier_semaphore()
+        for block in peers:
+            pl.semaphore_signal(barrier, inc=1, device_id={"blk": block}, device_id_type=mesh_ids)
+        pl.semaphore_wait(barrier, 3)
+
+        def rows_of(block):
+            return own_hbm.at[pl.ds(pl.multiple_of(block * rows, rows), rows), :]
+
+        here = att_ref.at[:, pl.ds(pl.multiple_of(me * own, own), own)]
+        copies = [
+            pltpu.make_async_remote_copy(
+                src_ref=rows_of(block), dst_ref=here, send_sem=sends.at[i], recv_sem=recvs.at[i],
+                device_id={"blk": block}, device_id_type=mesh_ids,
+            )
+            for i, block in enumerate(peers)
+        ]
+        for copy in copies[::-1]:
+            copy.start()
+        mine = pltpu.make_async_copy(rows_of(me), here, own_sem)
+        mine.start()
+        for i in (2, 0, 1):
+            loaded(i).start()
         sums[...] = jnp.zeros_like(sums)
+        mine.wait()
+        for i in range(3):
+            loaded(i).wait()
+        for copy in copies:
+            copy.wait_send()
+            copy.wait_recv()
+        saved(3).start()
         branch[...] = jnp.dot(att_ref[...], wo_ref[...], preferred_element_type=f32) + _row(bias_ref, 2)
 
         def normed(at):
@@ -268,6 +365,8 @@
 
         _each(rows, strip, normed)
         second_t[...] = second[...].T
+        for i in range(3):
+            saved(i).start()
 
     u = jnp.dot(second[...], up_ref[...], preferred_element_type=f32) + fb_ref[...]
     c1, c3 = 0.7978845608028654, 0.7978845608028654 * 0.044715
@@ -301,6 +400,8 @@
 
         _each(rows, strip, normed)
         _turn_blocks(turned_ref, low_ref[...], lax.rem(lax.axis_index("blk"), 2))
+        for i in range(4):
+            saved(i).wait()
         for i in range(3):
             small_ref[pl.ds(i, 1), :] = jnp.sum(sums[pl.ds(8 * i, 8), :], 0, keepdims=True)
 
@@ -320,32 +421,37 @@
         functools.partial(ffn_kernel, tiles=tiles, strip=rows // 4),
         grid=(tiles,),
         in_specs=[
-            _once(rows, width), _once(rows, width), _once(rows, width), _once(width, width),
+            *[pl.BlockSpec(memory_space=pl.ANY)] * 4,
             pl.BlockSpec((width, hid), lambda s: (0, s)), pl.BlockSpec((hid, width), lambda s: (s, 0)),
             _once(4, width), _once(4, width), _once(4, width), pl.BlockSpec((1, hid), lambda s: (0, s)),
         ],
         out_specs=[
-            _once(rows, width), _once(rows, width), _once(rows, width), _once(rows, 1), _once(rows, width),
-            _once(width, rows), _once(width, rows),
-            pl.BlockSpec((rows, hid), lambda s: (0, s)), pl.BlockSpec((rows, hid), lambda s: (0, s)), _once(8, width),
+            _once(rows, width), *[pl.BlockSpec(memory_space=pl.ANY)] * 2, _once(rows, 1), _once(rows, width),
+            _once(width, rows), pl.BlockSpec(memory_space=pl.ANY),
+            pl.BlockSpec((rows, hid), lambda s: (0, s)), pl.BlockSpec((rows, hid), lambda s: (0, s)), _once(8, width), pl.BlockSpec(memory_space=pl.ANY),
         ],
         out_shape=[
             shape((rows, width), bf16), shape((rows, width), f32), shape((rows, width), bf16), shape((rows, 1), f32),
             shape((rows, width), bf16), shape((width, rows), bf16), shape((width, rows), bf16),
-            shape((rows, hidden), bf16), shape((rows, hidden), bf16), shape((8, width), f32),
+            shape((rows, hidden), bf16), shape((rows, hidden), bf16), shape((8, width), f32), shape((rows, width), bf16),
         ],
-        scratch_shapes=[pltpu.VMEM((rows, width), bf16), pltpu.VMEM((rows, width), f32), pltpu.VMEM((rows, width), f32), pltpu.VMEM((24, width), f32)],
-        compiler_params=pltpu.CompilerParams(vmem_limit_bytes=52 * 2**20),
+        scratch_shapes=[
+            pltpu.VMEM((rows, width), bf16), pltpu.VMEM((rows, width), bf16), pltpu.VMEM((width, width), bf16), pltpu.VMEM((rows, width), f32),
+            pltpu.VMEM((rows, width), bf16), pltpu.VMEM((width, rows), bf16), pltpu.VMEM((rows, width), bf16),
+            pltpu.VMEM((rows, width), bf16), pltpu.VMEM((rows, width), f32), pltpu.VMEM((rows, width), f32), pltpu.VMEM((24, width), f32), pltpu.SemaphoreType.DMA((3,)), pltpu.SemaphoreType.DMA((3,)), pltpu.SemaphoreType.DMA(()),
+            pltpu.SemaphoreType.DMA((3,)), pltpu.SemaphoreType.DMA((4,)),
+        ],
+        compiler_params=pltpu.CompilerParams(collective_id=3, has_side_effects=True, vmem_limit_bytes=56 * 2**20),
         cost_estimate=pl.CostEstimate(flops=18 * rows * width * width, bytes_accessed=50 * 2**20, transcendentals=rows * hidden),
         name="ffn_forward",
     )(tokens, cotangent, attended, out_weight, up_weight, down_weight, norm_gain, norm_bias, proj_bias, ffn_bias.reshape(1, -1))
 
 
 def grads_kernel(
-    low_ref, turned_ref, second_t, act_ref, slope_ref, up_ref, down_ref, mid_hbm, n_hbm, r_ref, cot_ref, att_ref, wo_ref, gain_ref,
-    gmid_ref, small_ref, hid_ref, up_out, down_out, out_out, gown_out,
-    pre, gs, low, turned, gatt, sums, up_buf, up_in, up_y, down_send, down_keep, down_in, down_x,
-    up_core, up_core_in, up_far, up_far_in, down_core, down_core_in, down_far, down_far_in, up_done, down_done, own_sems, gatt_sends, gatt_recvs, *, tiles, strip, fold,
+    low_ref, turned_hbm, second_hbm, act_ref, slope_ref, up_ref, down_ref, mid_hbm, n_hbm, r_ref, cot_hbm, att_hbm, wo_hbm, gain_ref,
+    gmid_ref, small_ref, hid_ref, up_out, down_out, out_out, gown_out, out_line,
+    turned_ref, second_t, cot_ref, att_ref, wo_ref, pre, gs, low, turned, gatt, sums, up_buf, up_in, up_y, down_send, down_keep, down_in, down_x, up_z,
+    up_core, up_core_in, up_far, up_far_in, down_core, down_core_in, down_far, down_far_in, up_done, down_done, own_sems, gatt_sends, gatt_recvs, line_sends, line_recvs, save_sems, *, tiles, strip, fold,
 ):
     s = pl.program_id(0)
     rows, width = low_ref.shape
@@ -354,6 +460,7 @@
     pair, side = s // 2, lax.rem(s, 2)
     me, place = lax.axis_index("blk"), lax.axis_index("dp")
     core, chip, near = lax.rem(me, 2), me // 2, lax.rem(place, 2)
+    line = place // 2
     twin, other, beside = {"blk": me + 1 - 2 * core}, {"blk": lax.rem(me + 2, 4)}, {"dp": place + 1 - 2 * near}
     last = {"blk": 3 - me}
     half = tiles // 2
@@ -377,14 +484,32 @@
         return remote(down_keep.at[u, 1 - chip], down_x.at[u], down_far, down_far_in, u, other)
 
     def up_result(p):
+        if fold:
+            return pltpu.make_async_copy(up_y.at[p, line], up_out.at[p], up_done.at[p])
         return pltpu.make_async_copy(up_y.at[p], up_out.at[:, p], up_done.at[p])
+
+    def up_to_line(p, k):
+        ahead = lax.rem(line + k, 4)
+        return remote(up_y.at[p, ahead], up_z.at[k - 1, p], line_sends, line_recvs, 3 * p + k - 1, {"dp": 2 * ahead + near})
+
+    def join_line(p):
+        total = up_y[p, line].astype(f32)
+        for k in range(1, 4):
+            up_to_line(p, k).wait_recv()
+            total += up_z[k - 1, p].astype(f32)
+        up_y[p, line] = total.astype(bf16)
+        up_result(p).start()
 
     def down_result(u):
         tile = 4 * (u // 4) + 2 * lax.rem(u, 2) + lax.rem(u // 2, 2)
         return pltpu.make_async_copy(down_x.at[u], down_out.at[tile], down_done.at[u])
 
     def saved(i):
-        return pltpu.make_async_copy((mid_hbm, n_hbm)[i], (gmid_ref, low)[i], own_sems.at[i])
+        pairs = ((mid_hbm, gmid_ref), (n_hbm, low), (cot_hbm, cot_ref), (att_hbm, att_ref), (wo_hbm, wo_ref), (turned_hbm, turned_ref), (second_hbm, second_t))
+        return pltpu.make_async_copy(*pairs[i], save_sems.at[i])
+
+    def out_line_result():
+        return pltpu.make_async_copy(up_y.at[half], out_line, own_sems.at[0])
 
     def out_result(i):
         return pltpu.make_async_copy(up_buf.at[i], out_out.at[i], own_sems.at[2 + i])
@@ -408,23 +533,21 @@
     def join_far_up(p):
         up_to_beside(p).wait_recv()
         up_y[p] = (up_y[p].astype(f32) + up_in[p, :, near].astype(f32)).astype(bf16)
-        up_result(p).start()
-
-    def join_cores(p):
-        join_up(p)
-        for c in range(2):
-            u = 2 * p + c
-            down_to_twin(u, c).wait_recv()
-            down_keep[u] = (down_keep[u].astype(f32) + down_in[lax.rem(u, 4)].astype(f32)).astype(bf16)
-            down_to_other(u).start()
-
-    def join_far(p):
-        join_far_up(p)
-        for c in range(2):
-            u = 2 * p + c
-            down_to_other(u).wait_recv()
-            down_x[u] = (down_x[u].astype(f32) + down_keep[u, chip].astype(f32)).astype(bf16)
-            down_result(u).start()
+        if fold:
+            for k in range(1, 4):
+                up_to_line(p, k).start()
+        else:
+            up_result(p).start()
+
+    def join_down(u):
+        down_to_twin(u, 0).wait_recv()
+        down_keep[u] = (down_keep[u].astype(f32) + down_in[lax.rem(u, 4)].astype(f32)).astype(bf16)
+        down_to_other(u).start()
+
+    def join_far_down(u):
+        down_to_other(u).wait_recv()
+        down_x[u] = (down_x[u].astype(f32) + down_keep[u, chip].astype(f32)).astype(bf16)
+        down_result(u).start()
 
     @pl.when(s == 0)
     def _():
@@ -432,17 +555,28 @@
         for target in (twin, other, beside, last):
             pl.semaphore_signal(barrier, inc=1, device_id=target, device_id_type=mesh_ids)
         sums[...] = jnp.zeros_like(sums)
-        saved(0).start()
-        saved(1).start()
-        pl.semaphore_wait(barrier, 4)
+        for i in (5, 6, 0, 1, 2, 3, 4):
+            saved(i).start()
+        for i in range(1, 4 if fold else 1):
+            ahead = lax.rem(line + i, 4)
+            pl.semaphore_signal(barrier, inc=1, device_id={"dp": 2 * ahead + near}, device_id_type=mesh_ids)
+        pl.semaphore_wait(barrier, 7 if fold else 4)
+
+    @pl.when(s > 0)
+    def _():
+        join_down(s - 1)
 
     @pl.when((side == 0) & (s > 0))
     def _():
-        join_cores(pair - 1)
-
-    @pl.when(s == 6)
-    def _():
-        join_far(0)
+        join_up(pair - 1)
+
+    @pl.when(s >= 3)
+    def _():
+        join_far_down(s - 3)
+
+    @pl.when((s == 5) | (s == 7))
+    def _():
+        join_far_up((s - 5) // 2)
 
     g = lax.dot_general(low_ref[...], down_ref[...], NT, preferred_element_type=f32) * slope_ref[...].astype(f32)
     g = g.astype(bf16)
@@ -457,6 +591,11 @@
     @pl.when(s > 0)
     def _():
         gs[...] += part
+
+    @pl.when(s == 0)
+    def _():
+        saved(5).wait()
+        saved(6).wait()
 
     down_grad = jnp.dot(turned_ref[...], act_ref[...], preferred_element_type=f32).astype(bf16)
 
@@ -498,14 +637,16 @@
             sums[pl.ds(16, 8), :] += _fold(gm)
             sums[pl.ds(32, 8), :] += _fold(g.astype(f32))
 
-        join_cores(tiles // 2 - 1)
-        saved(0).wait()
-        saved(1).wait()
+        join_down(tiles - 1)
+        join_up(half - 1)
+        for i in range(5):
+            saved(i).wait()
         _each(rows, strip, normed)
         gatt[...] = lax.dot_general(low[...], wo_ref[...], NT, preferred_element_type=f32).astype(bf16)
         for i in range(3):
             columns_to(i).start()
         columns_here().start()
+        join_far_up(2)
         _turn_blocks(turned, low[...], core)
         grad = jnp.dot(turned[...], att_ref[...], preferred_element_type=f32).astype(bf16)
         up_to_twin(half - 1).wait_send()
@@ -524,10 +665,16 @@
             small_ref[pl.ds(i, 1), :] = jnp.sum(sums[pl.ds(8 * i, 8), :], 0, keepdims=True)
         if fold:
             join_up(half)
-        for p in range(1, half):
-            join_far(p)
+        join_far_up(3)
+        for u in range(tiles - 3, tiles):
+            join_far_down(u)
         if fold:
-            join_far_up(half)
+            for p in range(half):
+                join_line(p)
+            up_to_beside(half).wait_recv()
+            up_y[half] = (up_y[half].astype(f32) + up_in[half, :, near].astype(f32)).astype(bf16)
+            out_line_result().start()
+            out_line_result().wait()
         down_to_twin(tiles - 2, 0).wait_send()
         down_to_twin(tiles - 1, 1).wait_send()
         if fold:
@@ -537,7 +684,10 @@
             out_result(1).wait()
         for p in range(half + fold):
             up_to_beside(p).wait_send()
+        for p in range(half):
             up_result(p).wait()
+            for i in range(1, 4 if fold else 1):
+                up_to_line(p, i).wait_send()
         for u in range(tiles):
             down_to_other(u).wait_send()
             down_result(u).wait()
@@ -563,41 +713,47 @@
         functools.partial(grads_kernel, tiles=tiles, strip=rows // 4, fold=fold),
         grid=(tiles,),
         in_specs=[
-            _once(rows, width), _once(width, rows), _once(width, rows),
+            _once(rows, width), pl.BlockSpec(memory_space=pl.ANY), pl.BlockSpec(memory_space=pl.ANY),
             pl.BlockSpec((rows, hid), lambda s: (0, tile_of(s))), pl.BlockSpec((rows, hid), lambda s: (0, tile_of(s))),
             pl.BlockSpec((width, hid), lambda s: (0, tile_of(s))), pl.BlockSpec((hid, width), lambda s: (tile_of(s), 0)),
-            pl.BlockSpec(memory_space=pl.ANY), pl.BlockSpec(memory_space=pl.ANY), _once(rows, 1), _once(rows, width), _once(rows, width), _once(width, width), _once(4, width),
+            pl.BlockSpec(memory_space=pl.ANY), pl.BlockSpec(memory_space=pl.ANY), _once(rows, 1), *[pl.BlockSpec(memory_space=pl.ANY)] * 3, _once(4, width),
         ],
         out_specs=[
             _once(rows, width), _once(8, width), _once(tiles, 1, hid),
-            pl.BlockSpec(memory_space=pl.ANY), pl.BlockSpec(memory_space=pl.ANY), pl.BlockSpec(memory_space=pl.ANY), pl.BlockSpec(memory_space=pl.ANY),
+            *[pl.BlockSpec(memory_space=pl.ANY)] * 5,
         ],
         out_shape=[
             shape((rows, width), f32),
             shape((8, width), f32), shape((tiles, 1, hid), f32),
-            shape((parts // 2, half + fold, width // parts, hid), bf16), shape((tiles, own, hid), bf16), shape((2,) + thin, bf16),
-            shape((4 * rows, own), bf16),
+            shape((half, width // parts, hid) if fold else (parts // 2, half, width // parts, hid), bf16), shape((tiles, own, hid), bf16), shape((2,) + thin, bf16),
+            shape((4 * rows, own), bf16), shape((parts // 2, width // parts, hid), bf16),
         ],
         scratch_shapes=[
-            pltpu.VMEM((rows, hid), bf16), pltpu.VMEM((rows, width), f32), pltpu.VMEM((rows, width), bf16), pltpu.VMEM((width, rows), bf16), pltpu.VMEM((rows, width), bf16),
+            pltpu.VMEM((width, rows), bf16), pltpu.VMEM((width, rows), bf16), pltpu.VMEM((rows, width), bf16), pltpu.VMEM((rows, width), bf16),
+            pltpu.VMEM((width, width), bf16), pltpu.VMEM((rows, hid), bf16), pltpu.VMEM((rows, width), f32), pltpu.VMEM((rows, width), bf16), pltpu.VMEM((width, rows), bf16), pltpu.VMEM((rows, width), bf16),
             pltpu.VMEM((40, width), f32),
             pltpu.VMEM((2,) + thin, bf16), pltpu.VMEM((half + fold,) + thin, bf16), pltpu.VMEM((half + fold, parts // 2, width // parts, hid), bf16),
             pltpu.VMEM((2, 2, own, hid), bf16), pltpu.VMEM((tiles, 2, own, hid), bf16), pltpu.VMEM((4, 2, own, hid), bf16),
-            pltpu.VMEM((tiles, own, hid), bf16),
-            *[dma((half + fold,))] * 4, *[dma((tiles,))] * 4, dma((half + fold,)), dma((tiles,)), dma((5,)), dma((3,)), dma((3,)),
+            pltpu.VMEM((tiles, own, hid), bf16), pltpu.VMEM((3, half, width // parts, hid), bf16),
+            *[dma((half + fold,))] * 4, *[dma((tiles,))] * 4, dma((half + fold,)), dma((tiles,)), dma((5,)), dma((3,)), dma((3,)), dma((3 * half,)), dma((3 * half,)), dma((7,)),
         ],
         compiler_params=pltpu.CompilerParams(collective_id=1, has_side_effects=True, vmem_limit_bytes=60 * 2**20),
         name="ffn_backward",
     )(low, turned, second_t, act, slope, up_weight, down_weight, mid, n_one, r_one, cotangent, attended, out_weight, norm_gain)
 
 
-def project_kernel(x_ref, w_hbm, gain_ref, shift_ref, bias_ref, all_ref, qkv_ref, w_ref, w_sems, chip_send, chip_recv, core_send, core_recv, pass_send, pass_recv, *, pieces):
+def project_kernel(
+    x_hbm, w_hbm, gain_ref, shift_ref, bias_ref, all_out, qkv_out, w_out, x_ref, all_ref, qkv_ref, w_ref, x_sems, out_sems, w_sems, chip_send, chip_recv, core_send, core_recv, pass_send, pass_recv, *, pieces,
+):
     me = lax.axis_index("blk")
     core = lax.rem(me, 2)
     twin, other, last = me + 1 - 2 * core, lax.rem(me + 2, 4), 3 - me
     rows, width = x_ref.shape
     own = width // 4
     size = rows // pieces
+    fetch = [pltpu.make_async_copy(x_hbm.at[pl.ds(i * size, size), :], x_ref.at[pl.ds(i * size, size), :], x_sems.at[i]) for i in range(pieces)]
+    for copy in fetch:
+        copy.start()
     barrier = pltpu.get_barrier_semaphore()
     for target in (twin, other):
         pl.semaphore_signal(barrier, inc=1, device_id={"blk": target}, device_id_type=pl.DeviceIdType.MESH)
@@ -621,11 +777,20 @@
 
     def project(block, i):
         where = at(block, i)
-        got = jnp.dot(all_ref[where, :], w_ref[...], preferred_element_type=jnp.float32) + bias_ref[...]
-        qkv_ref[where, :] = got.astype(jnp.bfloat16)
-
-    sent = []
+        got = jnp.dot(all_ref[where, :], w_ref[...], preferred_element_type=jnp.float32)
+        for third in range(3):
+            part = got[:, third * own : (third + 1) * own]
+            if third != 1:
+                part = part + bias_ref[pl.ds(third // 2, 1), pl.ds(pl.multiple_of(me * own, own), own)]
+            qkv_ref[where, pl.ds(third * own, own)] = part.astype(jnp.bfloat16)
+        for src, dst in ((all_ref, all_out), (qkv_ref, qkv_out)):
+            copy = pltpu.make_async_copy(src.at[where, :], dst.at[where, :], out_sems.at[len(saved)])
+            copy.start()
+            saved.append(copy)
+
+    sent, saved = [], []
     for i in range(pieces):
+        fetch[i].wait()
         n, _ = _stats(x_ref[pl.ds(i * size, size), :].astype(jnp.float32))
         all_ref[at(me, i), :] = (n * gain_ref[pl.ds(0, 1), :] + shift_ref[pl.ds(0, 1), :]).astype(jnp.bfloat16)
         if i == 0:
@@ -636,6 +801,8 @@
             sent.append(copy)
     for load in loads:
         load.wait()
+    keep = pltpu.make_async_copy(w_ref, w_out, w_sems.at[3])
+    keep.start()
     for i in range(pieces):
         project(me, i)
     for i in range(pieces):
@@ -654,22 +821,287 @@
     project(last, pieces - 1)
     for copy in sent:
         copy.wait_send()
-
-
-def gather_project(tokens, qkv_weight, norm_gain, norm_bias, bias):
+    for copy in saved:
+        copy.wait()
+    keep.wait()
+
+
+def gather_project(tokens, qkv_weight, norm_gain, norm_bias, proj_bias):
     rows, width = tokens.shape
     pieces = 4
-    vmem = pl.BlockSpec(memory_space=pltpu.VMEM)
+    vmem, hbm = pl.BlockSpec(memory_space=pltpu.VMEM), pl.BlockSpec(memory_space=pl.ANY)
     dma = pltpu.SemaphoreType.DMA((pieces,))
     return pl.pallas_call(
         functools.partial(project_kernel, pieces=pieces),
-        in_specs=[vmem, pl.BlockSpec(memory_space=pl.ANY), vmem, vmem, vmem],
-        out_specs=[vmem, vmem],
-        out_shape=[jax.ShapeDtypeStruct((4 * rows, width), jnp.bfloat16), jax.ShapeDtypeStruct((4 * rows, 3 * width // 4), jnp.bfloat16)],
-        scratch_shapes=[pltpu.VMEM((width, 3 * width // 4), jnp.bfloat16), pltpu.SemaphoreType.DMA((3,))] + [dma] * 6,
+        in_specs=[hbm, hbm, vmem, vmem, vmem],
+        out_specs=[hbm] * 3,
+        out_shape=[jax.ShapeDtypeStruct((4 * rows, width), jnp.bfloat16), jax.ShapeDtypeStruct((4 * rows, 3 * width // 4), jnp.bfloat16), jax.ShapeDtypeStruct((width, 3 * width // 4), jnp.bfloat16)],
+        scratch_shapes=[
+            pltpu.VMEM((rows, width), jnp.bfloat16), pltpu.VMEM((4 * rows, width), jnp.bfloat16),
+            pltpu.VMEM((4 * rows, 3 * width // 4), jnp.bfloat16), pltpu.VMEM((width, 3 * width // 4), jnp.bfloat16),
+            dma, pltpu.SemaphoreType.DMA((8 * pieces,)), pltpu.SemaphoreType.DMA((4,)),
+        ] + [dma] * 6,
         compiler_params=pltpu.CompilerParams(collective_id=0, has_side_effects=True, vmem_limit_bytes=48 * 2**20),
         name="gather_project",
-    )(tokens, qkv_weight, norm_gain, norm_bias, bias)
+    )(tokens, qkv_weight, norm_gain, norm_bias, proj_bias)
+
+
+def tail_kernel(
+    d_hbm, first_hbm, w_hbm, x_hbm, gmid_hbm, gain_ref, up_ref, out_ref, sums_ref, three_ref, hid_ref,
+    token_ref, qkv_ref, up_grad_ref, out_grad_ref, gain_grad_ref, shift_grad_ref, bias_grad_ref, hid_grad_ref,
+    d, first, w, x, gmid, turned, core_out, core_in, far_out, far_in, mine, cols, cols_in, line_out, line_in, total, heads_in, part, part_in, both, both_in, sums, up_in, out_in, out_sum, out_far,
+    loads, core_send, core_recv, far_send, far_recv, y_send, y_recv, z_send, z_recv, q_send, q_recv, s_send, s_recv, b_send, b_recv, h_send, h_recv, o_send, o_recv, *, pieces,
+):
+    f32, bf16 = jnp.float32, jnp.bfloat16
+    rows, width = x.shape
+    own = width // 4
+    size = rows // pieces
+    thin = width // 8
+    me, place = lax.axis_index("blk"), lax.axis_index("dp")
+    core, near, line = lax.rem(me, 2), lax.rem(place, 2), place // 2
+    twin, other, last = me + 1 - 2 * core, lax.rem(me + 2, 4), 3 - me
+    mesh_ids = pl.DeviceIdType.MESH
+
+    def remote(src, dst, sends, recvs, i, target):
+        return pltpu.make_async_remote_copy(
+            src_ref=src, dst_ref=dst, send_sem=sends.at[i], recv_sem=recvs.at[i], device_id=target, device_id_type=mesh_ids
+        )
+
+    def rows_of(block, i):
+        return pl.ds(pl.multiple_of(block * rows + i * size, size), size)
+
+    def piece(i):
+        return pl.ds(i * size, size)
+
+    barrier = pltpu.get_barrier_semaphore()
+    for block in (twin, other, last):
+        pl.semaphore_signal(barrier, inc=1, device_id={"blk": block}, device_id_type=mesh_ids)
+    for k in range(1, 8):
+        pl.semaphore_signal(barrier, inc=1, device_id={"dp": lax.rem(place + k, 8)}, device_id_type=mesh_ids)
+
+    def block_rows(block):
+        return pl.ds(pl.multiple_of(block * rows, rows), rows)
+
+    fetch = [pltpu.make_async_copy(w_hbm, w, loads.at[0])]
+    for i, block in enumerate((last, other, me, twin)):
+        fetch.append(pltpu.make_async_copy(d_hbm.at[block_rows(block), :], d.at[block_rows(block), :], loads.at[1 + i]))
+    for i, (src, dst) in enumerate(((first_hbm, first), (x_hbm, x), (gmid_hbm, gmid))):
+        fetch.append(pltpu.make_async_copy(src, dst, loads.at[5 + i]))
+    for copy in fetch[:3]:
+        copy.start()
+
+    def partial(block, i):
+        return lax.dot_general(d[rows_of(block, i), :], w[...], NT, preferred_element_type=f32)
+
+    def to_twin(kind, i):
+        return remote(core_out.at[kind, piece(i), :], core_in.at[kind, piece(i), :], core_send, core_recv, kind * pieces + i, {"blk": twin})
+
+    def to_other(i):
+        return remote(far_out.at[piece(i), :], far_in.at[piece(i), :], far_send, far_recv, i, {"blk": other})
+
+    def to_beside(k):
+        return remote(cols.at[k, 1 - near], cols_in.at[k], y_send, y_recv, k, {"dp": place + 1 - 2 * near})
+
+    def to_line(k):
+        return remote(line_out.at[k], line_in.at[k], z_send, z_recv, k, {"dp": 2 * lax.rem(line + k, 4) + near})
+
+    pl.semaphore_wait(barrier, 10)
+    chip = me // 2
+    weights = remote(up_ref.at[pl.ds(2 * (1 - chip), 2)], up_in, h_send, h_recv, 0, {"blk": other})
+    weights.start()
+
+    def out_to_line(k):
+        ahead = lax.rem(line + k, 4)
+        return remote(out_ref.at[ahead], out_in.at[k - 1], o_send, o_recv, k - 1, {"dp": 2 * ahead + near})
+
+    out_to_other = remote(out_sum.at[1 - chip], out_far, h_send, h_recv, 1, {"blk": other})
+    for k in range(1, 4):
+        out_to_line(k).start()
+    fetch[0].wait()
+    fetch[1].wait()
+    for copy in fetch[3:]:
+        copy.start()
+    for i in range(pieces):
+        core_out[0, piece(i), :] = partial(last, i).astype(bf16)
+        to_twin(0, i).start()
+    fetch[2].wait()
+    for i in range(pieces):
+        got = partial(other, i)
+        to_twin(0, i).wait_recv()
+        far_out[piece(i), :] = (got + core_in[0, piece(i), :].astype(f32)).astype(bf16)
+        to_other(i).start()
+    fetch[3].wait()
+    fetch[4].wait()
+    for i in range(d.shape[0] // 256):
+        turned[:, pl.ds(i * 256, 256)] = d[pl.ds(i * 256, 256), :].T
+    fetch[5].wait()
+    for k in (1, 2, 3, 0):
+        where = pl.ds(pl.multiple_of(lax.rem(line + k, 4) * 2 * thin, 2 * thin), 2 * thin)
+        got = jnp.dot(turned[...], first[:, where], preferred_element_type=f32).astype(bf16)
+        cols[k, 0] = got[:, :thin]
+        cols[k, 1] = got[:, thin:]
+        to_beside(k).start()
+    for i in range(pieces):
+        core_out[1, piece(i), :] = partial(twin, i).astype(bf16)
+        to_twin(1, i).start()
+    for i in range(pieces):
+        mine[piece(i), :] = partial(me, i)
+    ones = jnp.ones((8, d.shape[0]), bf16)
+    column = jnp.dot(ones, d[...], preferred_element_type=f32)
+    part[...] = jnp.zeros_like(part)
+    for k in range(8):
+        lanes = pl.ds(k * thin, thin)
+        for i, (ref, j) in ((1, (sums_ref, 0)), (2, (sums_ref, 1)), (3, (three_ref, 0)), (5, (sums_ref, 2)), (6, (sums_ref, 3)), (7, (three_ref, 1)), (10, (sums_ref, 4)), (11, (three_ref, 2))):
+            part[k, pl.ds(i, 1), :] = ref[pl.ds(j, 1), lanes]
+        tile = 4 * (k // 4) + 2 * (k % 2) + k // 2 % 2
+        for i in range(4):
+            part[tile, pl.ds(12 + i, 1), :] = hid_ref[k, :, pl.ds(i * thin, thin)]
+    for h in range(2):
+        part[2 * me + h, pl.ds(8, 1), :] = column[:1, h * thin : (h + 1) * thin]
+        part[2 * me + h, pl.ds(9, 1), :] = column[:1, 2 * own + h * thin : 2 * own + (h + 1) * thin]
+    fetch[6].wait()
+    fetch[7].wait()
+    sums[...] = jnp.zeros_like(sums)
+
+    def tokens(i):
+        at = piece(i)
+        to_twin(1, i).wait_recv()
+        n, r = _stats(x[at, :].astype(f32))
+        got = mine[at, :] + core_in[1, at, :].astype(f32)
+        to_other(i).wait_recv()
+        y = got + far_in[at, :].astype(f32)
+        token_ref[at, :] = (gmid[at, :] + _pull(n, r, y * _row(gain_ref, 0))).astype(bf16)
+        sums[pl.ds(0, 8), :] += _fold(y * n)
+        sums[pl.ds(8, 8), :] += _fold(y)
+
+    for k in (1, 2, 3):
+        to_beside(k).wait_recv()
+        line_out[k] = (cols[k, near].astype(f32) + cols_in[k].astype(f32)).astype(bf16)
+        to_line(k).start()
+    for k in range(1, 4):
+        out_to_line(k).wait_recv()
+    got = out_ref[line].astype(f32)
+    for k in range(3):
+        got += out_in[k].astype(f32)
+    out_sum[0] = got[:, : 2 * thin].astype(bf16)
+    out_sum[1] = got[:, 2 * thin :].astype(bf16)
+    out_to_other.start()
+    weights.wait_recv()
+    for i in range(2):
+        up_grad_ref[:, pl.ds(i * 2 * own, 2 * own)] = up_ref[2 * chip + i].astype(f32) + up_in[i].astype(f32)
+    for i in range(pieces - 1):
+        tokens(i)
+    to_beside(0).wait_recv()
+    for k in (1, 2, 3):
+        to_line(k).wait_recv()
+    summed = cols[0, near].astype(f32) + cols_in[0].astype(f32)
+    for k in (1, 2, 3):
+        summed += line_in[k].astype(f32)
+    total[...] = summed.astype(bf16).reshape(total.shape)
+    def to_owner(third):
+        chunk = 4 * third + me
+        return remote(total.at[third], heads_in.at[lax.rem(chunk, 3)], q_send, q_recv, lax.rem(chunk, 3), {"blk": chunk // 3})
+
+    for third in range(3):
+        chunk = 4 * third + me
+
+        @pl.when(chunk // 3 != me)
+        def _(third=third):
+            to_owner(third).start()
+
+        @pl.when(chunk // 3 == me)
+        def _(third=third, chunk=chunk):
+            heads_in[lax.rem(chunk, 3)] = total[third]
+
+    out_to_other.wait_recv()
+    got = out_sum[chip].astype(f32) + out_far[...].astype(f32)
+    for i in range(2):
+        out_grad_ref[:, pl.ds(i * thin, thin)] = got[:, i * thin : (i + 1) * thin].T
+    tokens(pieces - 1)
+    for i in range(2):
+        line_sum = jnp.sum(sums[pl.ds(8 * i, 8), :], 0, keepdims=True)
+        for k in range(8):
+            part[k, pl.ds(4 * i, 1), :] = line_sum[:, k * thin : (k + 1) * thin]
+
+    def to_dp(k):
+        target = lax.rem(place + k, 8)
+        return remote(part.at[target], part_in.at[k], s_send, s_recv, k, {"dp": target})
+
+    def to_blk(k):
+        return remote(both, both_in.at[k], b_send, b_recv, k, {"blk": (twin, other, last)[k]})
+
+    for k in range(1, 8):
+        to_dp(k).start()
+    for s in range(3):
+        source = lax.rem(3 * me + s, 4)
+
+        @pl.when(source != me)
+        def _(s=s):
+            remote(total.at[0], heads_in.at[s], q_send, q_recv, s, {"blk": twin}).wait_recv()
+
+        qkv_ref[:, pl.ds(s * own, own)] = heads_in[s].astype(f32).T
+    acc = part[place]
+    for k in range(1, 8):
+        to_dp(k).wait_recv()
+        acc += part_in[k]
+    both[...] = acc
+    for k in range(3):
+        to_blk(k).start()
+    for k in range(3):
+        to_blk(k).wait_recv()
+        acc += both_in[k]
+    gain_grad_ref[...] = acc[:4]
+    shift_grad_ref[...] = acc[4:8]
+    bias_grad_ref[...] = acc[8:12]
+    hid_grad_ref[...] = acc[12:]
+    for i in range(pieces):
+        to_twin(0, i).wait_send()
+        to_twin(1, i).wait_send()
+        to_other(i).wait_send()
+    for k in range(4):
+        to_beside(k).wait_send()
+    for k in range(1, 4):
+        to_line(k).wait_send()
+    for third in range(3):
+
+        @pl.when((4 * third + me) // 3 != me)
+        def _(third=third):
+            to_owner(third).wait_send()
+
+    for k in range(1, 8):
+        to_dp(k).wait_send()
+    for k in range(3):
+        to_blk(k).wait_send()
+    weights.wait_send()
+    out_to_other.wait_send()
+    for k in range(1, 4):
+        out_to_line(k).wait_send()
+
+
+def finish(grads, first_all, own_weight, tokens, grad_middle, norm_gain, up_sum, out_line, sums, sums_three, hidden_bias):
+    rows, width = tokens.shape
+    total_rows, cols = grads.shape
+    own, thin, pieces = width // 4, width // 8, 4
+    bf16, f32 = jnp.bfloat16, jnp.float32
+    shape, vmem, hbm, dma = jax.ShapeDtypeStruct, pl.BlockSpec(memory_space=pltpu.VMEM), pl.BlockSpec(memory_space=pl.ANY), pltpu.SemaphoreType.DMA
+    buffers = [
+        ((total_rows, cols), bf16), ((total_rows, width), bf16), ((width, cols), bf16), ((rows, width), bf16), ((rows, width), f32),
+        ((cols, total_rows), bf16), ((2, rows, width), bf16), ((2, rows, width), bf16), ((rows, width), bf16), ((rows, width), bf16),
+        ((rows, width), f32), ((4, 2, cols, thin), bf16), ((4, cols, thin), bf16), ((4, cols, thin), bf16), ((4, cols, thin), bf16),
+        ((3, own, thin), bf16), ((3, own, thin), bf16), ((8, 16, thin), f32), ((8, 16, thin), f32), ((16, thin), f32), ((3, 16, thin), f32),
+        ((16, width), f32), ((2,) + up_sum.shape[1:], bf16), ((3,) + out_line.shape[1:], bf16), ((2, thin, own), bf16), ((thin, own), bf16),
+    ]
+    counts = [8, 2 * pieces, 2 * pieces, pieces, pieces, 4, 4, 4, 4, 3, 3, 8, 8, 3, 3, 2, 2, 3, 3]
+    return pl.pallas_call(
+        functools.partial(tail_kernel, pieces=pieces),
+        in_specs=[hbm] * 5 + [vmem] * 6,
+        out_specs=[vmem] * 8,
+        out_shape=[shape((rows, width), bf16), shape((thin, 3 * own), f32), shape((thin, width), f32), shape((thin, own), f32)] + [shape((4, thin), f32)] * 4,
+        scratch_shapes=[pltpu.VMEM(dims, kind) for dims, kind in buffers] + [dma((n,)) for n in counts],
+        compiler_params=pltpu.CompilerParams(collective_id=2, has_side_effects=True, vmem_limit_bytes=58 * 2**20),
+        cost_estimate=pl.CostEstimate(flops=60 * rows * width * width, bytes_accessed=2**27, transcendentals=0),
+        name="finish",
+    )(grads, first_all, own_weight, tokens, grad_middle, norm_gain, up_sum, out_line, sums, sums_three, hidden_bias)
 
 
 def outer_sum(left, right):
@@ -715,26 +1147,49 @@
     return pick(half, line, 0).astype(jnp.float32) + sum(piece.astype(jnp.float32) for piece in got)
 
 
-def weight_sums(up, down, out, own):
-    parts = lax.axis_size("dp")
-    chip = lax.axis_index("blk") // 2
-    width = 4 * own
-    groups = [[d for d in range(parts) if d % 2 == b] for b in range(2)]
-    up = lax.psum_scatter(up, "dp", scatter_dimension=0, axis_index_groups=groups, tiled=False)
-    halves = up[:4].reshape((2, 2) + up.shape[1:]).transpose(0, 2, 1, 3).reshape(2, up.shape[1], -1)
-    if parts == 8:
-        thin = up.shape[1]
-        halves = jnp.concatenate([halves, up[4].reshape(thin, 2, -1).transpose(1, 0, 2)], 2)
-    total = pick(halves, chip, 0).astype(jnp.float32) + exchange(pick(halves, 1 - chip, 0), "blk", 2).astype(jnp.float32)
-    if parts == 8:
-        out_grad = total[:, width:].reshape(thin, 2, thin).transpose(1, 0, 2).reshape(own, thin).T
-        down_grad = lax.psum_scatter(down, "dp", scatter_dimension=0, tiled=False).astype(jnp.float32).T
-    else:
-        down = down.transpose(1, 0, 2).reshape(own, parts, -1).transpose(1, 0, 2)
-        out = out.reshape(own, parts, width // parts).transpose(1, 0, 2)
-        both = lax.psum_scatter(jnp.concatenate([down, out], 2), "dp", scatter_dimension=0, tiled=False).astype(jnp.float32)
-        down_grad, out_grad = both[:, : down.shape[2]].T, both[:, down.shape[2] :].T
-    return total[:, :width], down_grad, out_grad
+def far_sums(values):
+    groups = [[d for d in range(lax.axis_size("dp")) if d % 2 == b] for b in range(2)]
+    return lax.psum_scatter(values, "dp", scatter_dimension=0, axis_index_groups=groups, tiled=False)
+
+
+def by_chip(up):
+    return up.reshape((2, 2) + up.shape[1:]).transpose(0, 2, 1, 3).reshape(2, up.shape[1], -1)
+
+
+def finish_plain(grads, first_all, own_weight, tokens, grad_middle, norm_gain, early, hidden_bias):
+    rows, width = tokens.shape
+    blocks, parts, me = lax.axis_size("blk"), lax.axis_size("dp"), lax.axis_index("blk")
+    core, chip, own = me % 2, me // 2, width // blocks
+    by_block = grads.reshape(2, 2, rows, 3 * own)
+    away = times_transposed(pick(by_block, 1 - core, 1).reshape(2 * rows, 3 * own), own_weight).astype(jnp.bfloat16)
+    got = exchange(away, "blk", 1)
+    stay = times_transposed(pick(by_block, core, 1).reshape(2 * rows, 3 * own), own_weight)
+    half = plus(stay, got).reshape(2, rows, width)
+    half, grads = lax.optimization_barrier((half, grads))
+    far = exchange(pick(half, 1 - chip, 0), "blk", 2)
+
+    term = outer_sum(first_all, grads).astype(jnp.bfloat16).reshape(parts // 2, 2, width // parts, 3 * own)
+    near = lax.rem(lax.axis_index("dp"), 2)
+    term = plus(pick(term, near, 1), exchange(pick(term, 1 - near, 1), "dp", 1))
+    qkv_term = far_sum(term).astype(jnp.bfloat16)
+    qkv_blocks = lax.all_gather(qkv_term, "blk", axis=0)
+    qkv_rows = qkv_blocks.reshape(blocks, -1, 3, own).transpose(1, 2, 0, 3).reshape(-1, 3 * width)
+    qkv_grad = lax.dynamic_slice_in_dim(qkv_rows, me * 3 * own, 3 * own, 1).astype(jnp.float32)
+
+    def spread(values):
+        return lax.dynamic_update_slice_in_dim(jnp.zeros((width,), jnp.float32), values, me * own, 0)
+
+    y = pick(half, chip, 0).astype(jnp.float32) + far.astype(jnp.float32)
+    n, r = _stats(tokens.astype(jnp.float32))
+    token_grad = (grad_middle + _pull(n, r, y * norm_gain[0])).astype(jnp.bfloat16)
+    late = {0: jnp.sum(y * n, 0), 4: jnp.sum(y, 0), 8: spread(column_sums(grads[:, :own])), 9: spread(column_sums(grads[:, 2 * own :]))}
+    small = jnp.stack([late.get(i, early[i]) for i in range(12)] + list(hidden_bias.reshape(-1, width)))
+    small = sum_everywhere(small)
+    place = lax.axis_index("dp")
+    chunk = width // parts
+    small_own = lax.dynamic_slice_in_dim(small[:12], place * chunk, chunk, 1)
+    hidden = lax.dynamic_slice_in_dim(small[12:].reshape(-1), place * 4 * chunk, 4 * chunk, 0)
+    return token_grad, qkv_grad, small_own, hidden
 
 
 def local(tokens, cotangent, lengths, qkv_weight, out_weight, up_weight, down_weight, norm_gain, norm_bias, proj_bias, ffn_bias):
@@ -745,67 +1200,37 @@
     core, chip = me % 2, me // 2
     own = width // blocks
 
-    def own_columns(values, third):
-        return lax.dynamic_slice_in_dim(values, third * width + me * own, own, values.ndim - 1)
-
-    own_weight = jnp.concatenate([own_columns(qkv_weight, third) for third in range(3)], 1)
-    query_bias = lax.dynamic_slice_in_dim(proj_bias[0], me * own, own)
-    value_bias = lax.dynamic_slice_in_dim(proj_bias[1], me * own, own)
-    own_bias = jnp.concatenate([query_bias, jnp.zeros_like(query_bias), value_bias]).reshape(1, -1)
-    first_all, qkv = gather_project(tokens, qkv_weight, norm_gain, norm_bias, own_bias)
+    first_all, qkv, own_weight = gather_project(tokens, qkv_weight, norm_gain, norm_bias, proj_bias)
     attended_own, log_total = attn_fwd(lengths, qkv)
-    attended = lax.all_to_all(attended_own, "blk", split_axis=0, concat_axis=1, tiled=True)
-
-    mixed, mid, n_one, r_one, low, turned, second_t, act, slope, sums_three = ffn_forward(
-        tokens, cotangent, attended, out_weight, up_weight, down_weight, norm_gain, norm_bias, proj_bias, ffn_bias
+
+    mixed, mid, n_one, r_one, low, turned, second_t, act, slope, sums_three, attended = ffn_forward(
+        tokens, cotangent, attended_own, out_weight, up_weight, down_weight, norm_gain, norm_bias, proj_bias, ffn_bias
     )
-    grad_middle, sums, hidden_bias, up_sum, down_sum, out_term, grad_own = ffn_backward(
+    grad_middle, sums, hidden_bias, up_sum, down_sum, out_term, grad_own, out_line = ffn_backward(
         parts, low, turned, second_t, act, slope, up_weight, down_weight, mid, n_one, r_one, cotangent, attended, out_weight, norm_gain
     )
+    grads = attn_bwd(lengths, qkv, grad_own, attended_own, log_total)
+
+    if parts == 8:
+        down_grad = lax.psum_scatter(down_sum, "dp", scatter_dimension=0, tiled=False).astype(jnp.float32).T
+        token_grad, qkv_grad, up_grad, out_grad, gains, shifts, biases, hidden = finish(
+            grads, first_all, own_weight, tokens, grad_middle, norm_gain, up_sum, out_line, sums, sums_three, hidden_bias
+        )
+        return (mixed, token_grad, qkv_grad, out_grad, up_grad, down_grad, gains, shifts, biases, hidden.reshape(-1))
+    early = [None, sums[0], sums[1], sums_three[0], None, sums[2], sums[3], sums_three[1], None, None, sums[4], sums_three[2]]
     hidden_bias = hidden_bias.reshape(2, 2, 2, -1).transpose(0, 2, 1, 3)
-    out_sum = None
-    if parts != 8:
-        out_term = out_term.reshape(2, 2, width // 2, width // 2).transpose(1, 2, 0, 3).reshape(2, 2, own, width)
-        out_half = plus(out_term[1], exchange(out_term[0], "blk", 1))
-        out_sum = plus(pick(out_half, chip, 0), exchange(pick(out_half, 1 - chip, 0), "blk", 2))
-    up_grad, down_grad, out_grad = weight_sums(up_sum, down_sum, out_sum, own)
-    grads = attn_bwd(lengths, qkv, grad_own, attended_own, log_total)
-
-    by_block = grads.reshape(2, 2, rows, 3 * own)
-    away = times_transposed(pick(by_block, 1 - core, 1).reshape(2 * rows, 3 * own), own_weight).astype(jnp.bfloat16)
-    got = exchange(away, "blk", 1)
-    stay = times_transposed(pick(by_block, core, 1).reshape(2 * rows, 3 * own), own_weight)
-    half = plus(stay, got).reshape(2, rows, width)
-    half, grads = lax.optimization_barrier((half, grads))
-    far = exchange(pick(half, 1 - chip, 0), "blk", 2)
-
-    term = outer_sum(first_all, grads).astype(jnp.bfloat16).reshape(parts // 2, 2, width // parts, 3 * own)
-    near = lax.rem(lax.axis_index("dp"), 2)
-    term = plus(pick(term, near, 1), exchange(pick(term, 1 - near, 1), "dp", 1))
-    qkv_term = far_sum(term).astype(jnp.bfloat16)
-    qkv_blocks = lax.all_gather(qkv_term, "blk", axis=0)
-    qkv_rows = qkv_blocks.reshape(blocks, -1, 3, own).transpose(1, 2, 0, 3).reshape(-1, 3 * width)
-    qkv_grad = lax.dynamic_slice_in_dim(qkv_rows, me * 3 * own, 3 * own, 1).astype(jnp.float32)
-
-    def spread(values):
-        return lax.dynamic_update_slice_in_dim(jnp.zeros((width,), jnp.float32), values, me * own, 0)
-
-    y = pick(half, chip, 0).astype(jnp.float32) + far.astype(jnp.float32)
-    n, r = _stats(tokens.astype(jnp.float32))
-    token_grad = (grad_middle + _pull(n, r, y * norm_gain[0])).astype(jnp.bfloat16)
-    small = jnp.stack(
-        [
-            jnp.sum(y * n, 0), sums[0], sums[1], sums_three[0], jnp.sum(y, 0), sums[2], sums[3], sums_three[1],
-            spread(column_sums(grads[:, :own])), spread(column_sums(grads[:, 2 * own :])), sums[4], sums_three[2],
-            *hidden_bias.reshape(-1, width),
-        ]
-    )
-    small = sum_everywhere(small)
-    place = lax.axis_index("dp")
-    chunk = width // parts
-    small_own = lax.dynamic_slice_in_dim(small[:12], place * chunk, chunk, 1)
-    hidden = lax.dynamic_slice_in_dim(small[12:].reshape(-1), place * 4 * chunk, 4 * chunk, 0)
-    return (mixed, token_grad, qkv_grad, out_grad, up_grad, down_grad, small_own[:4], small_own[4:8], small_own[8:], hidden)
+    thin = width // parts
+    halves = by_chip(far_sums(up_sum))
+    up_grad = pick(halves, chip, 0).astype(jnp.float32) + exchange(pick(halves, 1 - chip, 0), "blk", 2).astype(jnp.float32)
+    out_term = out_term.reshape(2, 2, width // 2, width // 2).transpose(1, 2, 0, 3).reshape(2, 2, own, width)
+    out_half = plus(out_term[1], exchange(out_term[0], "blk", 1))
+    out_sum = plus(pick(out_half, chip, 0), exchange(pick(out_half, 1 - chip, 0), "blk", 2))
+    down = down_sum.transpose(1, 0, 2).reshape(own, parts, -1).transpose(1, 0, 2)
+    out = out_sum.reshape(own, parts, thin).transpose(1, 0, 2)
+    both = lax.psum_scatter(jnp.concatenate([down, out], 2), "dp", scatter_dimension=0, tiled=False).astype(jnp.float32)
+    down_grad, out_grad = both[:, : down.shape[2]].T, both[:, down.shape[2] :].T
+    token_grad, qkv_grad, small, hidden = finish_plain(grads, first_all, own_weight, tokens, grad_middle, norm_gain, early, hidden_bias)
+    return (mixed, token_grad, qkv_grad, out_grad, up_grad, down_grad, small[:4], small[4:8], small[8:], hidden)
 
 
 def solution(mesh):

time: 475 us -> 424 us (0.89)
  Pallas kernels: 290 us -> 387 us
  waiting for transfers between devices: 60.4 us -> 0.04 us
  starting transfers between devices: 25.8 us -> 0.04 us
  matrix products: 20.2 us -> 0 us
  local copies, waits for them, and re-layouts: 31.4 us -> 13.6 us
  other arithmetic: 15.5 us -> 1.12 us
  blocking collectives: 8.59 us -> 0 us
    pallas_call x1 -> x2, Pallas kernels: 51.7 us -> 114 us  [the longest x1 66.1 us: finish(): pl.pallas_call(functools.partial(tail_kernel, pieces=pieces), in_specs=[h...]
    ppermute x12 -> x0, waiting for transfers between devices: 41.8 us -> none  [exchange(): lax.ppermute(values, axis, [(i, i ^ bit) for i in range(lax.axis_size(axi...]
    pallas_call x1, Pallas kernels: 41.4 us -> 72.9 us  [ffn_forward(): pl.pallas_call(functools.partial(ffn_kernel, tiles=tiles, strip=rows // 4...]
    ppermute x12 -> x0, starting transfers between devices: 22 us -> none  [exchange(): lax.ppermute(values, axis, [(i, i ^ bit) for i in range(lax.axis_size(axi...]
    dot_general x3 -> x0, matrix products: 20.2 us -> none  [the longest x2 12.2 us: times_transposed(): return lax.dot_general(left, right, NT, preferred_element_type=jnp.float32)]
    all_to_all x1 -> x0, waiting for transfers between devices: 18.6 us -> none  [local(): lax.all_to_all(attended_own, 'blk', split_axis=0, concat_axis=1, tiled=True)]
    all_gather x1 -> x0, blocking collectives: 8.59 us -> none  [local(): qkv_blocks = lax.all_gather(qkv_term, 'blk', axis=0)]
    reduce_sum x4 -> x0, other arithmetic: 7.15 us -> none  [the longest x1 3.73 us: local(): jnp.sum(y * n, 0)]
  transfers between devices with their start and end apart: 15 -> 1, of which waited for: 9 -> 0; matrix products, arithmetic and copies ran while one was open for 11% -> 0% of each run, Pallas kernels for 13% -> 31%
where the time goes in v4:
time: 424 us; the launch traced here: 416 us
  Pallas kernels  387 us (91%)
  between operations  14.4 us (3%)
  local copies, waits for them, and re-layouts  13.6 us (3%)
    pallas_call x1, Pallas kernels, ffn_backward(): pl.pallas_call(functools.partial(grads_kernel, tiles=tiles, strip=rows //...  92.2 us
    pallas_call x1, Pallas kernels, ffn_forward(): pl.pallas_call(functools.partial(ffn_kernel, tiles=tiles, strip=rows // 4...  72.9 us
    pallas_call x1, Pallas kernels, finish(): pl.pallas_call(functools.partial(tail_kernel, pieces=pieces), in_specs=[h...  66.1 us
    pallas_call x1, Pallas kernels, attn_bwd(): pl.pallas_call(functools.partial(bwd_kernel, heads=heads, wide=wide), gri...  62.8 us
    pallas_call x1, Pallas kernels, attn_fwd(): pl.pallas_call(functools.partial(fwd_kernel, heads=heads), grid_spec=pltp...  47.8 us
    pallas_call x1, Pallas kernels, gather_project(): pl.pallas_call(functools.partial(project_kernel, pieces=pieces), in_specs...  44.9 us
    unnamed x38, local copies, waits for them, and re-layouts  13.6 us
  transfers between devices with their start and end apart: 1, of which 0 were waited for; matrix products, arithmetic and copies ran while one was open for 0% of the time, Pallas kernels for 31%

profile of v4, /device:TPU:0, one launch (start us, length us, event | category | flops | bytes accessed | tf_op | source)
XLA Modules:
  0.0 415.8 jit_solution(6868715703495076111)
XLA Ops:
  7.2 1.4 copy-done
  8.7 0.7 copy-done.1
  9.4 0.7 copy-done.2
  10.1 0.7 copy-done.3
  10.8 44.9 %gather_project.1 = (bf16[3328,1024]{1,0:T(8,128)(2,1)}, bf16[3328,768]{1,0:T(8,128)(2,1)}, bf16[1024,768]{1,0:T(8,128)(2,1)S(1)}) custom-call(bf16[832,1024]{1,0:T(8,128)(2,1)S(1)} %copy-done, bf16[1024,3072]{1,0:T(8,128)(2,1)} %w_hbm.1, f32[4,1024]{1,0:T(4,128)S(1)} %copy-done.1, f32[4,1024]{1,0:T(4,128)S(1)} %copy-done.2, f32[4,1024]{1,0:T(4,128)S(1)} %copy-done.3), custom_call_target="tpu_custom_call" | custom-call | tf_op jit(solution)/shard_map/gather_project/pallas_call | solution.py:834
  55.7 1.1 copy-done.4
  56.9 47.8 %attn_fwd.1 = (bf16[3328,256]{1,0:T(8,128)(2,1)}, f32[4,3328]{1,0:T(4,128)}) custom-call(s32[1,3]{1,0:T(1,128)} %len_ref.3, bf16[3328,768]{1,0:T(8,128)(2,1)} %get-tuple-element.41.q_ref.k_ref.v_ref, bf16[3328,768]{1,0:T(8,128)(2,1)} %get-tuple-element.41.q_ref.k_ref.v_ref, bf16[3328,768]{1,0:T(8,128)(2,1)} %get-tuple-element.41.q_ref.k_ref.v_ref), custom_call_target="tpu_custom_call" | custom-call | flops 25518145536 | bytes 8519680 | tf_op jit(solution)/shard_map/attn_fwd/pallas_call | solution.py:167
  104.7 72.9 %ffn_forward.1 = (bf16[832,1024]{1,0:T(8,128)(2,1)}, f32[832,1024]{1,0:T(8,128)}, bf16[832,1024]{1,0:T(8,128)(2,1)}, f32[832,1]{1,0:T(8,128)}, bf16[832,1024]{1,...) custom-call(bf16[832,1024]{1,0:T(8,128)(2,1)} %x_hbm.5, ...), custom_call_target="tpu_custom_call" | custom-call | flops 15703474176 | bytes 52428800 | tf_op jit(solution)/shard_map/ffn_forward/pallas_call | solution.py:420
  177.6 92.2 %ffn_backward.1 = (f32[832,1024]{1,0:T(8,128)}, f32[8,1024]{1,0:T(8,128)}, f32[8,1,512]{2,1,0:T(1,128)}, bf16[4,128,512]{2,1,0:T(8,128)(2,1)}, bf16[8,256,512]{2...) custom-call(bf16[832,1024]{1,0:T(8,128)(2,1)} %get-tuple-element.44., ...), custom_call_target="tpu_custom_call" | custom-call | tf_op jit(solution)/shard_map/ffn_backward/pallas_call | solution.py:712
  269.8 62.8 %attn_bwd.1.d_hbm = bf16[3328,768]{1,0:T(8,128)(2,1)} custom-call(s32[1,3]{1,0:T(1,128)} %len_ref.3, bf16[3328,768]{1,0:T(8,128)(2,1)} %get-tuple-element.41.q_ref.k_ref.v_ref, bf16[3328,256]{1,0:T(8,128)(2,1)} %get-tuple-element.53.do_ref, bf16[3328,256]{1,0:T(8,128)(2,1)} %get-tuple-element.42.own_hbm.o_ref, f32[4,3328]{1,0:T(4,128)} %get-tuple-element.54.lse_ref, ...), custom_call_target="tpu_custom_call" | custom-call | flops 31188844544 | bytes 17039360 | tf_op jit(solution)/shard_map/attn_bwd/pallas_call | solution.py:241
  332.6 66.1 %finish.1 = (bf16[832,1024]{1,0:T(8,128)(2,1)}, f32[128,768]{1,0:T(8,128)}, f32[128,1024]{1,0:T(8,128)}, f32[128,256]{1,0:T(8,128)}, f32[4,128]{1,0:T(4,128)}, /...) custom-call(bf16[3328,768]{1,0:T(8,128)(2,1)} %attn_bwd.1.d_hbm, ...), custom_call_target="tpu_custom_call" | custom-call | flops 52344913920 | bytes 134217728 | tf_op jit(solution)/shard_map/finish/pallas_call | solution.py:1095
  398.8 1.1 convert_bitcast_fusion
  399.9 1.0 copy.21
  400.9 1.2 copy.31
  402.1 0.9 copy-done.6
  403.0 1.2 copy.32
  404.2 0.0 copy-done.8
  404.2 0.7 copy.33
  405.0 0.7 copy.34
  405.7 0.8 copy.35
  406.4 0.6 copy.36
  407.0 0.6 copy.37
  407.6 0.6 copy.38
  408.2 0.6 copy.39
  (24 shorter events, 0.1 us)
Async XLA Ops:
  7.2 391.6 %reduce-scatter.2.cloned.1.call-start = ((), (), s32[]{:S(2)}) async-start(), calls=%async_computation.1 | async-start | bytes 2359296 | tf_op jit(solution)/shard_map/reduce_scatter | solution.py:1215
  7.2 1.5 copy-start
  8.7 0.7 copy-start.1
  9.4 0.7 copy-start.2
  10.1 0.7 copy-start.3
  55.7 1.1 copy-start.4
  398.8 2.2 copy-start.5
  400.9 2.1 copy-start.6
  403.0 1.2 copy-start.8
  403.0 2.0 copy-start.9
  403.0 2.6 copy-start.7
  404.2 2.2 copy-start.13
  404.2 2.8 copy-start.12
  404.2 3.4 copy-start.11
  404.2 4.0 copy-start.10
Sparse Core Ops, SparseCore 0:
  269.9 69.2 reduce-scatter.1

commit v5 on v4

--- a/solution.py
+++ b/solution.py
@@ -59,58 +59,7 @@
         dst[pl.ds(h * TILE, TILE), :] = jnp.where(lane == h, value, jnp.zeros_like(value))
 
 
-def _span(len_ref, qb):
-    l0 = len_ref[0, 0]
-    e1 = l0 + len_ref[0, 1]
-
-    def start_of(r):
-        return jnp.where(r >= e1, e1, jnp.where(r >= l0, l0, 0))
-
-    rows = qb * TILE + lax.broadcasted_iota(jnp.int32, (1, TILE), 1)
-    kmin = start_of(qb * TILE) // TILE
-    return kmin, qb + 1 - kmin, rows, start_of(rows)
-
-
-def _at(kb):
-    return pl.ds(pl.multiple_of(kb * TILE, TILE), TILE)
-
-
-def _mask(kb, rows, starts):
-    kpos = kb * TILE + lax.broadcasted_iota(jnp.int32, (TILE, TILE), 0)
-    return (kpos >= starts) & (kpos <= rows)
-
-
-def _pipeline(kmin, count, load, work, use):
-    odd = lax.rem(count, 2)
-    end = kmin + count - 1
-
-    @pl.when(odd == 1)
-    def _():
-        load(kmin, 0)
-        load(jnp.minimum(kmin + 1, end), 1)
-        work(kmin, 0)
-
-    @pl.when(odd == 0)
-    def _():
-        load(kmin, 1)
-
-    first = kmin + odd
-
-    def two(i, carry):
-        kb = first + 2 * i
-        load(jnp.minimum(kb + 1, end), 0)
-        work(kb, 1)
-        use(jnp.maximum(kb - 1, kmin), 0)
-        load(jnp.minimum(kb + 2, end), 1)
-        work(kb + 1, 0)
-        use(kb, 1)
-        return carry
-
-    lax.fori_loop(0, count // 2, two, 0)
-    use(end, 0)
-
-
-def fwd_kernel(len_ref, q_ref, k_ref, v_ref, o_ref, lse_ref, qm, acc, s_one, s_two, p_one, p_two, fade_one, fade_two, top, norm, vt, *, heads):
+def fwd_kernel(len_ref, q_ref, k_ref, v_ref, o_ref, lse_ref, qm, acc, ps, vt, *, heads, wide):
     qb = pl.program_id(0)
 
     @pl.when(qb == 0)
@@ -119,70 +68,64 @@
 
     _fill_masked(qm, q_ref[...] * jnp.bfloat16(0.125), heads)
     acc[...] = jnp.zeros_like(acc)
-    p_one[...] = jnp.zeros_like(p_one)
-    fade_one[...] = jnp.zeros_like(fade_one)
-    top[...] = jnp.full(top.shape, 0.1 * NEG, jnp.float32)
-    norm[...] = jnp.zeros_like(norm)
-    kmin, count, rows, starts = _span(len_ref, qb)
-    scores, probs, fades = (s_one, s_two), (p_one, p_two), (fade_one, fade_two)
-
-    def load(kb, slot):
+
+    def step(at, size, mask, carry):
+        keys = pl.ds(at, size)
+        scores = [
+            lax.dot_general(k_ref[keys, :], qm[pl.ds(h * TILE, TILE), :], NT, preferred_element_type=jnp.float32)
+            for h in range(heads)
+        ]
+        out, fades = [], []
         for h in range(heads):
-            mine = pl.ds(h * TILE, TILE)
-            scores[slot][:, mine] = lax.dot_general(k_ref[_at(kb), :], qm[mine, :], NT, preferred_element_type=jnp.float32)
-
-    def work(kb, slot):
-        mask = _mask(kb, rows, starts)
-        for h in range(heads):
-            mine, row = pl.ds(h * TILE, TILE), pl.ds(h, 1)
-            s = jnp.where(mask, scores[slot][:, mine], NEG)
-            m = top[row, :]
-            new = jnp.maximum(m, jnp.max(s, 0, keepdims=True))
-            p = jnp.exp(s - new)
-            fade = jnp.exp(m - new)
-            top[row, :] = new
-            norm[row, :] = norm[row, :] * fade + jnp.sum(p, 0, keepdims=True)
-            fades[slot][row, :] = fade
-            probs[slot][:, mine] = p.astype(jnp.bfloat16)
-
-    def use(kb, slot):
+            m, l = carry[h]
+            s = scores[h]
+            if mask is not None:
+                s = jnp.where(mask, s, NEG)
+            top = jnp.maximum(m, jnp.max(s, 0, keepdims=True))
+            p = jnp.exp(s - top)
+            if mask is not None:
+                p = jnp.where(mask, p, 0.0)
+            fade = jnp.exp(m - top)
+            ps[pl.ds(0, size), pl.ds(h * TILE, TILE)] = p.astype(jnp.bfloat16)
+            out.append((top, l * fade + jnp.sum(p, 0, keepdims=True)))
+            fades.append(fade)
         for h in range(heads):
             lanes = pl.ds(h * HD, HD)
-            part = jnp.dot(vt[lanes, _at(kb)], probs[slot][:, pl.ds(h * TILE, TILE)], preferred_element_type=jnp.float32)
-            acc[lanes, :] = acc[lanes, :] * fades[slot][pl.ds(h, 1), :] + part
-
-    _pipeline(kmin, count, load, work, use)
+            part = jnp.dot(vt[lanes, keys], ps[pl.ds(0, size), pl.ds(h * TILE, TILE)], preferred_element_type=jnp.float32)
+            acc[lanes, :] = acc[lanes, :] * fades[h] + part
+        return tuple(out)
+
+    carry = tuple((jnp.full((1, TILE), NEG, jnp.float32), jnp.zeros((1, TILE), jnp.float32)) for _ in range(heads))
+    carry = _walk(len_ref, qb, step, carry, wide)
     for h in range(heads):
-        row, lanes = pl.ds(h, 1), pl.ds(h * HD, HD)
-        lse_ref[row, :] = top[row, :] + jnp.log(norm[row, :])
-        acc[lanes, :] = acc[lanes, :] / norm[row, :]
+        m, l = carry[h]
+        lse_ref[pl.ds(h, 1), :] = m + jnp.log(l)
+        acc[pl.ds(h * HD, HD), :] = acc[pl.ds(h * HD, HD), :] / l
     o_ref[...] = acc[...].T.astype(jnp.bfloat16)
 
 
-def attn_fwd(lengths, qkv):
-    n, lane = qkv.shape[0], qkv.shape[1] // 3
+def attn_fwd(lengths, qkv, pair=0, lane=256, wide=(1,)):
+    n = qkv.shape[0]
     heads = lane // HD
-    wide = heads * TILE
-    f32, bf16 = jnp.float32, jnp.bfloat16
     return pl.pallas_call(
-        functools.partial(fwd_kernel, heads=heads),
+        functools.partial(fwd_kernel, heads=heads, wide=wide),
         grid_spec=pltpu.PrefetchScalarGridSpec(
             num_scalar_prefetch=1,
             grid=(n // TILE,),
             in_specs=[
-                pl.BlockSpec((TILE, lane), lambda i, L: (i, 0)),
-                pl.BlockSpec((n, lane), lambda i, L: (0, 1)),
-                pl.BlockSpec((n, lane), lambda i, L: (0, 2)),
+                pl.BlockSpec((TILE, lane), lambda i, L: (i, 3 * pair)),
+                pl.BlockSpec((n, lane), lambda i, L: (0, 3 * pair + 1)),
+                pl.BlockSpec((n, lane), lambda i, L: (0, 3 * pair + 2)),
             ],
             out_specs=[pl.BlockSpec((TILE, lane), lambda i, L: (i, 0)), pl.BlockSpec((heads, TILE), lambda i, L: (0, i))],
             scratch_shapes=[
-                pltpu.VMEM((wide, lane), bf16), pltpu.VMEM((lane, TILE), f32),
-                pltpu.VMEM((TILE, wide), f32), pltpu.VMEM((TILE, wide), f32), pltpu.VMEM((TILE, wide), bf16), pltpu.VMEM((TILE, wide), bf16),
-                pltpu.VMEM((heads, TILE), f32), pltpu.VMEM((heads, TILE), f32), pltpu.VMEM((heads, TILE), f32), pltpu.VMEM((heads, TILE), f32),
-                pltpu.VMEM((lane, n), bf16),
+                pltpu.VMEM((heads * TILE, lane), jnp.bfloat16),
+                pltpu.VMEM((lane, TILE), jnp.float32),
+                pltpu.VMEM((wide[0] * TILE, heads * TILE), jnp.bfloat16),
+                pltpu.VMEM((lane, n), jnp.bfloat16),
             ],
         ),
-        out_shape=[jax.ShapeDtypeStruct((n, lane), bf16), jax.ShapeDtypeStruct((heads, n), f32)],
+        out_shape=[jax.ShapeDtypeStruct((n, lane), jnp.bfloat16), jax.ShapeDtypeStruct((heads, n), jnp.float32)],
         compiler_params=pltpu.CompilerParams(vmem_limit_bytes=58 * 2**20),
         cost_estimate=pl.CostEstimate(flops=n * n * lane * 9, bytes_accessed=10 * n * lane, transcendentals=n * n * heads // 2),
         name="attn_fwd",
@@ -562,14 +505,6 @@
             pl.semaphore_signal(barrier, inc=1, device_id={"dp": 2 * ahead + near}, device_id_type=mesh_ids)
         pl.semaphore_wait(barrier, 7 if fold else 4)
 
-    @pl.when(s > 0)
-    def _():
-        join_down(s - 1)
-
-    @pl.when((side == 0) & (s > 0))
-    def _():
-        join_up(pair - 1)
-
     @pl.when(s >= 3)
     def _():
         join_far_down(s - 3)
@@ -606,6 +541,15 @@
     down_send[side] = down_grad[: width // 2].reshape(2, own, -1)
     down_to_twin(s, side).start()
     down_keep[s] = down_grad[width // 2 :].reshape(2, own, -1)
+
+    @pl.when(s > 0)
+    def _():
+        join_down(s - 1)
+
+    @pl.when((side == 0) & (s > 0))
+    def _():
+        join_up(pair - 1)
+
     up_grad = jnp.dot(second_t[...], pre[...], preferred_element_type=f32).astype(bf16).reshape(up_buf.shape[1:])
 
     @pl.when(side == core)
@@ -637,11 +581,11 @@
             sums[pl.ds(16, 8), :] += _fold(gm)
             sums[pl.ds(32, 8), :] += _fold(g.astype(f32))
 
-        join_down(tiles - 1)
-        join_up(half - 1)
         for i in range(5):
             saved(i).wait()
         _each(rows, strip, normed)
+        join_down(tiles - 1)
+        join_up(half - 1)
         gatt[...] = lax.dot_general(low[...], wo_ref[...], NT, preferred_element_type=f32).astype(bf16)
         for i in range(3):
             columns_to(i).start()
@@ -841,7 +785,7 @@
             pltpu.VMEM((4 * rows, 3 * width // 4), jnp.bfloat16), pltpu.VMEM((width, 3 * width // 4), jnp.bfloat16),
             dma, pltpu.SemaphoreType.DMA((8 * pieces,)), pltpu.SemaphoreType.DMA((4,)),
         ] + [dma] * 6,
-        compiler_params=pltpu.CompilerParams(collective_id=0, has_side_effects=True, vmem_limit_bytes=48 * 2**20),
+        compiler_params=pltpu.CompilerParams(collective_id=0, has_side_effects=True, vmem_limit_bytes=60 * 2**20),
         name="gather_project",
     )(tokens, qkv_weight, norm_gain, norm_bias, proj_bias)
 
@@ -1104,6 +1048,29 @@
     )(grads, first_all, own_weight, tokens, grad_middle, norm_gain, up_sum, out_line, sums, sums_three, hidden_bias)
 
 
+def emit_kernel(token_in, qkv_in, up_in, out_in, down_in, gain_in, shift_in, bias_in, hid_in, token_ref, qkv_ref, up_ref, out_ref, down_ref, gain_ref, shift_ref, bias_ref, hid_ref):
+    for src, dst in (
+        (token_in, token_ref), (qkv_in, qkv_ref), (up_in, up_ref), (out_in, out_ref),
+        (gain_in, gain_ref), (shift_in, shift_ref), (bias_in, bias_ref), (hid_in, hid_ref),
+    ):
+        dst[...] = src[...]
+    down_ref[...] = down_in[...].astype(jnp.float32).T
+
+
+def emit(token_grad, qkv_grad, up_grad, out_grad, down_grad, gains, shifts, biases, hidden):
+    arrays = (token_grad, qkv_grad, up_grad, out_grad, down_grad, gains, shifts, biases, hidden)
+    shapes = [jax.ShapeDtypeStruct(a.shape, a.dtype) for a in arrays]
+    shapes[4] = jax.ShapeDtypeStruct(down_grad.shape[::-1], jnp.float32)
+    return pl.pallas_call(
+        emit_kernel,
+        in_specs=[pl.BlockSpec(memory_space=pltpu.VMEM)] * 9,
+        out_specs=[pl.BlockSpec(memory_space=pltpu.VMEM)] * 9,
+        out_shape=shapes,
+        compiler_params=pltpu.CompilerParams(vmem_limit_bytes=60 * 2**20),
+        name="emit",
+    )(*arrays)
+
+
 def outer_sum(left, right):
     return lax.dot_general(left, right, (((0,), (0,)), ((), ())), preferred_element_type=jnp.float32)
 
@@ -1212,9 +1179,12 @@
     grads = attn_bwd(lengths, qkv, grad_own, attended_own, log_total)
 
     if parts == 8:
-        down_grad = lax.psum_scatter(down_sum, "dp", scatter_dimension=0, tiled=False).astype(jnp.float32).T
+        down_grad = lax.psum_scatter(down_sum, "dp", scatter_dimension=0, tiled=False)
         token_grad, qkv_grad, up_grad, out_grad, gains, shifts, biases, hidden = finish(
             grads, first_all, own_weight, tokens, grad_middle, norm_gain, up_sum, out_line, sums, sums_three, hidden_bias
+        )
+        token_grad, qkv_grad, up_grad, out_grad, down_grad, gains, shifts, biases, hidden = emit(
+            token_grad, qkv_grad, up_grad, out_grad, down_grad, gains, shifts, biases, hidden
         )
         return (mixed, token_grad, qkv_grad, out_grad, up_grad, down_grad, gains, shifts, biases, hidden.reshape(-1))
     early = [None, sums[0], sums[1], sums_three[0], None, sums[2], sums[3], sums_three[1], None, None, sums[4], sums_three[2]]

time: 424 us -> 400 us (0.943)
  local copies, waits for them, and re-layouts: 13.6 us -> 1.19 us
  Pallas kernels: 387 us -> 378 us
    pallas_call x1, Pallas kernels: 72.9 us -> 58.7 us  [ffn_forward(): pl.pallas_call(functools.partial(ffn_kernel, tiles=tiles, strip=rows // 4...]
    pallas_call x1 -> x2, Pallas kernels: 47.8 us -> 61.9 us  [the longest x1 58.2 us: attn_fwd(): pl.pallas_call(functools.partial(fwd_kernel, heads=heads, wide=wide), gri...]
    unnamed x38 -> x3, local copies, waits for them, and re-layouts: 13.6 us -> 1.19 us
    pallas_call x1, Pallas kernels: 92.2 us -> 82.3 us  [ffn_backward(): pl.pallas_call(functools.partial(grads_kernel, tiles=tiles, strip=rows //...]
    pallas_call x1, Pallas kernels: 62.8 us -> 68.7 us  [attn_bwd(): pl.pallas_call(functools.partial(bwd_kernel, heads=heads, wide=wide), gri...]
    pallas_call x1, Pallas kernels: 66.1 us -> 61.3 us  [finish(): pl.pallas_call(functools.partial(tail_kernel, pieces=pieces), in_specs=[h...]
  transfers between devices with their start and end apart: 1 -> 1, of which waited for: 0 -> 0; matrix products, arithmetic and copies ran while one was open for 0% -> 0% of each run, Pallas kernels for 31% -> 33%
where the time goes in v5:
time: 400 us; the launch traced here: 394 us
  Pallas kernels  378 us (94%)
  between operations  14.3 us (4%)
    pallas_call x1, Pallas kernels, ffn_backward(): pl.pallas_call(functools.partial(grads_kernel, tiles=tiles, strip=rows //...  82.3 us
    pallas_call x1, Pallas kernels, attn_bwd(): pl.pallas_call(functools.partial(bwd_kernel, heads=heads, wide=wide), gri...  68.7 us
    pallas_call x1, Pallas kernels, finish(): pl.pallas_call(functools.partial(tail_kernel, pieces=pieces), in_specs=[h...  61.3 us
    pallas_call x1, Pallas kernels, ffn_forward(): pl.pallas_call(functools.partial(ffn_kernel, tiles=tiles, strip=rows // 4...  58.7 us
    pallas_call x1, Pallas kernels, attn_fwd(): pl.pallas_call(functools.partial(fwd_kernel, heads=heads, wide=wide), gri...  58.2 us
    pallas_call x1, Pallas kernels, gather_project(): pl.pallas_call(functools.partial(project_kernel, pieces=pieces), in_specs...  45.4 us
  transfers between devices with their start and end apart: 1, of which 0 were waited for; matrix products, arithmetic and copies ran while one was open for 0% of the time, Pallas kernels for 33%

profile of v5, /device:TPU:0, one launch (start us, length us, event | category | flops | bytes accessed | tf_op | source)
XLA Modules:
  0.0 393.8 jit_solution(5131812670937435056)
XLA Ops:
  7.2 0.0 reduce-scatter.2.cloned.1.call-start
  7.2 45.4 %gather_project.1 = (bf16[3328,1024]{1,0:T(8,128)(2,1)}, bf16[3328,768]{1,0:T(8,128)(2,1)}, bf16[1024,768]{1,0:T(8,128)(2,1)}) custom-call(bf16[832,1024]{1,0:T(8,128)(2,1)} %x_hbm.5, bf16[1024,3072]{1,0:T(8,128)(2,1)} %w_hbm.1, f32[4,1024]{1,0:T(4,128)} %gain_ref.7, f32[4,1024]{1,0:T(4,128)} %shift_ref.3, f32[4,1024]{1,0:T(4,128)} %bias_ref.3), custom_call_target="tpu_custom_call" | custom-call | tf_op jit(solution)/shard_map/gather_project/pallas_call | solution.py:778
  52.6 58.2 %attn_fwd.1 = (bf16[3328,256]{1,0:T(8,128)(2,1)}, f32[4,3328]{1,0:T(4,128)}) custom-call(s32[1,3]{1,0:T(1,128)} %len_ref.3, bf16[3328,768]{1,0:T(8,128)(2,1)} %get-tuple-element.50.q_ref.k_ref.v_ref, bf16[3328,768]{1,0:T(8,128)(2,1)} %get-tuple-element.50.q_ref.k_ref.v_ref, bf16[3328,768]{1,0:T(8,128)(2,1)} %get-tuple-element.50.q_ref.k_ref.v_ref), custom_call_target="tpu_custom_call" | custom-call | flops 25518145536 | bytes 8519680 | tf_op jit(solution)/shard_map/attn_fwd/pallas_call | solution.py:110
  110.8 58.7 %ffn_forward.1 = (bf16[832,1024]{1,0:T(8,128)(2,1)}, f32[832,1024]{1,0:T(8,128)}, bf16[832,1024]{1,0:T(8,128)(2,1)}, f32[832,1]{1,0:T(8,128)}, bf16[832,1024]{1,...) custom-call(bf16[832,1024]{1,0:T(8,128)(2,1)} %x_hbm.5, ...), custom_call_target="tpu_custom_call" | custom-call | flops 15703474176 | bytes 52428800 | tf_op jit(solution)/shard_map/ffn_forward/pallas_call | solution.py:363
  169.5 82.3 %ffn_backward.1 = (f32[832,1024]{1,0:T(8,128)}, f32[8,1024]{1,0:T(8,128)}, f32[8,1,512]{2,1,0:T(1,128)}, bf16[4,128,512]{2,1,0:T(8,128)(2,1)}, bf16[8,256,512]{2...) custom-call(bf16[832,1024]{1,0:T(8,128)(2,1)} %get-tuple-element.53., ...), custom_call_target="tpu_custom_call" | custom-call | tf_op jit(solution)/shard_map/ffn_backward/pallas_call | solution.py:656
  251.7 0.0 reduce-scatter.2.cloned.1.call-update
  251.7 68.7 %attn_bwd.1.d_hbm = bf16[3328,768]{1,0:T(8,128)(2,1)} custom-call(s32[1,3]{1,0:T(1,128)} %len_ref.3, bf16[3328,768]{1,0:T(8,128)(2,1)} %get-tuple-element.50.q_ref.k_ref.v_ref, bf16[3328,256]{1,0:T(8,128)(2,1)} %get-tuple-element.62.do_ref, bf16[3328,256]{1,0:T(8,128)(2,1)} %get-tuple-element.51.own_hbm.o_ref, f32[4,3328]{1,0:T(4,128)} %get-tuple-element.63.lse_ref, ...), custom_call_target="tpu_custom_call" | custom-call | flops 31188844544 | bytes 17039360 | tf_op jit(solution)/shard_map/attn_bwd/pallas_call | solution.py:184
  320.4 61.3 %finish.1 = (bf16[832,1024]{1,0:T(8,128)(2,1)}, f32[128,768]{1,0:T(8,128)}, f32[128,1024]{1,0:T(8,128)}, f32[128,256]{1,0:T(8,128)}, f32[4,128]{1,0:T(4,128)}, /...) custom-call(bf16[3328,768]{1,0:T(8,128)(2,1)} %attn_bwd.1.d_hbm, ...), custom_call_target="tpu_custom_call" | custom-call | flops 52344913920 | bytes 134217728 | tf_op jit(solution)/shard_map/finish/pallas_call | solution.py:1039
  381.7 0.0 copy-start
  381.7 0.0 reduce-scatter.2.cloned.1.call-done
  381.8 3.7 emit.1
  385.5 0.0 copy-done
  385.5 1.2 copy.22
Async XLA Ops:
  7.2 374.6 %reduce-scatter.2.cloned.1.call-start = ((), (), s32[]{:S(2)}) async-start(), calls=%async_computation.1 | async-start | bytes 2359296 | tf_op jit(solution)/shard_map/reduce_scatter | solution.py:1182
  381.7 3.8 copy-start
Sparse Core Ops, SparseCore 0:
  251.9 69.0 reduce-scatter.1

commit v6 on v5

--- a/solution.py
+++ b/solution.py
@@ -32,25 +32,23 @@
 def _walk(len_ref, qb, step, carry, wide):
     kmin, kmid, rows, starts = _bounds(len_ref, qb)
 
-    def masked(kb, carry):
-        at = pl.multiple_of(kb * TILE, TILE)
-        kpos = at + lax.broadcasted_iota(jnp.int32, (TILE, TILE), 0)
-        return step(at, TILE, (kpos >= starts) & (kpos <= rows), carry)
-
-    def plain(size):
-        def run(kb, carry):
-            return step(pl.multiple_of(kb * TILE, TILE), size * TILE, None, carry)
-
-        return run
-
-    carry = lax.fori_loop(kmin, kmid, masked, carry)
-    at, left = kmid, qb - kmid
-    for size in wide:
-        count = left // size
-        base = at
-        carry = lax.fori_loop(0, count, lambda i, c, base=base, size=size: plain(size)(base + i * size, c), carry)
-        at, left = at + count * size, left - count * size
-    return masked(qb, carry)
+    def run(masked, size):
+        def body(kb, carry):
+            at = pl.multiple_of(kb * TILE, TILE)
+            mask = None
+            if masked:
+                kpos = at + lax.broadcasted_iota(jnp.int32, (size * TILE, TILE), 0)
+                mask = (kpos >= starts) & (kpos <= rows)
+            return step(at, size * TILE, mask, carry)
+
+        return body
+
+    for masked, at, left in ((True, kmin, kmid - kmin), (False, kmid, qb - kmid)):
+        for size in wide:
+            count, body = left // size, run(masked, size)
+            carry = lax.fori_loop(0, count, lambda i, c, at=at, size=size, body=body: body(at + i * size, c), carry)
+            at, left = at + count * size, left - count * size
+    return run(True, 1)(qb, carry)
 
 
 def _fill_masked(dst, value, heads):
@@ -83,8 +81,6 @@
                 s = jnp.where(mask, s, NEG)
             top = jnp.maximum(m, jnp.max(s, 0, keepdims=True))
             p = jnp.exp(s - top)
-            if mask is not None:
-                p = jnp.where(mask, p, 0.0)
             fade = jnp.exp(m - top)
             ps[pl.ds(0, size), pl.ds(h * TILE, TILE)] = p.astype(jnp.bfloat16)
             out.append((top, l * fade + jnp.sum(p, 0, keepdims=True)))
@@ -95,7 +91,7 @@
             acc[lanes, :] = acc[lanes, :] * fades[h] + part
         return tuple(out)
 
-    carry = tuple((jnp.full((1, TILE), NEG, jnp.float32), jnp.zeros((1, TILE), jnp.float32)) for _ in range(heads))
+    carry = tuple((jnp.full((1, TILE), 0.1 * NEG, jnp.float32), jnp.zeros((1, TILE), jnp.float32)) for _ in range(heads))
     carry = _walk(len_ref, qb, step, carry, wide)
     for h in range(heads):
         m, l = carry[h]
@@ -104,7 +100,7 @@
     o_ref[...] = acc[...].T.astype(jnp.bfloat16)
 
 
-def attn_fwd(lengths, qkv, pair=0, lane=256, wide=(1,)):
+def attn_fwd(lengths, qkv, pair=0, lane=256, wide=(2, 1)):
     n = qkv.shape[0]
     heads = lane // HD
     return pl.pallas_call(
@@ -176,7 +172,7 @@
         d_ref[:, pl.ds(2 * c, c)] = dv[...].astype(jnp.bfloat16)
 
 
-def attn_bwd(lengths, qkv, do, o, lse, pair=0, lane=256, wide=(1,)):
+def attn_bwd(lengths, qkv, do, o, lse, pair=0, lane=256, wide=(2, 1)):
     n = qkv.shape[0]
     heads = lane // HD
     row = lambda col: pl.BlockSpec((TILE, lane), lambda i, L: (i, col))
@@ -311,23 +307,26 @@
         for i in range(3):
             saved(i).start()
 
-    u = jnp.dot(second[...], up_ref[...], preferred_element_type=f32) + fb_ref[...]
     c1, c3 = 0.7978845608028654, 0.7978845608028654 * 0.044715
-    sq = u * u
-    t = jnp.tanh(u * (c1 + c3 * sq))
-    half = 0.5 + 0.5 * t
-    a = (u * half).astype(jnp.bfloat16)
-    act_ref[...] = a
-    slope_ref[...] = (half + (0.5 * u) * (1.0 - t * t) * (c1 + 3.0 * c3 * sq)).astype(jnp.bfloat16)
-    part = jnp.dot(a, down_ref[...], preferred_element_type=f32)
+    strips = [pl.ds(i * (rows // 2), rows // 2) for i in range(2)]
+    us = [jnp.dot(second[at, :], up_ref[...], preferred_element_type=f32) + fb_ref[...] for at in strips]
+    parts = []
+    for at, u in zip(strips, us):
+        sq = u * u
+        t = jnp.tanh(u * (c1 + c3 * sq))
+        half = 0.5 + 0.5 * t
+        a = (u * half).astype(jnp.bfloat16)
+        act_ref[at, :] = a
+        slope_ref[at, :] = (half + (0.5 * u) * (1.0 - t * t) * (c1 + 3.0 * c3 * sq)).astype(jnp.bfloat16)
+        parts.append(jnp.dot(a, down_ref[...], preferred_element_type=f32))
 
     @pl.when(s == 0)
     def _():
-        ffn[...] = part + _row(bias_ref, 3)
-
-    @pl.when(s > 0)
-    def _():
-        ffn[...] += part
+        for at in strips:
+            ffn[at, :] = jnp.zeros((rows // 2, width), f32) + _row(bias_ref, 3)
+
+    for at, part in zip(strips, parts):
+        ffn[at, :] += part
 
     @pl.when(s == tiles - 1)
     def _():

time: 400 us -> 389 us (0.973)
  Pallas kernels: 378 us -> 368 us
    pallas_call x1, Pallas kernels: 58.2 us -> 45.5 us  [attn_fwd(): pl.pallas_call(functools.partial(fwd_kernel, heads=heads, wide=wide), gri...]
    pallas_call x1, Pallas kernels: 68.7 us -> 58.9 us  [attn_bwd(): pl.pallas_call(functools.partial(bwd_kernel, heads=heads, wide=wide), gri...]
    pallas_call x1, Pallas kernels: 82.3 us -> 88.7 us  [ffn_backward(): pl.pallas_call(functools.partial(grads_kernel, tiles=tiles, strip=rows //...]
    pallas_call x1, Pallas kernels: 61.3 us -> 67.2 us  [finish(): pl.pallas_call(functools.partial(tail_kernel, pieces=pieces), in_specs=[h...]
where the time goes in v6:
time: 389 us; the launch traced here: 383 us
  Pallas kernels  368 us (95%)
  between operations  14.3 us (4%)
    pallas_call x1, Pallas kernels, ffn_backward(): pl.pallas_call(functools.partial(grads_kernel, tiles=tiles, strip=rows //...  88.7 us
    pallas_call x1, Pallas kernels, finish(): pl.pallas_call(functools.partial(tail_kernel, pieces=pieces), in_specs=[h...  67.2 us
    pallas_call x1, Pallas kernels, attn_bwd(): pl.pallas_call(functools.partial(bwd_kernel, heads=heads, wide=wide), gri...  58.9 us
    pallas_call x1, Pallas kernels, ffn_forward(): pl.pallas_call(functools.partial(ffn_kernel, tiles=tiles, strip=rows // 4...  58.5 us
    pallas_call x1, Pallas kernels, attn_fwd(): pl.pallas_call(functools.partial(fwd_kernel, heads=heads, wide=wide), gri...  45.5 us
    pallas_call x1, Pallas kernels, gather_project(): pl.pallas_call(functools.partial(project_kernel, pieces=pieces), in_specs...  45.4 us
  transfers between devices with their start and end apart: 1, of which 0 were waited for; matrix products, arithmetic and copies ran while one was open for 0% of the time, Pallas kernels for 33%

profile of v6, /device:TPU:0, one launch (start us, length us, event | category | flops | bytes accessed | tf_op | source)
XLA Modules:
  0.0 383.5 jit_solution(12594604783152787575)
XLA Ops:
  7.2 0.0 reduce-scatter.2.cloned.1.call-start
  7.2 45.4 %gather_project.1 = (bf16[3328,1024]{1,0:T(8,128)(2,1)}, bf16[3328,768]{1,0:T(8,128)(2,1)}, bf16[1024,768]{1,0:T(8,128)(2,1)}) custom-call(bf16[832,1024]{1,0:T(8,128)(2,1)} %x_hbm.5, bf16[1024,3072]{1,0:T(8,128)(2,1)} %w_hbm.1, f32[4,1024]{1,0:T(4,128)} %gain_ref.7, f32[4,1024]{1,0:T(4,128)} %shift_ref.3, f32[4,1024]{1,0:T(4,128)} %bias_ref.3), custom_call_target="tpu_custom_call" | custom-call | tf_op jit(solution)/shard_map/gather_project/pallas_call | solution.py:777
  52.6 45.5 %attn_fwd.1 = (bf16[3328,256]{1,0:T(8,128)(2,1)}, f32[4,3328]{1,0:T(4,128)}) custom-call(s32[1,3]{1,0:T(1,128)} %len_ref.3, bf16[3328,768]{1,0:T(8,128)(2,1)} %get-tuple-element.50.q_ref.k_ref.v_ref, bf16[3328,768]{1,0:T(8,128)(2,1)} %get-tuple-element.50.q_ref.k_ref.v_ref, bf16[3328,768]{1,0:T(8,128)(2,1)} %get-tuple-element.50.q_ref.k_ref.v_ref), custom_call_target="tpu_custom_call" | custom-call | flops 25518145536 | bytes 8519680 | tf_op jit(solution)/shard_map/attn_fwd/pallas_call | solution.py:106
  98.1 58.5 %ffn_forward.1 = (bf16[832,1024]{1,0:T(8,128)(2,1)}, f32[832,1024]{1,0:T(8,128)}, bf16[832,1024]{1,0:T(8,128)(2,1)}, f32[832,1]{1,0:T(8,128)}, bf16[832,1024]{1,...) custom-call(bf16[832,1024]{1,0:T(8,128)(2,1)} %x_hbm.5, ...), custom_call_target="tpu_custom_call" | custom-call | flops 15703474176 | bytes 52428800 | tf_op jit(solution)/shard_map/ffn_forward/pallas_call | solution.py:362
  156.6 88.7 %ffn_backward.1 = (f32[832,1024]{1,0:T(8,128)}, f32[8,1024]{1,0:T(8,128)}, f32[8,1,512]{2,1,0:T(1,128)}, bf16[4,128,512]{2,1,0:T(8,128)(2,1)}, bf16[8,256,512]{2...) custom-call(bf16[832,1024]{1,0:T(8,128)(2,1)} %get-tuple-element.53., ...), custom_call_target="tpu_custom_call" | custom-call | tf_op jit(solution)/shard_map/ffn_backward/pallas_call | solution.py:655
  245.3 0.0 reduce-scatter.2.cloned.1.call-update
  245.3 58.9 %attn_bwd.1.d_hbm = bf16[3328,768]{1,0:T(8,128)(2,1)} custom-call(s32[1,3]{1,0:T(1,128)} %len_ref.3, bf16[3328,768]{1,0:T(8,128)(2,1)} %get-tuple-element.50.q_ref.k_ref.v_ref, bf16[3328,256]{1,0:T(8,128)(2,1)} %get-tuple-element.62.do_ref, bf16[3328,256]{1,0:T(8,128)(2,1)} %get-tuple-element.51.own_hbm.o_ref, f32[4,3328]{1,0:T(4,128)} %get-tuple-element.63.lse_ref, ...), custom_call_target="tpu_custom_call" | custom-call | flops 31188844544 | bytes 17039360 | tf_op jit(solution)/shard_map/attn_bwd/pallas_call | solution.py:180
  304.2 67.2 %finish.1 = (bf16[832,1024]{1,0:T(8,128)(2,1)}, f32[128,768]{1,0:T(8,128)}, f32[128,1024]{1,0:T(8,128)}, f32[128,256]{1,0:T(8,128)}, f32[4,128]{1,0:T(4,128)}, /...) custom-call(bf16[3328,768]{1,0:T(8,128)(2,1)} %attn_bwd.1.d_hbm, ...), custom_call_target="tpu_custom_call" | custom-call | flops 52344913920 | bytes 134217728 | tf_op jit(solution)/shard_map/finish/pallas_call | solution.py:1038
  371.4 0.0 copy-start
  371.5 0.0 reduce-scatter.2.cloned.1.call-done
  371.5 3.7 emit.1
  375.2 0.0 copy-done
  375.2 1.2 copy.22
Async XLA Ops:
  7.2 364.3 %reduce-scatter.2.cloned.1.call-start = ((), (), s32[]{:S(2)}) async-start(), calls=%async_computation.1 | async-start | bytes 2359296 | tf_op jit(solution)/shard_map/reduce_scatter | solution.py:1181
  371.4 3.8 copy-start
Sparse Core Ops, SparseCore 0:
  245.4 68.5 reduce-scatter.1

commit v7 on v6

--- a/solution.py
+++ b/solution.py
@@ -504,9 +504,9 @@
             pl.semaphore_signal(barrier, inc=1, device_id={"dp": 2 * ahead + near}, device_id_type=mesh_ids)
         pl.semaphore_wait(barrier, 7 if fold else 4)
 
-    @pl.when(s >= 3)
-    def _():
-        join_far_down(s - 3)
+    @pl.when(s >= 4)
+    def _():
+        join_far_down(s - 4)
 
     @pl.when((s == 5) | (s == 7))
     def _():
@@ -609,7 +609,7 @@
         if fold:
             join_up(half)
         join_far_up(3)
-        for u in range(tiles - 3, tiles):
+        for u in range(tiles - 4, tiles):
             join_far_down(u)
         if fold:
             for p in range(half):

time: 389 us -> 386 us (level)
  Pallas kernels: 368 us -> 364 us
    pallas_call x1, Pallas kernels: 67.2 us -> 58.9 us  [finish(): pl.pallas_call(functools.partial(tail_kernel, pieces=pieces), in_specs=[h...]
    pallas_call x1, Pallas kernels: 88.7 us -> 81.5 us  [ffn_backward(): pl.pallas_call(functools.partial(grads_kernel, tiles=tiles, strip=rows //...]
    pallas_call x1, Pallas kernels: 58.9 us -> 65.5 us  [attn_bwd(): pl.pallas_call(functools.partial(bwd_kernel, heads=heads, wide=wide), gri...]
    pallas_call x1, Pallas kernels: 45.5 us -> 50.6 us  [attn_fwd(): pl.pallas_call(functools.partial(fwd_kernel, heads=heads, wide=wide), gri...]
where the time goes in v7:
time: 386 us; the launch traced here: 380 us
  Pallas kernels  364 us (94%)
  between operations  14.3 us (4%)
    pallas_call x1, Pallas kernels, ffn_backward(): pl.pallas_call(functools.partial(grads_kernel, tiles=tiles, strip=rows //...  81.5 us
    pallas_call x1, Pallas kernels, attn_bwd(): pl.pallas_call(functools.partial(bwd_kernel, heads=heads, wide=wide), gri...  65.5 us
    pallas_call x1, Pallas kernels, finish(): pl.pallas_call(functools.partial(tail_kernel, pieces=pieces), in_specs=[h...  58.9 us
    pallas_call x1, Pallas kernels, ffn_forward(): pl.pallas_call(functools.partial(ffn_kernel, tiles=tiles, strip=rows // 4...  58.5 us
    pallas_call x1, Pallas kernels, attn_fwd(): pl.pallas_call(functools.partial(fwd_kernel, heads=heads, wide=wide), gri...  50.6 us
    pallas_call x1, Pallas kernels, gather_project(): pl.pallas_call(functools.partial(project_kernel, pieces=pieces), in_specs...  45.4 us
  transfers between devices with their start and end apart: 1, of which 0 were waited for; matrix products, arithmetic and copies ran while one was open for 0% of the time, Pallas kernels for 33%

profile of v7, /device:TPU:0, one launch (start us, length us, event | category | flops | bytes accessed | tf_op | source)
XLA Modules:
  0.0 379.7 jit_solution(9128933148880181088)
XLA Ops:
  7.2 0.0 reduce-scatter.2.cloned.1.call-start
  7.2 45.4 %gather_project.1 = (bf16[3328,1024]{1,0:T(8,128)(2,1)}, bf16[3328,768]{1,0:T(8,128)(2,1)}, bf16[1024,768]{1,0:T(8,128)(2,1)}) custom-call(bf16[832,1024]{1,0:T(8,128)(2,1)} %x_hbm.5, bf16[1024,3072]{1,0:T(8,128)(2,1)} %w_hbm.1, f32[4,1024]{1,0:T(4,128)} %gain_ref.7, f32[4,1024]{1,0:T(4,128)} %shift_ref.3, f32[4,1024]{1,0:T(4,128)} %bias_ref.3), custom_call_target="tpu_custom_call" | custom-call | tf_op jit(solution)/shard_map/gather_project/pallas_call | solution.py:777
  52.6 50.6 %attn_fwd.1 = (bf16[3328,256]{1,0:T(8,128)(2,1)}, f32[4,3328]{1,0:T(4,128)}) custom-call(s32[1,3]{1,0:T(1,128)} %len_ref.3, bf16[3328,768]{1,0:T(8,128)(2,1)} %get-tuple-element.50.q_ref.k_ref.v_ref, bf16[3328,768]{1,0:T(8,128)(2,1)} %get-tuple-element.50.q_ref.k_ref.v_ref, bf16[3328,768]{1,0:T(8,128)(2,1)} %get-tuple-element.50.q_ref.k_ref.v_ref), custom_call_target="tpu_custom_call" | custom-call | flops 25518145536 | bytes 8519680 | tf_op jit(solution)/shard_map/attn_fwd/pallas_call | solution.py:106
  103.2 58.5 %ffn_forward.1 = (bf16[832,1024]{1,0:T(8,128)(2,1)}, f32[832,1024]{1,0:T(8,128)}, bf16[832,1024]{1,0:T(8,128)(2,1)}, f32[832,1]{1,0:T(8,128)}, bf16[832,1024]{1,...) custom-call(bf16[832,1024]{1,0:T(8,128)(2,1)} %x_hbm.5, ...), custom_call_target="tpu_custom_call" | custom-call | flops 15703474176 | bytes 52428800 | tf_op jit(solution)/shard_map/ffn_forward/pallas_call | solution.py:362
  161.6 81.5 %ffn_backward.1 = (f32[832,1024]{1,0:T(8,128)}, f32[8,1024]{1,0:T(8,128)}, f32[8,1,512]{2,1,0:T(1,128)}, bf16[4,128,512]{2,1,0:T(8,128)(2,1)}, bf16[8,256,512]{2...) custom-call(bf16[832,1024]{1,0:T(8,128)(2,1)} %get-tuple-element.53., ...), custom_call_target="tpu_custom_call" | custom-call | tf_op jit(solution)/shard_map/ffn_backward/pallas_call | solution.py:655
  243.1 0.0 reduce-scatter.2.cloned.1.call-update
  243.2 65.5 %attn_bwd.1.d_hbm = bf16[3328,768]{1,0:T(8,128)(2,1)} custom-call(s32[1,3]{1,0:T(1,128)} %len_ref.3, bf16[3328,768]{1,0:T(8,128)(2,1)} %get-tuple-element.50.q_ref.k_ref.v_ref, bf16[3328,256]{1,0:T(8,128)(2,1)} %get-tuple-element.62.do_ref, bf16[3328,256]{1,0:T(8,128)(2,1)} %get-tuple-element.51.own_hbm.o_ref, f32[4,3328]{1,0:T(4,128)} %get-tuple-element.63.lse_ref, ...), custom_call_target="tpu_custom_call" | custom-call | flops 31188844544 | bytes 17039360 | tf_op jit(solution)/shard_map/attn_bwd/pallas_call | solution.py:180
  308.7 58.9 %finish.1 = (bf16[832,1024]{1,0:T(8,128)(2,1)}, f32[128,768]{1,0:T(8,128)}, f32[128,1024]{1,0:T(8,128)}, f32[128,256]{1,0:T(8,128)}, f32[4,128]{1,0:T(4,128)}, /...) custom-call(bf16[3328,768]{1,0:T(8,128)(2,1)} %attn_bwd.1.d_hbm, ...), custom_call_target="tpu_custom_call" | custom-call | flops 52344913920 | bytes 134217728 | tf_op jit(solution)/shard_map/finish/pallas_call | solution.py:1038
  367.6 0.0 copy-start
  367.6 0.0 reduce-scatter.2.cloned.1.call-done
  367.7 3.7 emit.1
  371.4 0.0 copy-done
  371.4 1.2 copy.22
Async XLA Ops:
  7.2 360.5 %reduce-scatter.2.cloned.1.call-start = ((), (), s32[]{:S(2)}) async-start(), calls=%async_computation.1 | async-start | bytes 2359296 | tf_op jit(solution)/shard_map/reduce_scatter | solution.py:1181
  367.6 3.8 copy-start
Sparse Core Ops, SparseCore 0:
  243.3 67.6 reduce-scatter.1
